TPU v7x, 32 devices: a whole 2x2x4 slice. The times are simulated.
32 devices in a mesh: dp: 4 (over y, x), expert: 8 (over z, core).
Axes of the slice: x: 2, y: 2, z: 4, core: 2. Of those that a mesh axis runs over, the one named last changes fastest.
Arguments:
- tokens: bfloat16 [4096, 512], P(('dp', 'expert')), may hold values from -6 to 6
- codes: int32 [4096, 2], P(('dp', 'expert')), may hold values from 0 to 7, as said below
- cotangent: bfloat16 [4096, 512], P(('dp', 'expert')), may hold values from -6 to 6
- w_gate: bfloat16 [8, 512, 1024], P('expert'), may hold values from -0.25 to 0.25
- w_up: bfloat16 [8, 512, 1024], P('expert'), may hold values from -0.25 to 0.25
- w_down: bfloat16 [8, 1024, 512], P('expert'), may hold values from -0.1875 to 0.1875
Outputs:
- head_output: bfloat16 [4096, 512], P(('dp', 'expert'))
- grad_tokens: bfloat16 [4096, 512], P(('dp', 'expert'))
- grad_gate: bfloat16 [8, 512, 1024], P('expert', None, 'dp')
- grad_up: bfloat16 [8, 512, 1024], P('expert', None, 'dp')
- grad_down: bfloat16 [8, 1024, 512], P('expert', 'dp')
Inputs may be any that keep to these rules, and one draw needn't show every extreme that they name: A token's two codes differ. Within each device's 128 tokens (aligned blocks of 128 rows), each arm is named at most 64 times over both columns, and one arm, the same for every block, is named exactly 64 times in every block.
All inputs are finite; a program needn't handle non-finite values.
Results may differ from a plain program's by a relative error of at most 0.009.
Values may be sent and summed in bfloat16 or wider, within the bound.
No kernel may reach another device: no remote copies, remote signals or barrier semaphores. Data moves between devices by JAX's collectives and lax.ppermute only.
A program may use at most 64 MiB of HBM per device.

v0:
```python
import jax
import jax.numpy as jnp
from jax import lax
from jax.sharding import PartitionSpec as P

fact_share = 0.7
counter_share = 0.3


def rounded(value):
    return lax.optimization_barrier(value.astype(jnp.bfloat16)).astype(jnp.float32)


def silu_parts(gate_pre):
    sigmoid_gate = jax.nn.sigmoid(gate_pre)
    return (gate_pre * sigmoid_gate, sigmoid_gate * (1.0 + gate_pre * (1.0 - sigmoid_gate)))


def arm_forward(rows_in, gate_w, up_w):
    gate_pre = jnp.einsum("arc,ach->arh", rows_in, gate_w, preferred_element_type=jnp.float32)
    up_pre = jnp.einsum("arc,ach->arh", rows_in, up_w, preferred_element_type=jnp.float32)
    activated, silu_slope = silu_parts(gate_pre)
    hidden = (activated * up_pre).astype(jnp.bfloat16)
    return (up_pre, activated, silu_slope, hidden)


def arm_backward(up_pre, activated, silu_slope, cot_in, down_w):
    d_hidden = jnp.einsum("arc,ahc->arh", cot_in, down_w, preferred_element_type=jnp.float32)
    d_up = (d_hidden * activated).astype(jnp.bfloat16)
    d_gate = (d_hidden * up_pre * silu_slope).astype(jnp.bfloat16)
    return (d_gate, d_up)


def on_device(tokens, codes, cotangent, w_gate, w_up, w_down):
    token_count, feature_width = tokens.shape
    local_arms = w_gate.shape[0]
    arm_count = local_arms * lax.axis_size("expert")
    capacity = 4 * token_count // arm_count
    flat_codes = codes.reshape(-1)
    arm_ids = jnp.arange(arm_count, dtype=jnp.int32)
    onehot = (flat_codes[:, None] == arm_ids[None, :]).astype(jnp.int32)
    earlier = jnp.cumsum(onehot, axis=0) - onehot
    destination = flat_codes * capacity + jnp.sum(earlier * onehot, axis=1)
    shares = jnp.tile(jnp.array([fact_share, counter_share], jnp.float32), token_count)
    token_rows = jnp.repeat(tokens, 2, axis=0)
    cot_rows = (jnp.repeat(cotangent.astype(jnp.float32), 2, axis=0) * shares[:, None]).astype(
        jnp.bfloat16
    )
    blank_rows = jnp.zeros((arm_count * capacity, feature_width), jnp.bfloat16)
    send_tokens = (
        blank_rows.at[destination].set(token_rows).reshape(arm_count, capacity, feature_width)
    )
    send_cot = blank_rows.at[destination].set(cot_rows).reshape(arm_count, capacity, feature_width)
    arm_tokens, arm_cot = (
        lax.all_to_all(send_tokens, "expert", split_axis=0, concat_axis=1, tiled=True),
        lax.all_to_all(send_cot, "expert", split_axis=0, concat_axis=1, tiled=True),
    )
    up_pre, activated, silu_slope, hidden = arm_forward(arm_tokens, w_gate, w_up)
    out_rows = jnp.einsum(
        "arh,ahc->arc", hidden, w_down, preferred_element_type=jnp.float32
    ).astype(jnp.bfloat16)
    d_gate, d_up = arm_backward(up_pre, activated, silu_slope, arm_cot, w_down)
    input_rows = (
        jnp.einsum("arh,ach->arc", d_gate, w_gate, preferred_element_type=jnp.float32)
        + jnp.einsum("arh,ach->arc", d_up, w_up, preferred_element_type=jnp.float32)
    ).astype(jnp.bfloat16)
    back_out, back_input = (
        lax.all_to_all(out_rows, "expert", split_axis=1, concat_axis=0, tiled=True),
        lax.all_to_all(input_rows, "expert", split_axis=1, concat_axis=0, tiled=True),
    )
    back_out = back_out.reshape(arm_count * capacity, feature_width)[destination]
    back_out = back_out.reshape(token_count, 2, feature_width).astype(jnp.float32)
    back_input = back_input.reshape(arm_count * capacity, feature_width)[destination]
    back_input = back_input.reshape(token_count, 2, feature_width).astype(jnp.float32)
    head_output = (fact_share * back_out[:, 0] + counter_share * back_out[:, 1]).astype(
        jnp.bfloat16
    )
    grad_tokens = (back_input[:, 0] + back_input[:, 1]).astype(jnp.bfloat16)
    all_tokens, all_cot = (
        lax.all_gather(arm_tokens, "dp", axis=1, tiled=True),
        lax.all_gather(arm_cot, "dp", axis=1, tiled=True),
    )
    group_count = lax.axis_size("dp")
    hidden_width = w_gate.shape[2]
    quarter = hidden_width // group_count
    first_unit = lax.axis_index("dp") * quarter
    gate_share = lax.dynamic_slice_in_dim(w_gate, first_unit, quarter, 2)
    up_share = lax.dynamic_slice_in_dim(w_up, first_unit, quarter, 2)
    down_share = lax.dynamic_slice_in_dim(w_down, first_unit, quarter, 1)
    row_count = arm_tokens.shape[1]
    total_gate = jnp.zeros((local_arms, feature_width, quarter), jnp.float32)
    total_up = jnp.zeros((local_arms, feature_width, quarter), jnp.float32)
    total_down = jnp.zeros((local_arms, quarter, feature_width), jnp.float32)
    for group_index in range(group_count):
        some_tokens = all_tokens[:, group_index * row_count : (group_index + 1) * row_count]
        some_cot = all_cot[:, group_index * row_count : (group_index + 1) * row_count]
        piece_up, piece_act, piece_slope, piece_hidden = arm_forward(
            some_tokens, gate_share, up_share
        )
        piece_dgate, piece_dup = arm_backward(
            piece_up, piece_act, piece_slope, some_cot, down_share
        )
        total_gate = total_gate + rounded(
            jnp.einsum("arc,arh->ach", some_tokens, piece_dgate, preferred_element_type=jnp.float32)
        )
        total_up = total_up + rounded(
            jnp.einsum("arc,arh->ach", some_tokens, piece_dup, preferred_element_type=jnp.float32)
        )
        total_down = total_down + rounded(
            jnp.einsum("arh,arc->ahc", piece_hidden, some_cot, preferred_element_type=jnp.float32)
        )
    grad_gate = total_gate.astype(jnp.bfloat16)
    grad_up = total_up.astype(jnp.bfloat16)
    grad_down = total_down.astype(jnp.bfloat16)
    return (head_output, grad_tokens, grad_gate, grad_up, grad_down)


def solution(mesh):
    return jax.shard_map(
        on_device,
        mesh=mesh,
        in_specs=(
            P(("dp", "expert"), None),
            P(("dp", "expert"), None),
            P(("dp", "expert"), None),
            P("expert", None, None),
            P("expert", None, None),
            P("expert", None, None),
        ),
        out_specs=(
            P(("dp", "expert"), None),
            P(("dp", "expert"), None),
            P("expert", None, "dp"),
            P("expert", None, "dp"),
            P("expert", "dp", None),
        ),
        check_vma=False,
    )
```

profile of v0, /device:TPU:0, one launch (start us, length us, event | category | flops | bytes accessed | tf_op | source)
XLA Modules:
  0.0 138.0 jit_solution(5883585185104703527)
XLA Ops:
  7.2 0.8 broadcast_multiply_fusion
  8.0 0.8 copy.33
  9.3 0.6 reduce-window.6
  10.2 1.1 broadcast_in_dim.7
  11.5 1.7 %scatter_custom_fusion = bf16[512,512]{1,0:T(8,128)(2,1)S(1)} fusion(s32[256]{0:T(256)S(1)} %bitcast.161, bf16[256,512]{1,0:T(8,128)(2,1)S(1)} %reshape.384, bf16[]{:T(256)} %constant.11.clone.1), kind=kCustom, calls=%fused_computation.115 | custom fusion | bytes 524290 | tf_op jit(solution)/shard_map/scatter | solution.py:51
  13.1 21.6 %all_to_all.42 = bf16[8,64,512]{2,1,0:T(8,128)(2,1)} all-to-all(bf16[8,64,512]{2,1,0:T(8,128)(2,1)S(1)} %bitcast.160), channel_id=1, replica_groups=mesh['dp'=4,'expert'=8] {'expert'}, dimensions={0} | all-to-all | bytes 1048576 | tf_op jit(solution)/shard_map/all_to_all | solution.py:55
  35.4 2.4 %scatter_custom_fusion.1 = bf16[512,512]{1,0:T(8,128)(2,1)} fusion(s32[256]{0:T(256)S(1)} %bitcast.162, f32[256,512]{1,0:T(8,128)S(1)} %reshape.347, f32[256]{0:T(256)S(1)} %mul.196, bf16[]{:T(256)} %constant.11.clone.1), kind=kCustom, calls=%fused_computation.94 | custom fusion | flops 262144 | bytes 1049602 | tf_op jit(solution)/shard_map/scatter | solution.py:53
  37.8 3.5 %all-to-all-start.2 = ((bf16[8,64,512]{2,1,0:T(8,128)(2,1)}), bf16[8,64,512]{2,1,0:T(8,128)(2,1)S(1)}, u32[]{:S(2)}, u32[]{:S(2)}) async-start(bf16[8,64,512]{2,1,0:T(8,128)(2,1)} %bitcast.11), calls=%async_computation.2 | async-start | bytes 1048576 | tf_op jit(solution)/shard_map/all_to_all | solution.py:56
  41.6 2.1 %fusion.24 = f32[512,1024]{1,0:T(8,128)} fusion(bf16[512,512]{1,0:T(8,128)(2,1)S(1)} %bitcast.152, bf16[1,512,1024]{2,1,0:T(8,128)(2,1)S(1)} %copy-done), kind=kOutput, calls=%fused_computation.46 | convolution fusion | flops 536870912 | bytes 3670016 | tf_op jit(solution)/shard_map/arc,ach->arh/dot_general | solution.py:20
  43.7 2.0 %fusion.20 = f32[512,1024]{1,0:T(8,128)} fusion(bf16[512,512]{1,0:T(8,128)(2,1)S(1)} %bitcast.153, bf16[1,512,1024]{2,1,0:T(8,128)(2,1)S(1)} %copy-done.4), kind=kOutput, calls=%fused_computation.42 | convolution fusion | flops 536870912 | bytes 3670016 | tf_op jit(solution)/shard_map/arc,ach->arh/dot_general | solution.py:21
  45.7 10.9 %all-to-all-done.2 = bf16[8,64,512]{2,1,0:T(8,128)(2,1)S(1)} async-done(((bf16[8,64,512]{2,1,0:T(8,128)(2,1)}), bf16[8,64,512]{2,1,0:T(8,128)(2,1)S(1)}, u32[]{:S(2)}, u32[]{:S(2)}) %all-to-all-start.2) | async-done | bytes 524320 | tf_op jit(solution)/shard_map/all_to_all | solution.py:56
  56.6 0.8 copy-done.3
  57.5 2.3 %fusion.16 = f32[512,1024]{1,0:T(8,128)S(1)} fusion(bf16[512,512]{1,0:T(8,128)(2,1)} %bitcast.155, bf16[1,1024,512]{2,1,0:T(8,128)(2,1)} %param.12), kind=kOutput, calls=%fused_computation.38 | convolution fusion | flops 536870912 | bytes 3670016 | tf_op jit(solution)/shard_map/arc,ahc->arh/dot_general | solution.py:28
  59.8 2.6 %fusion.22 = f32[512,512]{1,0:T(8,128)S(1)} fusion(bf16[1,512,1024]{2,1,0:T(8,128)(2,1)S(1)} %copy-done, f32[512,1024]{1,0:T(8,128)S(1)} %copy-done.9, f32[512,1024]{1,0:T(8,128)S(1)} %fusion.16, f32[512,1024]{1,0:T(8,128)} %fusion.20), kind=kOutput, calls=%fused_computation.44 | convolution fusion | flops 542113792 | bytes 8388608 | tf_op jit(solution)/shard_map/arh,ach->arc/dot_general | solution.py:64
  62.4 0.8 fusion.3
  63.2 0.8 copy.73
  64.0 0.5 broadcast.136
  64.5 4.6 %reduce.3 = bf16[512,512]{1,0:T(8,128)(2,1)} reduce(bf16[512,1,512]{2,1,0:T(2,128)(2,1)S(1)} %bitcast.158, bf16[]{:T(256)} %broadcast.136), dimensions={1}, to_apply=%bitcast.145.reduce_sub_computation | reduce | bytes 1048578
  69.1 2.2 %reshape.403 = bf16[8,2,16384]{2,1,0:T(2,128)(2,1)} reshape(bf16[512,512]{1,0:T(8,128)(2,1)} %reduce.3) | data formatting | bytes 1048576
  71.4 3.7 %all-to-all-start.3 = ((bf16[8,2,16384]{2,1,0:T(2,128)(2,1)}), bf16[8,2,16384]{2,1,0:T(2,128)(2,1)S(1)}, u32[]{:S(2)}, u32[]{:S(2)}) async-start(bf16[8,2,16384]{2,1,0:T(2,128)(2,1)} %reshape.403), calls=%async_computation.3 | async-start | bytes 1048576 | tf_op jit(solution)/shard_map/all_to_all | solution.py:69
  75.1 2.9 %fusion.2 = bf16[1,512,512]{2,1,0:T(8,128)(2,1)S(1)} fusion(f32[512,1024]{1,0:T(8,128)} %fusion.20, bf16[1,1024,512]{2,1,0:T(8,128)(2,1)S(1)} %copy-done.6, f32[512,1024]{1,0:T(8,128)} %fusion.24), kind=kOutput, calls=%fused_computation.12 | convolution fusion | flops 540278784 | bytes 5767168 | tf_op jit(solution)/shard_map/arh,ahc->arc/dot_general | solution.py:59
  78.0 0.8 copy.74
  78.8 3.8 %reduce.2 = bf16[512,512]{1,0:T(8,128)(2,1)S(1)} reduce(bf16[512,1,512]{2,1,0:T(2,128)(2,1)S(1)} %bitcast.159, bf16[]{:T(256)} %broadcast.136), dimensions={1}, to_apply=%bitcast.146.reduce_sub_computation | reduce | bytes 1048578
  82.7 1.2 reshape.401
  83.9 6.3 %all-to-all-done.3 = bf16[8,2,16384]{2,1,0:T(2,128)(2,1)S(1)} async-done(((bf16[8,2,16384]{2,1,0:T(2,128)(2,1)}), bf16[8,2,16384]{2,1,0:T(2,128)(2,1)S(1)}, u32[]{:S(2)}, u32[]{:S(2)}) %all-to-all-start.3) | async-done | bytes 524320 | tf_op jit(solution)/shard_map/all_to_all | solution.py:69
  90.1 3.8 %all-to-all-start.1 = ((bf16[8,2,16384]{2,1,0:T(2,128)(2,1)}), bf16[8,2,16384]{2,1,0:T(2,128)(2,1)S(1)}, u32[]{:S(2)}, u32[]{:S(2)}) async-start(bf16[8,2,16384]{2,1,0:T(2,128)(2,1)} %reshape.401), calls=%async_computation.1 | async-start | bytes 1048576 | tf_op jit(solution)/shard_map/all_to_all | solution.py:68
  93.9 0.5 reshape.404
  94.6 1.2 gather_fusion.1
  95.8 1.1 reshape.363
  96.9 12.0 %all-to-all-done.1 = bf16[8,2,16384]{2,1,0:T(2,128)(2,1)S(1)} async-done(((bf16[8,2,16384]{2,1,0:T(2,128)(2,1)}), bf16[8,2,16384]{2,1,0:T(2,128)(2,1)S(1)}, u32[]{:S(2)}, u32[]{:S(2)}) %all-to-all-start.1) | async-done | bytes 524320 | tf_op jit(solution)/shard_map/all_to_all | solution.py:68
  108.9 0.5 reshape.402
  109.6 1.2 gather_fusion
  112.0 0.8 fusion.76
  112.7 2.2 %fusion.42 = f32[512,256]{1,0:T(8,128)} fusion(bf16[1,2048,512]{2,1,0:T(8,128)(2,1)} %all-gather.3.cloned.1.call-done, bf16[1,512,1024]{2,1,0:T(8,128)(2,1)S(1)} %copy-done, s32[]{:T(128)S(6)} %select_n.19), kind=kOutput, calls=%fused_computation.92 | convolution fusion | flops 134217728 | bytes 1310724 | tf_op jit(solution)/shard_map/arc,ach->arh/dot_general | solution.py:20
  114.9 2.4 %fusion.43 = f32[512,256]{1,0:T(8,128)} fusion(bf16[1,2048,512]{2,1,0:T(8,128)(2,1)} %all-gather.3.cloned.1.call-done, bf16[1,512,1024]{2,1,0:T(8,128)(2,1)} %param.11, s32[]{:T(128)S(6)} %select_n.19), kind=kOutput, calls=%fused_computation.93 | convolution fusion | flops 134217728 | bytes 1310724 | tf_op jit(solution)/shard_map/arc,ach->arh/dot_general | solution.py:21
  117.3 1.8 %fusion.15 = bf16[1,256,512]{2,1,0:T(8,128)(2,1)S(1)} fusion(bf16[1,2048,512]{2,1,0:T(8,128)(2,1)} %all-gather.5.cloned.1.call-done, f32[512,256]{1,0:T(8,128)} %fusion.43, f32[512,256]{1,0:T(8,128)} %fusion.42), kind=kOutput, calls=%fused_computation.37 | convolution fusion | flops 135135232 | bytes 1835008 | tf_op jit(solution)/shard_map/arh,arc->ahc/dot_general | solution.py:110
  119.7 0.9 copy-done.8
  123.1 0.5 copy-done.7
  123.9 0.4 fusion.11
  124.4 0.6 copy-done.12
  125.0 0.5 fusion.7
  125.8 0.4 fusion.10
  126.2 0.5 fusion.6
  127.5 0.5 fusion.5
  128.4 0.4 fusion.8
  128.8 0.5 fusion.4
  129.3 0.8 add_convert_fusion
  130.1 1.0 add_convert_fusion.1
  (67 shorter events, 8.1 us)
Async XLA Ops:
  7.2 34.4 %copy-start = (bf16[1,512,1024]{2,1,0:T(8,128)(2,1)S(1)}, bf16[1,512,1024]{2,1,0:T(8,128)(2,1)}, u32[]{:S(2)}) copy-start(bf16[1,512,1024]{2,1,0:T(8,128)(2,1)} %param.10) | copy-start | bytes 3145732
  7.2 27.6 %copy-start.14 = (f32[2]{0:T(128)S(1)}, f32[2]{0:T(128)}, u32[]{:S(2)}) copy-start(f32[2]{0:T(128)} %constant.31.clone) | copy-start | bytes 28
  7.2 27.7 %copy-start.13 = (bf16[128,512]{1,0:T(8,128)(2,1)S(1)}, bf16[128,512]{1,0:T(8,128)(2,1)}, u32[]{:S(2)}) copy-start(bf16[128,512]{1,0:T(8,128)(2,1)} %param.9) | copy-start | bytes 393220
  7.2 105.5 %all-gather.3.cloned.1.call-start = ((), (), s32[]{:S(2)}) async-start(), calls=%async_computation.4 | async-start | bytes 2621440 | tf_op jit(solution)/shard_map/all_gather | solution.py:80
  34.8 6.8 %copy-start.2 = (bf16[8,64,512]{2,1,0:T(8,128)(2,1)S(1)}, bf16[8,64,512]{2,1,0:T(8,128)(2,1)}, u32[]{:S(2)}) copy-start(bf16[8,64,512]{2,1,0:T(8,128)(2,1)} %all_to_all.42) | copy-start | bytes 1572868
  37.8 18.8 %all-to-all-start.2 = ((bf16[8,64,512]{2,1,0:T(8,128)(2,1)}), bf16[8,64,512]{2,1,0:T(8,128)(2,1)S(1)}, u32[]{:S(2)}, u32[]{:S(2)}) async-start(bf16[8,64,512]{2,1,0:T(8,128)(2,1)} %bitcast.11), calls=%async_computation.2 | async-start | bytes 1048576 | tf_op jit(solution)/shard_map/all_to_all | solution.py:56
  41.3 2.3 %copy-start.4 = (bf16[1,512,1024]{2,1,0:T(8,128)(2,1)S(1)}, bf16[1,512,1024]{2,1,0:T(8,128)(2,1)}, u32[]{:S(2)}) copy-start(bf16[1,512,1024]{2,1,0:T(8,128)(2,1)} %param.11) | copy-start | bytes 3145732
  41.3 75.9 %all-gather.5.cloned.1.call-start = ((), (), s32[]{:S(2)}) async-start(), calls=%async_computation.5 | async-start | bytes 2621440 | tf_op jit(solution)/shard_map/all_gather | solution.py:81
  56.6 0.8 copy-start.3
  57.5 2.3 %copy-start.9 = (f32[512,1024]{1,0:T(8,128)S(1)}, f32[512,1024]{1,0:T(8,128)}, u32[]{:S(2)}) copy-start(f32[512,1024]{1,0:T(8,128)} %fusion.24) | copy-start | bytes 6291460
  64.0 11.1 %copy-start.6 = (bf16[1,1024,512]{2,1,0:T(8,128)(2,1)S(1)}, bf16[1,1024,512]{2,1,0:T(8,128)(2,1)}, u32[]{:S(2)}) copy-start(bf16[1,1024,512]{2,1,0:T(8,128)(2,1)} %param.12) | copy-start | bytes 3145732
  71.4 18.8 %all-to-all-start.3 = ((bf16[8,2,16384]{2,1,0:T(2,128)(2,1)}), bf16[8,2,16384]{2,1,0:T(2,128)(2,1)S(1)}, u32[]{:S(2)}, u32[]{:S(2)}) async-start(bf16[8,2,16384]{2,1,0:T(2,128)(2,1)} %reshape.403), calls=%async_computation.3 | async-start | bytes 1048576 | tf_op jit(solution)/shard_map/all_to_all | solution.py:69
  90.1 18.8 %all-to-all-start.1 = ((bf16[8,2,16384]{2,1,0:T(2,128)(2,1)}), bf16[8,2,16384]{2,1,0:T(2,128)(2,1)S(1)}, u32[]{:S(2)}, u32[]{:S(2)}) async-start(bf16[8,2,16384]{2,1,0:T(2,128)(2,1)} %reshape.401), calls=%async_computation.1 | async-start | bytes 1048576 | tf_op jit(solution)/shard_map/all_to_all | solution.py:68
  109.5 1.6 %copy-start.10 = (f32[128,2,512]{2,1,0:T(2,128)S(1)}, f32[128,2,512]{2,1,0:T(2,128)}, u32[]{:S(2)}) copy-start(f32[128,2,512]{2,1,0:T(2,128)} %reshape.363) | copy-start | bytes 1572868
  114.9 4.2 %copy-start.1 = (bf16[1,2048,512]{2,1,0:T(8,128)(2,1)S(1)}, bf16[1,2048,512]{2,1,0:T(8,128)(2,1)}, u32[]{:S(2)}) copy-start(bf16[1,2048,512]{2,1,0:T(8,128)(2,1)} %all-gather.3.cloned.1.call-done) | copy-start | bytes 6291460
  117.2 2.2 %copy-start.5 = (bf16[1,512,1024]{2,1,0:T(8,128)(2,1)S(1)}, bf16[1,512,1024]{2,1,0:T(8,128)(2,1)}, u32[]{:S(2)}) copy-start(bf16[1,512,1024]{2,1,0:T(8,128)(2,1)} %param.11) | copy-start | bytes 3145732
  119.1 1.6 %copy-start.8 = (bf16[1,2048,512]{2,1,0:T(8,128)(2,1)S(1)}, bf16[1,2048,512]{2,1,0:T(8,128)(2,1)}, u32[]{:S(2)}) copy-start(bf16[1,2048,512]{2,1,0:T(8,128)(2,1)} %all-gather.5.cloned.1.call-done) | copy-start | bytes 6291460
  122.4 1.2 copy-start.7
  122.7 1.2 copy-start.11
  123.9 1.0 copy-start.12
Sparse Core Ops, SparseCore 0:
  34.9 34.2 all-gather.2
  71.0 35.2 all-gather.4
where the time goes:
time: 139 us; the launch traced here: 138 us
  waiting for transfers between devices  29.3 us (21%)
  matrix products  27 us (19%)
  blocking collectives  21.6 us (16%)
  local copies, waits for them, and re-layouts  19.4 us (14%)
  other arithmetic  15 us (11%)
  between operations  14.6 us (11%)
  starting transfers between devices  11.2 us (8%)
    all_to_all x1, blocking collectives, on_device(): lax.all_to_all(send_tokens, 'expert', split_axis=0, concat_axis=1, tiled=...  21.6 us
    all_to_all x1, waiting for transfers between devices, on_device(): lax.all_to_all(out_rows, 'expert', split_axis=1, concat_axis=0, tiled=True)  12 us
    all_to_all x1, waiting for transfers between devices, on_device(): lax.all_to_all(send_cot, 'expert', split_axis=0, concat_axis=1, tiled=True)  10.9 us
    unnamed x38, local copies, waits for them, and re-layouts  8.94 us
    unnamed x2, other arithmetic  8.43 us
    all_to_all x1, waiting for transfers between devices, on_device(): lax.all_to_all(input_rows, 'expert', split_axis=1, concat_axis=0, tiled=T...  6.27 us
    dot_general x5, matrix products, arm_forward(): jnp.einsum('arc,ach->arh', rows_in, up_w, preferred_element_type=jnp.floa...  5.34 us
    dot_general x5, matrix products, arm_forward(): jnp.einsum('arc,ach->arh', rows_in, gate_w, preferred_element_type=jnp.fl...  5.13 us
  transfers between devices with their start and end apart: 5, of which 3 were waited for; matrix products, arithmetic and copies ran while one was open for 30% of the time, Pallas kernels for 0%

commit v1 on v0

--- a/solution.py
+++ b/solution.py
@@ -1,11 +1,19 @@
+import functools
+
 import jax
 import jax.numpy as jnp
 from jax import lax
+from jax.experimental import pallas as pl
+from jax.experimental.pallas import tpu as pltpu
 from jax.sharding import PartitionSpec as P
 
 fact_share = 0.7
 counter_share = 0.3
 
+F32 = jnp.float32
+BF16 = jnp.bfloat16
+CODE_ROWS = 16
+VMEM_BYTES = 32 * 1024 * 1024
 
 def rounded(value):
     return lax.optimization_barrier(value.astype(jnp.bfloat16)).astype(jnp.float32)
@@ -115,9 +123,297 @@
     return (head_output, grad_tokens, grad_gate, grad_up, grad_down)
 
 
+def mm(left, right):
+    return jnp.dot(left, right, preferred_element_type=F32)
+
+
+def mm_nt(left, right):
+    return lax.dot_general(left, right, (((1,), (1,)), ((), ())), preferred_element_type=F32)
+
+
+def mm_tn(left, right):
+    return lax.dot_general(left, right, (((0,), (0,)), ((), ())), preferred_element_type=F32)
+
+
+def selection(code_tile, arm, capacity):
+    count = code_tile.shape[1]
+    named = (code_tile == arm).astype(BF16)
+    before = lax.broadcasted_iota(jnp.int32, (count, count), 0)
+    after = lax.broadcasted_iota(jnp.int32, (count, count), 1)
+    ranks = mm(named, (before < after).astype(BF16))
+    named = named.astype(F32)
+    hit = named[0:1] + named[1:2]
+    rank = ranks[0:1] + ranks[1:2]
+    slot = lax.broadcasted_iota(jnp.int32, (capacity, count), 0).astype(F32)
+    chosen = jnp.where(slot == rank, hit, 0.0)
+    share = jnp.sum(
+        chosen * (fact_share * named[0:1] + counter_share * named[1:2]), axis=1, keepdims=True
+    )
+    return chosen.astype(BF16), share
+
+
+def forward_kernel(blocks, arm_ref, *refs):
+    token_refs = refs[:blocks]
+    gate_ref, up_ref, down_ref = refs[blocks : blocks + 3]
+    keep_ref, give_ref, rows_ref, sel_ref, share_ref, hid_ref, act_ref, slope_ref, total = refs[
+        blocks + 3 :
+    ]
+    step = pl.program_id(0)
+    capacity, count = sel_ref.shape[1:]
+
+    @pl.when(step == 0)
+    def _():
+        arm = arm_ref[0].astype(F32)
+        for b in range(blocks):
+            chosen, share = selection(
+                token_refs[b][count : count + CODE_ROWS, 0:count].astype(F32), arm, capacity
+            )
+            sel_ref[b] = chosen
+            share_ref[b * capacity : (b + 1) * capacity] = jnp.broadcast_to(share, (capacity, 128))
+            rows_ref[b * capacity : (b + 1) * capacity] = mm(chosen, token_refs[b][0:count]).astype(
+                BF16
+            )
+        total[...] = jnp.zeros_like(total)
+
+    gate_pre = mm(rows_ref[...], gate_ref[...])
+    up_pre = mm(rows_ref[...], up_ref[...])
+    sig = jax.nn.sigmoid(gate_pre)
+    activated = gate_pre * sig
+    hidden = (activated * up_pre).astype(BF16)
+    hid_ref[0] = hidden
+    act_ref[0] = activated.astype(BF16)
+    slope_ref[0] = (up_pre * (sig * (1.0 + gate_pre * (1.0 - sig)))).astype(BF16)
+    total[...] += mm(hidden, down_ref[...])
+
+    @pl.when(step == pl.num_programs(0) - 1)
+    def _():
+        for b in range(blocks):
+            at = slice(b * capacity, (b + 1) * capacity)
+            out_rows = total[at].astype(BF16).astype(F32) * share_ref[at, 0:1]
+            placed = mm_tn(sel_ref[b], out_rows.astype(BF16)).astype(BF16)
+            if b < blocks // 2:
+                keep_ref[b] = placed
+            else:
+                give_ref[b - blocks // 2] = placed
+
+
+def backward_kernel(blocks, *refs):
+    cot_refs = refs[:blocks]
+    sel_ref, share_ref, act_ref, slope_ref, gate_ref, up_ref, down_ref = refs[blocks : blocks + 7]
+    keep_ref, give_ref, cots_ref, dgate_ref, dup_ref, total = refs[blocks + 7 :]
+    step = pl.program_id(0)
+    capacity, count = sel_ref.shape[1:]
+
+    @pl.when(step == 0)
+    def _():
+        for b in range(blocks):
+            at = slice(b * capacity, (b + 1) * capacity)
+            picked = mm(sel_ref[b], cot_refs[b][...])
+            cots_ref[at] = (picked * share_ref[at, 0:1]).astype(BF16)
+        total[...] = jnp.zeros_like(total)
+
+    d_hidden = mm_nt(cots_ref[...], down_ref[...])
+    d_up = (d_hidden * act_ref[0].astype(F32)).astype(BF16)
+    d_gate = (d_hidden * slope_ref[0].astype(F32)).astype(BF16)
+    dup_ref[0] = d_up
+    dgate_ref[0] = d_gate
+    total[...] += mm_nt(d_gate, gate_ref[...]) + mm_nt(d_up, up_ref[...])
+
+    @pl.when(step == pl.num_programs(0) - 1)
+    def _():
+        for b in range(blocks):
+            at = slice(b * capacity, (b + 1) * capacity)
+            placed = mm_tn(sel_ref[b], total[at].astype(BF16)).astype(BF16)
+            if b < blocks // 2:
+                keep_ref[b] = placed
+            else:
+                give_ref[b - blocks // 2] = placed
+
+
+def weight_kernel(place_ref, rows_ref, cots_ref, hid_ref, dgate_ref, dup_ref, *outs):
+    half = rows_ref.shape[1] // 2
+    for j, (first, second) in zip((3, 2, 1, 0), zip(outs[0::2], outs[1::2])):
+        quarter = place_ref[0] ^ j
+        for k, d_ref in enumerate((dgate_ref, dup_ref)):
+            part = mm_tn(rows_ref[...], d_ref[quarter]).astype(BF16)
+            first[k] = part[:half]
+            second[k] = part[half:]
+        part = mm_tn(hid_ref[quarter], cots_ref[...]).astype(BF16)
+        first[2] = part[:, :half]
+        second[2] = part[:, half:]
+
+
+def vmem():
+    return pl.BlockSpec(memory_space=pltpu.VMEM)
+
+
+def smem():
+    return pl.BlockSpec(memory_space=pltpu.SMEM)
+
+
+def weight_specs(width, chunk):
+    tall = pl.BlockSpec((width, chunk), lambda c: (0, c))
+    wide = pl.BlockSpec((chunk, width), lambda c: (c, 0))
+    return [tall, tall, wide]
+
+
+def run_forward(arm, tokens, capacity, w_gate, w_up, w_down, chunk):
+    blocks = len(tokens)
+    width, hidden_width = w_gate.shape
+    count = tokens[0].shape[0] - CODE_ROWS
+    rows = blocks * capacity
+    steps = hidden_width // chunk
+    whole = lambda *shape: pl.BlockSpec(shape, lambda c: (0,) * len(shape))
+    piece = pl.BlockSpec((1, rows, chunk), lambda c: (c, 0, 0))
+    return pl.pallas_call(
+        functools.partial(forward_kernel, blocks),
+        grid=(steps,),
+        in_specs=[smem()]
+        + [whole(*tokens[0].shape)] * blocks
+        + weight_specs(width, chunk),
+        out_specs=[whole(blocks // 2, count, width)] * 2
+        + [whole(rows, width), whole(blocks, capacity, count), whole(rows, 128)]
+        + [piece] * 3,
+        out_shape=[jax.ShapeDtypeStruct((blocks // 2, count, width), BF16)] * 2
+        + [
+            jax.ShapeDtypeStruct((rows, width), BF16),
+            jax.ShapeDtypeStruct((blocks, capacity, count), BF16),
+            jax.ShapeDtypeStruct((rows, 128), F32),
+        ]
+        + [jax.ShapeDtypeStruct((steps, rows, chunk), BF16)] * 3,
+        scratch_shapes=[pltpu.VMEM((rows, width), F32)],
+        compiler_params=pltpu.CompilerParams(vmem_limit_bytes=VMEM_BYTES),
+        cost_estimate=pl.CostEstimate(
+            flops=6 * rows * width * hidden_width, bytes_accessed=8 << 20, transcendentals=0
+        ),
+        name="arm_forward",
+    )(arm, *tokens, w_gate, w_up, w_down)
+
+
+def run_backward(cots, sel, share, act, slope, w_gate, w_up, w_down, chunk):
+    blocks = len(cots)
+    width, hidden_width = w_gate.shape
+    capacity, count = sel.shape[1:]
+    rows = blocks * capacity
+    steps = hidden_width // chunk
+    whole = lambda *shape: pl.BlockSpec(shape, lambda c: (0,) * len(shape))
+    piece = pl.BlockSpec((1, rows, chunk), lambda c: (c, 0, 0))
+    return pl.pallas_call(
+        functools.partial(backward_kernel, blocks),
+        grid=(steps,),
+        in_specs=[whole(count, width)] * blocks
+        + [whole(*sel.shape), whole(*share.shape), piece, piece]
+        + weight_specs(width, chunk),
+        out_specs=[whole(blocks // 2, count, width)] * 2 + [whole(rows, width), piece, piece],
+        out_shape=[jax.ShapeDtypeStruct((blocks // 2, count, width), BF16)] * 2
+        + [jax.ShapeDtypeStruct((rows, width), BF16)]
+        + [jax.ShapeDtypeStruct((steps, rows, chunk), BF16)] * 2,
+        scratch_shapes=[pltpu.VMEM((rows, width), F32)],
+        compiler_params=pltpu.CompilerParams(vmem_limit_bytes=VMEM_BYTES),
+        cost_estimate=pl.CostEstimate(
+            flops=6 * rows * width * hidden_width, bytes_accessed=8 << 20, transcendentals=0
+        ),
+        name="arm_backward",
+    )(*cots, sel, share, act, slope, w_gate, w_up, w_down)
+
+
+def run_weights(place, rows, cots, hid, dgate, dup):
+    width = rows.shape[1]
+    chunk = hid.shape[2]
+    return pl.pallas_call(
+        weight_kernel,
+        in_specs=[smem()] + [vmem()] * 5,
+        out_specs=[vmem()] * 8,
+        out_shape=[jax.ShapeDtypeStruct((3, width // 2, chunk), BF16)] * 8,
+        compiler_params=pltpu.CompilerParams(vmem_limit_bytes=VMEM_BYTES),
+        cost_estimate=pl.CostEstimate(
+            flops=6 * rows.shape[0] * width * hid.shape[0] * chunk,
+            bytes_accessed=8 << 20,
+            transcendentals=0,
+        ),
+        name="arm_weights",
+    )(place, rows, cots, hid, dgate, dup)
+
+
+def on_line(tokens, codes, cotangent, w_gate, w_up, w_down):
+    token_count, width = tokens.shape
+    arm_count = lax.axis_size("expert")
+    capacity = 4 * token_count // arm_count
+    w_gate, w_up, w_down = w_gate[0], w_up[0], w_down[0]
+    hidden_width = w_gate.shape[1]
+    chunk = hidden_width // lax.axis_size("dp")
+    expert = lax.axis_index("expert")
+    arm = jnp.reshape(expert, (1,)).astype(jnp.int32)
+    place = jnp.reshape(lax.axis_index("dp"), (1,)).astype(jnp.int32)
+    z = expert // 2
+    edge = (z == 0) | (z == 3)
+
+    def along(pairs):
+        return [(2 * s + c, 2 * d + c) for s, d in pairs for c in (0, 1)]
+
+    far = along([(0, 3), (3, 0), (1, 2), (2, 1)])
+    near = along([(0, 1), (1, 0), (2, 3), (3, 2)])
+    skip = along([(0, 2), (2, 3), (3, 1), (1, 0)])
+    skip_back = along([(2, 0), (3, 2), (1, 3), (0, 1)])
+    core = [(e, e ^ 1) for e in range(8)]
+    x_pair = [(i, i ^ 1) for i in range(4)]
+    y_pair = [(i, i ^ 2) for i in range(4)]
+    send = lambda value, pairs: lax.ppermute(value, "expert", pairs)
+    send_dp = lambda value, pairs: lax.ppermute(value, "dp", pairs)
+
+    code_rows = jnp.pad(
+        codes.T.astype(BF16), ((0, CODE_ROWS - 2), (0, width - token_count))
+    )
+    token_part = jnp.concatenate([tokens, code_rows], axis=0)
+
+    def gather(own):
+        from_far = send(own, far)
+        from_near = send(own, near)
+        from_skip = send(jnp.where(edge, own, from_far), skip)
+        mine = [own, from_far, from_near, from_skip]
+        return mine + [send(part, core) for part in mine]
+
+    all_tokens = gather(token_part)
+    all_cots = gather(cotangent)
+
+    head_keep, head_give, rows, sel, share, hid, act, slope = run_forward(
+        arm, all_tokens, capacity, w_gate, w_up, w_down, chunk
+    )
+    grad_keep, grad_give, cots, dgate, dup = run_backward(
+        all_cots, sel, share, act, slope, w_gate, w_up, w_down, chunk
+    )
+
+    def reduce(keep, give):
+        got = send(give, core)
+        both = [keep[k].astype(F32) + got[k].astype(F32) for k in range(4)]
+        own, for_far, for_near, for_skip = both
+        from_skip = send(for_skip.astype(BF16), skip_back).astype(F32)
+        from_near = send(for_near.astype(BF16), near).astype(F32)
+        for_far = for_far + jnp.where(edge, 0.0, from_skip)
+        from_far = send(for_far.astype(BF16), far).astype(F32)
+        return (own + from_near + from_far + jnp.where(edge, from_skip, 0.0)).astype(BF16)
+
+    head_output = reduce(head_keep, head_give)
+    grad_tokens = reduce(grad_keep, grad_give)
+
+    d0, d1, y0, y1, x0, x1, k0, k1 = run_weights(place, rows, cots, hid, dgate, dup)
+    add = lambda a, b: a.astype(F32) + b.astype(F32)
+    y0 = add(y0, send_dp(d0, x_pair))
+    x1 = add(x1, send_dp(d1, y_pair))
+    k0 = add(k0, send_dp(x0, x_pair))
+    k1 = add(k1, send_dp(y1, y_pair))
+    k0 = add(k0, send_dp(y0.astype(BF16), y_pair)).astype(BF16)
+    k1 = add(k1, send_dp(x1.astype(BF16), x_pair)).astype(BF16)
+    grad_gate = jnp.concatenate([k0[0], k1[0]], axis=0)[None]
+    grad_up = jnp.concatenate([k0[1], k1[1]], axis=0)[None]
+    grad_down = jnp.concatenate([k0[2], k1[2]], axis=1)[None]
+    return (head_output, grad_tokens, grad_gate, grad_up, grad_down)
+
+
 def solution(mesh):
+    on_square_of_lines = mesh.shape["dp"] == 4 and mesh.shape["expert"] == 8
     return jax.shard_map(
-        on_device,
+        on_line if on_square_of_lines else on_device,
         mesh=mesh,
         in_specs=(
             P(("dp", "expert"), None),

time: 139 us -> 89.4 us (0.64)
  matrix products: 27 us -> 0 us
  blocking collectives: 21.6 us -> 0 us
  local copies, waits for them, and re-layouts: 19.4 us -> 2.52 us
  starting transfers between devices: 11.2 us -> 27.3 us
  between operations: 14.6 us -> 0.85 us
  Pallas kernels: 0 us -> 11.3 us
  waiting for transfers between devices: 29.3 us -> 39.2 us
  other arithmetic: 15 us -> 7.36 us
    ppermute x0 -> x28, waiting for transfers between devices: none -> 39.2 us  [the longest x22 30.7 us: on_line(): send = lambda value, pairs: lax.ppermute(value, 'expert', pairs)]
    all_to_all x3 -> x0, waiting for transfers between devices: 29.2 us -> none  [the longest x1 12 us: on_device(): lax.all_to_all(out_rows, 'expert', split_axis=1, concat_axis=0, tiled=True)]
    ppermute x0 -> x28, starting transfers between devices: none -> 27.3 us  [the longest x22 20 us: on_line(): send = lambda value, pairs: lax.ppermute(value, 'expert', pairs)]
    dot_general x30 -> x0, matrix products: 27 us -> none  [the longest x5 5.34 us: arm_forward(): jnp.einsum('arc,ach->arh', rows_in, up_w, preferred_element_type=jnp.floa...]
    all_to_all x1 -> x0, blocking collectives: 21.6 us -> none  [on_device(): lax.all_to_all(send_tokens, 'expert', split_axis=0, concat_axis=1, tiled=...]
    pallas_call x0 -> x3, Pallas kernels: none -> 11.3 us  [the longest x1 4.85 us: run_forward(): pl.pallas_call(functools.partial(forward_kernel, blocks), grid=(steps,),...]
    all_to_all x3 -> x0, starting transfers between devices: 11 us -> none  [the longest x1 3.78 us: on_device(): lax.all_to_all(out_rows, 'expert', split_axis=1, concat_axis=0, tiled=True)]
    unnamed x2 -> x0, other arithmetic: 8.43 us -> none
  transfers between devices with their start and end apart: 5 -> 28, of which waited for: 3 -> 8; matrix products, arithmetic and copies ran while one was open for 30% -> 6% of each run, Pallas kernels for 0% -> 5%
where the time goes in v1:
time: 89.4 us; the launch traced here: 88.6 us
  waiting for transfers between devices  39.2 us (44%)
  starting transfers between devices  27.3 us (31%)
  Pallas kernels  11.3 us (13%)
  other arithmetic  7.36 us (8%)
  local copies, waits for them, and re-layouts  2.52 us (3%)
    ppermute x22, waiting for transfers between devices, on_line(): send = lambda value, pairs: lax.ppermute(value, 'expert', pairs)  30.7 us
    ppermute x22, starting transfers between devices, on_line(): send = lambda value, pairs: lax.ppermute(value, 'expert', pairs)  20 us
    ppermute x6, waiting for transfers between devices, on_line(): send_dp = lambda value, pairs: lax.ppermute(value, 'dp', pairs)  8.5 us
    ppermute x6, starting transfers between devices, on_line(): send_dp = lambda value, pairs: lax.ppermute(value, 'dp', pairs)  7.25 us
    pallas_call x1, Pallas kernels, run_forward(): pl.pallas_call(functools.partial(forward_kernel, blocks), grid=(steps,),...  4.85 us
    pallas_call x1, Pallas kernels, run_backward(): pl.pallas_call(functools.partial(backward_kernel, blocks), grid=(steps,),...  4.61 us
    unnamed x12, local copies, waits for them, and re-layouts  2.47 us
    select_n x2, other arithmetic, gather(): from_skip = send(jnp.where(edge, own, from_far), skip)  1.86 us
  transfers between devices with their start and end apart: 28, of which 8 were waited for; matrix products, arithmetic and copies ran while one was open for 6% of the time, Pallas kernels for 5%

profile of v1, /device:TPU:0, one launch (start us, length us, event | category | flops | bytes accessed | tf_op | source)
XLA Modules:
  0.0 88.6 jit_solution(3939438878766777732)
XLA Ops:
  0.6 0.8 convert_bitcast_fusion
  1.4 0.9 %fusion.11.refs_0_ = bf16[144,512]{1,0:T(8,128)(2,1)S(1)} fusion(bf16[2,128]{1,0:T(2,128)(2,1)S(1)} %convert_bitcast_fusion, bf16[128,512]{1,0:T(8,128)(2,1)} %param.6), kind=kLoop, calls=%fused_computation.29 | loop fusion | flops 442368 | bytes 279040 | tf_op jit(solution)/shard_map/concatenate | solution.py:367
  2.3 5.1 %collective-permute-start = (bf16[144,512]{1,0:T(8,128)(2,1)S(1)}, bf16[144,512]{1,0:T(8,128)(2,1)S(1)}, u32[]{:S(2)}, u32[]{:S(2)}) collective-permute-start(bf16[144,512]{1,0:T(8,128)(2,1)S(1)} %fusion.11.refs_0_), channel_id=1, source_target_pairs={{0,6},{1,7},{6,0},{7,1},{2,4},{3,5},{4,2},{5,3},{8,14},{9,15},{14,... | collective-permute-start | bytes 442376 | tf_op jit(solution)/shard_map/ppermute | solution.py:361
  7.4 4.7 %collective-permute-done.refs_1_ = bf16[144,512]{1,0:T(8,128)(2,1)S(1)} collective-permute-done((bf16[144,512]{1,0:T(8,128)(2,1)S(1)}, bf16[144,512]{1,0:T(8,128)(2,1)S(1)}, u32[]{:S(2)}, u32[]{:S(2)}) %collective-permute-start) | collective-permute-done | bytes 147488 | tf_op jit(solution)/shard_map/ppermute | solution.py:361
  12.2 0.9 %broadcast_select_fusion = bf16[144,512]{1,0:T(8,128)(2,1)S(1)} fusion(bf16[144,512]{1,0:T(8,128)(2,1)S(1)} %collective-permute-done.refs_1_, pred[]{:T(512)S(6)} %or.3, bf16[2,128]{1,0:T(2,128)(2,1)S(1)} %convert_bitcast_fusion, bf16[128,512]{1,0:T(8,128)(2,1)} %param.6), kind=kLoop, calls=%fused_computation.30 | loop fusion | flops 516096 | bytes 426497 | tf_op jit(solution)/shard_map/jit(_where)/select_n | solution.py:372
  13.1 3.1 %collective-permute-start.2 = (bf16[144,512]{1,0:T(8,128)(2,1)S(1)}, bf16[144,512]{1,0:T(8,128)(2,1)S(1)}, u32[]{:S(2)}, u32[]{:S(2)}) collective-permute-start(bf16[144,512]{1,0:T(8,128)(2,1)S(1)} %broadcast_select_fusion), channel_id=1, source_target_pairs={{0,4},{1,5},{4,6},{5,7},{6,2},{7,3},{2,0},{3,1},{8,12},{9,13},{12,... | collective-permute-start | bytes 442376 | tf_op jit(solution)/shard_map/ppermute | solution.py:361
  16.2 1.3 %collective-permute-start.11 = (bf16[128,512]{1,0:T(8,128)(2,1)}, bf16[128,512]{1,0:T(8,128)(2,1)S(1)}, u32[]{:S(2)}, u32[]{:S(2)}) collective-permute-start(bf16[128,512]{1,0:T(8,128)(2,1)} %refs_0_.1), channel_id=1, source_target_pairs={{0,6},{1,7},{6,0},{7,1},{2,4},{3,5},{4,2},{5,3},{8,14},{9,15},{14,... | collective-permute-start | bytes 393224 | tf_op jit(solution)/shard_map/ppermute | solution.py:361
  17.5 0.6 collective-permute-start.12
  18.1 6.6 %collective-permute-done.11.refs_1_ = bf16[128,512]{1,0:T(8,128)(2,1)S(1)} collective-permute-done((bf16[128,512]{1,0:T(8,128)(2,1)}, bf16[128,512]{1,0:T(8,128)(2,1)S(1)}, u32[]{:S(2)}, u32[]{:S(2)}) %collective-permute-start.11) | collective-permute-done | bytes 131104 | tf_op jit(solution)/shard_map/ppermute | solution.py:361
  24.7 0.5 collective-permute-start.5
  25.2 0.1 collective-permute-start.6
  25.3 0.9 %broadcast_select_fusion.1 = bf16[128,512]{1,0:T(8,128)(2,1)S(1)} fusion(bf16[128,512]{1,0:T(8,128)(2,1)} %refs_0_.1, bf16[128,512]{1,0:T(8,128)(2,1)S(1)} %collective-permute-done.11.refs_1_, pred[]{:T(512)S(6)} %or.3), kind=kLoop, calls=%fused_computation.41 | loop fusion | flops 65536 | bytes 393217 | tf_op jit(solution)/shard_map/jit(_where)/select_n | solution.py:372
  26.2 0.4 collective-permute-start.13
  26.6 0.2 collective-permute-start.14
  26.8 5.3 %collective-permute-done.13.refs_3_ = bf16[128,512]{1,0:T(8,128)(2,1)S(1)} collective-permute-done((bf16[128,512]{1,0:T(8,128)(2,1)S(1)}, bf16[128,512]{1,0:T(8,128)(2,1)S(1)}, u32[]{:S(2)}, u32[]{:S(2)}) %collective-permute-start.13) | collective-permute-done | bytes 131104 | tf_op jit(solution)/shard_map/ppermute | solution.py:361
  32.1 0.5 collective-permute-start.16
  32.6 0.1 collective-permute-start.17
  32.7 1.2 %copy-done.1 = bf16[1,512,1024]{2,1,0:T(8,128)(2,1)S(1)} copy-done((bf16[1,512,1024]{2,1,0:T(8,128)(2,1)S(1)}, bf16[1,512,1024]{2,1,0:T(8,128)(2,1)}, u32[]{:S(2)}) %copy-start.1) | copy-done | bytes 1048600
  33.9 1.2 %copy-done.3 = bf16[1,1024,512]{2,1,0:T(8,128)(2,1)S(1)} copy-done((bf16[1,1024,512]{2,1,0:T(8,128)(2,1)S(1)}, bf16[1,1024,512]{2,1,0:T(8,128)(2,1)}, u32[]{:S(2)}) %copy-start.3) | copy-done | bytes 1048600
  35.2 4.8 %arm_forward.1 = (bf16[4,128,512]{2,1,0:T(8,128)(2,1)S(1)}, bf16[4,128,512]{2,1,0:T(8,128)(2,1)S(1)}, bf16[512,512]{1,0:T(8,128)(2,1)S(1)}, bf16[8,64,128]{2,1,0...) custom-call(s32[1]{0:T(128)} %bitcast.arm_ref, ...), custom_call_target="tpu_custom_call" | custom-call | flops 1610612736 | bytes 8388608 | tf_op jit(solution)/shard_map/arm_forward/pallas_call | solution.py:268
  40.1 4.6 %arm_backward.1 = (bf16[4,128,512]{2,1,0:T(8,128)(2,1)S(1)}, bf16[4,128,512]{2,1,0:T(8,128)(2,1)S(1)}, bf16[512,512]{1,0:T(8,128)(2,1)S(1)}, bf16[4,512,256]{2,1,0:T(8,128)(2,1)S(1)}, bf16[4,512,256]{2,1,0:T(8,128)(2,1)S(1)}) custom-call(bf16[128,512]{1,0:T(8,128)(2,1)S(1)} %copy-done.5, bf16[128,512]{1,0:T(8,128)(2,1)S(1)} %collective-permute-done.11.refs_1_, ...), custom_call_target="tpu_custom_call" | custom-call | flops 1610612736 | bytes 8388608 | tf_op jit(solution)/shard_map/arm_backward/pallas_call | solution.py:301
  44.7 1.9 %arm_weights.1 = (bf16[3,256,256]{2,1,0:T(8,128)(2,1)S(1)}, bf16[3,256,256]{2,1,0:T(8,128)(2,1)S(1)}, bf16[3,256,256]{2,1,0:T(8,128)(2,1)S(1)}, bf16[3,256,256]{...) custom-call(s32[1]{0:T(128)} %bitcast.13.place_ref, ...), custom_call_target="tpu_custom_call" | custom-call | flops 1610612736 | bytes 8388608 | tf_op jit(solution)/shard_map/arm_weights/pallas_call | solution.py:323
  46.6 1.6 %collective-permute-start.23 = (bf16[3,256,256]{2,1,0:T(8,128)(2,1)S(1)}, bf16[3,256,256]{2,1,0:T(8,128)(2,1)S(1)}, u32[]{:S(2)}, u32[]{:S(2)}) collective-permute-start(bf16[3,256,256]{2,1,0:T(8,128)(2,1)S(1)} %get-tuple-element.42), channel_id=1, source_target_pairs={{0,8},{8,0},{16,24},{24,16},{1,9},{9,1},{17,25},{25,17},{2,10},{10... | collective-permute-start | bytes 1179656 | tf_op jit(solution)/shard_map/ppermute | solution.py:362
  48.1 1.5 %collective-permute-start.26 = (bf16[3,256,256]{2,1,0:T(8,128)(2,1)S(1)}, bf16[3,256,256]{2,1,0:T(8,128)(2,1)S(1)}, u32[]{:S(2)}, u32[]{:S(2)}) collective-permute-start(bf16[3,256,256]{2,1,0:T(8,128)(2,1)S(1)} %get-tuple-element.46), channel_id=1, source_target_pairs={{0,16},{8,24},{16,0},{24,8},{1,17},{9,25},{17,1},{25,9},{2,18},{10... | collective-permute-start | bytes 1179656 | tf_op jit(solution)/shard_map/ppermute | solution.py:362
  49.7 0.5 collective-permute-start.18
  50.2 0.5 collective-permute-start.22
  50.7 7.9 %collective-permute-done.23 = bf16[3,256,256]{2,1,0:T(8,128)(2,1)S(1)} collective-permute-done((bf16[3,256,256]{2,1,0:T(8,128)(2,1)S(1)}, bf16[3,256,256]{2,1,0:T(8,128)(2,1)S(1)}, u32[]{:S(2)}, u32[]{:S(2)}) %collective-permute-start.23) | collective-permute-done | bytes 393248 | tf_op jit(solution)/shard_map/ppermute | solution.py:362
  58.6 1.5 %collective-permute-start.25 = (bf16[3,256,256]{2,1,0:T(8,128)(2,1)S(1)}, bf16[3,256,256]{2,1,0:T(8,128)(2,1)S(1)}, u32[]{:S(2)}, u32[]{:S(2)}) collective-permute-start(bf16[3,256,256]{2,1,0:T(8,128)(2,1)S(1)} %get-tuple-element.44), channel_id=1, source_target_pairs={{0,16},{8,24},{16,0},{24,8},{1,17},{9,25},{17,1},{25,9},{2,18},{10... | collective-permute-start | bytes 1179656 | tf_op jit(solution)/shard_map/ppermute | solution.py:362
  60.1 0.1 add_convert_fusion.3
  60.2 0.6 collective-permute-start.24
  60.8 0.1 add_convert_fusion.1
  61.0 1.5 %collective-permute-start.27 = (bf16[3,256,256]{2,1,0:T(8,128)(2,1)S(1)}, bf16[3,256,256]{2,1,0:T(8,128)(2,1)S(1)}, u32[]{:S(2)}, u32[]{:S(2)}) collective-permute-start(bf16[3,256,256]{2,1,0:T(8,128)(2,1)S(1)} %add_convert_fusion.1), channel_id=1, source_target_pairs={{0,8},{8,0},{16,24},{24,16},{1,9},{9,1},{17,25},{25,17},{2,10},{10... | collective-permute-start | bytes 1179656 | tf_op jit(solution)/shard_map/ppermute | solution.py:362
  62.4 0.1 fusion.12
  62.5 1.3 %collective-permute-start.9 = (bf16[128,512]{1,0:T(8,128)(2,1)S(1)}, bf16[128,512]{1,0:T(8,128)(2,1)S(1)}, u32[]{:S(2)}, u32[]{:S(2)}) collective-permute-start(bf16[128,512]{1,0:T(8,128)(2,1)S(1)} %get-tuple-element.50), channel_id=1, source_target_pairs={{4,0},{5,1},{6,4},{7,5},{2,6},{3,7},{0,2},{1,3},{12,8},{13,9},{14,... | collective-permute-start | bytes 393224 | tf_op jit(solution)/shard_map/ppermute | solution.py:361
  63.9 4.5 %collective-permute-done.9 = bf16[128,512]{1,0:T(8,128)(2,1)S(1)} collective-permute-done((bf16[128,512]{1,0:T(8,128)(2,1)S(1)}, bf16[128,512]{1,0:T(8,128)(2,1)S(1)}, u32[]{:S(2)}, u32[]{:S(2)}) %collective-permute-start.9) | collective-permute-done | bytes 131104 | tf_op jit(solution)/shard_map/ppermute | solution.py:361
  68.4 0.4 collective-permute-start.20
  68.9 5.5 %collective-permute-done.20 = bf16[128,512]{1,0:T(8,128)(2,1)S(1)} collective-permute-done((bf16[128,512]{1,0:T(8,128)(2,1)S(1)}, bf16[128,512]{1,0:T(8,128)(2,1)S(1)}, u32[]{:S(2)}, u32[]{:S(2)}) %collective-permute-start.20) | collective-permute-done | bytes 131104 | tf_op jit(solution)/shard_map/ppermute | solution.py:361
  74.5 2.1 %collective-permute-start.19 = (bf16[128,512]{1,0:T(8,128)(2,1)S(1)}, bf16[128,512]{1,0:T(8,128)(2,1)S(1)}, u32[]{:S(2)}, u32[]{:S(2)}) collective-permute-start(bf16[128,512]{1,0:T(8,128)(2,1)S(1)} %get-tuple-element.47), channel_id=1, source_target_pairs={{0,2},{1,3},{2,0},{3,1},{4,6},{5,7},{6,4},{7,5},{8,10},{9,11},{10,... | collective-permute-start | bytes 393224 | tf_op jit(solution)/shard_map/ppermute | solution.py:361
  76.6 0.6 collective-permute-done.24
  77.2 2.1 %collective-permute-start.10 = (bf16[128,512]{1,0:T(8,128)(2,1)S(1)}, bf16[128,512]{1,0:T(8,128)(2,1)S(1)}, u32[]{:S(2)}, u32[]{:S(2)}) collective-permute-start(bf16[128,512]{1,0:T(8,128)(2,1)S(1)} %fusion.2), channel_id=1, source_target_pairs={{0,6},{1,7},{6,0},{7,1},{2,4},{3,5},{4,2},{5,3},{8,14},{9,15},{14,... | collective-permute-start | bytes 393224 | tf_op jit(solution)/shard_map/ppermute | solution.py:361
  79.3 0.2 add_convert_fusion.2
  79.5 1.8 %collective-permute-start.21 = (bf16[128,512]{1,0:T(8,128)(2,1)S(1)}, bf16[128,512]{1,0:T(8,128)(2,1)S(1)}, u32[]{:S(2)}, u32[]{:S(2)}) collective-permute-start(bf16[128,512]{1,0:T(8,128)(2,1)S(1)} %fusion.6), channel_id=1, source_target_pairs={{0,6},{1,7},{6,0},{7,1},{2,4},{3,5},{4,2},{5,3},{8,14},{9,15},{14,... | collective-permute-start | bytes 393224 | tf_op jit(solution)/shard_map/ppermute | solution.py:361
  81.3 0.2 add_convert_fusion
  81.5 4.0 %collective-permute-done.10 = bf16[128,512]{1,0:T(8,128)(2,1)S(1)} collective-permute-done((bf16[128,512]{1,0:T(8,128)(2,1)S(1)}, bf16[128,512]{1,0:T(8,128)(2,1)S(1)}, u32[]{:S(2)}, u32[]{:S(2)}) %collective-permute-start.10) | collective-permute-done | bytes 131104 | tf_op jit(solution)/shard_map/ppermute | solution.py:361
  85.5 0.7 fusion.4
  86.3 0.7 maximum_bitcast_fusion.2
  87.0 0.8 maximum_bitcast_fusion
  87.8 0.8 fusion.8
  (41 shorter events, 0.3 us)
Async XLA Ops:
  0.6 32.1 %copy-start = (bf16[1,512,1024]{2,1,0:T(8,128)(2,1)S(1)}, bf16[1,512,1024]{2,1,0:T(8,128)(2,1)}, u32[]{:S(2)}) copy-start(bf16[1,512,1024]{2,1,0:T(8,128)(2,1)} %param.9) | copy-start | bytes 3145732
  2.3 9.8 %collective-permute-start = (bf16[144,512]{1,0:T(8,128)(2,1)S(1)}, bf16[144,512]{1,0:T(8,128)(2,1)S(1)}, u32[]{:S(2)}, u32[]{:S(2)}) collective-permute-start(bf16[144,512]{1,0:T(8,128)(2,1)S(1)} %fusion.11.refs_0_), channel_id=1, source_target_pairs={{0,6},{1,7},{6,0},{7,1},{2,4},{3,5},{4,2},{5,3},{8,14},{9,15},{14,... | collective-permute-start | bytes 442376 | tf_op jit(solution)/shard_map/ppermute | solution.py:361
  7.4 17.3 %collective-permute-start.1 = (bf16[144,512]{1,0:T(8,128)(2,1)S(1)}, bf16[144,512]{1,0:T(8,128)(2,1)S(1)}, u32[]{:S(2)}, u32[]{:S(2)}) collective-permute-start(bf16[144,512]{1,0:T(8,128)(2,1)S(1)} %fusion.11.refs_0_), channel_id=1, source_target_pairs={{0,2},{1,3},{2,0},{3,1},{4,6},{5,7},{6,4},{7,5},{8,10},{9,11},{10,... | collective-permute-start | bytes 442376 | tf_op jit(solution)/shard_map/ppermute | solution.py:361
  13.1 12.1 %collective-permute-start.2 = (bf16[144,512]{1,0:T(8,128)(2,1)S(1)}, bf16[144,512]{1,0:T(8,128)(2,1)S(1)}, u32[]{:S(2)}, u32[]{:S(2)}) collective-permute-start(bf16[144,512]{1,0:T(8,128)(2,1)S(1)} %broadcast_select_fusion), channel_id=1, source_target_pairs={{0,4},{1,5},{4,6},{5,7},{6,2},{7,3},{2,0},{3,1},{8,12},{9,13},{12,... | collective-permute-start | bytes 442376 | tf_op jit(solution)/shard_map/ppermute | solution.py:361
  16.2 8.5 %collective-permute-start.11 = (bf16[128,512]{1,0:T(8,128)(2,1)}, bf16[128,512]{1,0:T(8,128)(2,1)S(1)}, u32[]{:S(2)}, u32[]{:S(2)}) collective-permute-start(bf16[128,512]{1,0:T(8,128)(2,1)} %refs_0_.1), channel_id=1, source_target_pairs={{0,6},{1,7},{6,0},{7,1},{2,4},{3,5},{4,2},{5,3},{8,14},{9,15},{14,... | collective-permute-start | bytes 393224 | tf_op jit(solution)/shard_map/ppermute | solution.py:361
  17.5 8.7 %collective-permute-start.12 = (bf16[128,512]{1,0:T(8,128)(2,1)}, bf16[128,512]{1,0:T(8,128)(2,1)S(1)}, u32[]{:S(2)}, u32[]{:S(2)}) collective-permute-start(bf16[128,512]{1,0:T(8,128)(2,1)} %refs_0_.1), channel_id=1, source_target_pairs={{0,2},{1,3},{2,0},{3,1},{4,6},{5,7},{6,4},{7,5},{8,10},{9,11},{10,... | collective-permute-start | bytes 393224 | tf_op jit(solution)/shard_map/ppermute | solution.py:361
  18.1 8.5 %collective-permute-start.3 = (bf16[144,512]{1,0:T(8,128)(2,1)S(1)}, bf16[144,512]{1,0:T(8,128)(2,1)S(1)}, u32[]{:S(2)}, u32[]{:S(2)}) collective-permute-start(bf16[144,512]{1,0:T(8,128)(2,1)S(1)} %fusion.11.refs_0_), channel_id=1, source_target_pairs={{0,1},{1,0},{2,3},{3,2},{4,5},{5,4},{6,7},{7,6},{8,9},{9,8},{10,11... | collective-permute-start | bytes 442376 | tf_op jit(solution)/shard_map/ppermute | solution.py:361
  24.7 7.9 %collective-permute-start.4 = (bf16[144,512]{1,0:T(8,128)(2,1)S(1)}, bf16[144,512]{1,0:T(8,128)(2,1)S(1)}, u32[]{:S(2)}, u32[]{:S(2)}) collective-permute-start(bf16[144,512]{1,0:T(8,128)(2,1)S(1)} %collective-permute-done.refs_1_), channel_id=1, source_target_pairs={{0,1},{1,0},{2,3},{3,2},{4,5},{5,4},{6,7},{7,6},{8,9},{9,8},{10,11... | collective-permute-start | bytes 442376 | tf_op jit(solution)/shard_map/ppermute | solution.py:361
  24.7 7.4 %collective-permute-start.5 = (bf16[144,512]{1,0:T(8,128)(2,1)S(1)}, bf16[144,512]{1,0:T(8,128)(2,1)S(1)}, u32[]{:S(2)}, u32[]{:S(2)}) collective-permute-start(bf16[144,512]{1,0:T(8,128)(2,1)S(1)} %collective-permute-done.1.refs_2_), channel_id=1, source_target_pairs={{0,1},{1,0},{2,3},{3,2},{4,5},{5,4},{6,7},{7,6},{8,9},{9,8},{10,11... | collective-permute-start | bytes 442376 | tf_op jit(solution)/shard_map/ppermute | solution.py:361
  25.2 7.5 %collective-permute-start.6 = (bf16[144,512]{1,0:T(8,128)(2,1)S(1)}, bf16[144,512]{1,0:T(8,128)(2,1)S(1)}, u32[]{:S(2)}, u32[]{:S(2)}) collective-permute-start(bf16[144,512]{1,0:T(8,128)(2,1)S(1)} %collective-permute-done.2.refs_3_), channel_id=1, source_target_pairs={{0,1},{1,0},{2,3},{3,2},{4,5},{5,4},{6,7},{7,6},{8,9},{9,8},{10,11... | collective-permute-start | bytes 442376 | tf_op jit(solution)/shard_map/ppermute | solution.py:361
  26.2 5.9 %collective-permute-start.13 = (bf16[128,512]{1,0:T(8,128)(2,1)S(1)}, bf16[128,512]{1,0:T(8,128)(2,1)S(1)}, u32[]{:S(2)}, u32[]{:S(2)}) collective-permute-start(bf16[128,512]{1,0:T(8,128)(2,1)S(1)} %broadcast_select_fusion.1), channel_id=1, source_target_pairs={{0,4},{1,5},{4,6},{5,7},{6,2},{7,3},{2,0},{3,1},{8,12},{9,13},{12,... | collective-permute-start | bytes 393224 | tf_op jit(solution)/shard_map/ppermute | solution.py:361
  26.6 13.4 %collective-permute-start.14 = (bf16[128,512]{1,0:T(8,128)(2,1)}, bf16[128,512]{1,0:T(8,128)(2,1)S(1)}, u32[]{:S(2)}, u32[]{:S(2)}) collective-permute-start(bf16[128,512]{1,0:T(8,128)(2,1)} %refs_0_.1), channel_id=1, source_target_pairs={{0,1},{1,0},{2,3},{3,2},{4,5},{5,4},{6,7},{7,6},{8,9},{9,8},{10,11... | collective-permute-start | bytes 393224 | tf_op jit(solution)/shard_map/ppermute | solution.py:361
  32.1 7.9 %collective-permute-start.15 = (bf16[128,512]{1,0:T(8,128)(2,1)S(1)}, bf16[128,512]{1,0:T(8,128)(2,1)S(1)}, u32[]{:S(2)}, u32[]{:S(2)}) collective-permute-start(bf16[128,512]{1,0:T(8,128)(2,1)S(1)} %collective-permute-done.11.refs_1_), channel_id=1, source_target_pairs={{0,1},{1,0},{2,3},{3,2},{4,5},{5,4},{6,7},{7,6},{8,9},{9,8},{10,11... | collective-permute-start | bytes 393224 | tf_op jit(solution)/shard_map/ppermute | solution.py:361
  32.1 7.9 %collective-permute-start.16 = (bf16[128,512]{1,0:T(8,128)(2,1)S(1)}, bf16[128,512]{1,0:T(8,128)(2,1)S(1)}, u32[]{:S(2)}, u32[]{:S(2)}) collective-permute-start(bf16[128,512]{1,0:T(8,128)(2,1)S(1)} %collective-permute-done.12.refs_2_), channel_id=1, source_target_pairs={{0,1},{1,0},{2,3},{3,2},{4,5},{5,4},{6,7},{7,6},{8,9},{9,8},{10,11... | collective-permute-start | bytes 393224 | tf_op jit(solution)/shard_map/ppermute | solution.py:361
  32.6 7.4 %collective-permute-start.17 = (bf16[128,512]{1,0:T(8,128)(2,1)S(1)}, bf16[128,512]{1,0:T(8,128)(2,1)S(1)}, u32[]{:S(2)}, u32[]{:S(2)}) collective-permute-start(bf16[128,512]{1,0:T(8,128)(2,1)S(1)} %collective-permute-done.13.refs_3_), channel_id=1, source_target_pairs={{0,1},{1,0},{2,3},{3,2},{4,5},{5,4},{6,7},{7,6},{8,9},{9,8},{10,11... | collective-permute-start | bytes 393224 | tf_op jit(solution)/shard_map/ppermute | solution.py:361
  32.7 1.2 %copy-start.1 = (bf16[1,512,1024]{2,1,0:T(8,128)(2,1)S(1)}, bf16[1,512,1024]{2,1,0:T(8,128)(2,1)}, u32[]{:S(2)}) copy-start(bf16[1,512,1024]{2,1,0:T(8,128)(2,1)} %param.10) | copy-start | bytes 3145732
  33.9 1.2 %copy-start.3 = (bf16[1,1024,512]{2,1,0:T(8,128)(2,1)S(1)}, bf16[1,1024,512]{2,1,0:T(8,128)(2,1)}, u32[]{:S(2)}) copy-start(bf16[1,1024,512]{2,1,0:T(8,128)(2,1)} %param.11) | copy-start | bytes 3145732
  35.2 4.9 %copy-start.2 = (bf16[1,512,1024]{2,1,0:T(8,128)(2,1)S(1)}, bf16[1,512,1024]{2,1,0:T(8,128)(2,1)}, u32[]{:S(2)}) copy-start(bf16[1,512,1024]{2,1,0:T(8,128)(2,1)} %param.10) | copy-start | bytes 3145732
  35.2 4.9 %copy-start.4 = (bf16[1,1024,512]{2,1,0:T(8,128)(2,1)S(1)}, bf16[1,1024,512]{2,1,0:T(8,128)(2,1)}, u32[]{:S(2)}) copy-start(bf16[1,1024,512]{2,1,0:T(8,128)(2,1)} %param.11) | copy-start | bytes 3145732
  35.2 4.9 %copy-start.5 = (bf16[128,512]{1,0:T(8,128)(2,1)S(1)}, bf16[128,512]{1,0:T(8,128)(2,1)}, u32[]{:S(2)}) copy-start(bf16[128,512]{1,0:T(8,128)(2,1)} %refs_0_.1) | copy-start | bytes 393220
  46.6 12.0 %collective-permute-start.23 = (bf16[3,256,256]{2,1,0:T(8,128)(2,1)S(1)}, bf16[3,256,256]{2,1,0:T(8,128)(2,1)S(1)}, u32[]{:S(2)}, u32[]{:S(2)}) collective-permute-start(bf16[3,256,256]{2,1,0:T(8,128)(2,1)S(1)} %get-tuple-element.42), channel_id=1, source_target_pairs={{0,8},{8,0},{16,24},{24,16},{1,9},{9,1},{17,25},{25,17},{2,10},{10... | collective-permute-start | bytes 1179656 | tf_op jit(solution)/shard_map/ppermute | solution.py:362
  48.1 12.1 %collective-permute-start.26 = (bf16[3,256,256]{2,1,0:T(8,128)(2,1)S(1)}, bf16[3,256,256]{2,1,0:T(8,128)(2,1)S(1)}, u32[]{:S(2)}, u32[]{:S(2)}) collective-permute-start(bf16[3,256,256]{2,1,0:T(8,128)(2,1)S(1)} %get-tuple-element.46), channel_id=1, source_target_pairs={{0,16},{8,24},{16,0},{24,8},{1,17},{9,25},{17,1},{25,9},{2,18},{10... | collective-permute-start | bytes 1179656 | tf_op jit(solution)/shard_map/ppermute | solution.py:362
  49.7 11.3 %collective-permute-start.7 = (bf16[4,128,512]{2,1,0:T(8,128)(2,1)S(1)}, bf16[4,128,512]{2,1,0:T(8,128)(2,1)S(1)}, u32[]{:S(2)}, u32[]{:S(2)}) collective-permute-start(bf16[4,128,512]{2,1,0:T(8,128)(2,1)S(1)} %get-tuple-element.27), channel_id=1, source_target_pairs={{0,1},{1,0},{2,3},{3,2},{4,5},{5,4},{6,7},{7,6},{8,9},{9,8},{10,11... | collective-permute-start | bytes 1572872 | tf_op jit(solution)/shard_map/ppermute | solution.py:361
  49.7 12.9 %collective-permute-start.18 = (bf16[4,128,512]{2,1,0:T(8,128)(2,1)S(1)}, bf16[4,128,512]{2,1,0:T(8,128)(2,1)S(1)}, u32[]{:S(2)}, u32[]{:S(2)}) collective-permute-start(bf16[4,128,512]{2,1,0:T(8,128)(2,1)S(1)} %get-tuple-element.33), channel_id=1, source_target_pairs={{0,1},{1,0},{2,3},{3,2},{4,5},{5,4},{6,7},{7,6},{8,9},{9,8},{10,11... | collective-permute-start | bytes 1572872 | tf_op jit(solution)/shard_map/ppermute | solution.py:361
  50.2 24.3 %collective-permute-start.22 = (bf16[3,256,256]{2,1,0:T(8,128)(2,1)S(1)}, bf16[3,256,256]{2,1,0:T(8,128)(2,1)S(1)}, u32[]{:S(2)}, u32[]{:S(2)}) collective-permute-start(bf16[3,256,256]{2,1,0:T(8,128)(2,1)S(1)} %get-tuple-element.40), channel_id=1, source_target_pairs={{0,8},{8,0},{16,24},{24,16},{1,9},{9,1},{17,25},{25,17},{2,10},{10... | collective-permute-start | bytes 1179656 | tf_op jit(solution)/shard_map/ppermute | solution.py:362
  58.6 20.9 %collective-permute-start.25 = (bf16[3,256,256]{2,1,0:T(8,128)(2,1)S(1)}, bf16[3,256,256]{2,1,0:T(8,128)(2,1)S(1)}, u32[]{:S(2)}, u32[]{:S(2)}) collective-permute-start(bf16[3,256,256]{2,1,0:T(8,128)(2,1)S(1)} %get-tuple-element.44), channel_id=1, source_target_pairs={{0,16},{8,24},{16,0},{24,8},{1,17},{9,25},{17,1},{25,9},{2,18},{10... | collective-permute-start | bytes 1179656 | tf_op jit(solution)/shard_map/ppermute | solution.py:362
  60.2 17.0 %collective-permute-start.24 = (bf16[3,256,256]{2,1,0:T(8,128)(2,1)S(1)}, bf16[3,256,256]{2,1,0:T(8,128)(2,1)S(1)}, u32[]{:S(2)}, u32[]{:S(2)}) collective-permute-start(bf16[3,256,256]{2,1,0:T(8,128)(2,1)S(1)} %add_convert_fusion.3), channel_id=1, source_target_pairs={{0,16},{8,24},{16,0},{24,8},{1,17},{9,25},{17,1},{25,9},{2,18},{10... | collective-permute-start | bytes 1179656 | tf_op jit(solution)/shard_map/ppermute | solution.py:362
  61.0 20.4 %collective-permute-start.27 = (bf16[3,256,256]{2,1,0:T(8,128)(2,1)S(1)}, bf16[3,256,256]{2,1,0:T(8,128)(2,1)S(1)}, u32[]{:S(2)}, u32[]{:S(2)}) collective-permute-start(bf16[3,256,256]{2,1,0:T(8,128)(2,1)S(1)} %add_convert_fusion.1), channel_id=1, source_target_pairs={{0,8},{8,0},{16,24},{24,16},{1,9},{9,1},{17,25},{25,17},{2,10},{10... | collective-permute-start | bytes 1179656 | tf_op jit(solution)/shard_map/ppermute | solution.py:362
  62.5 5.9 %collective-permute-start.9 = (bf16[128,512]{1,0:T(8,128)(2,1)S(1)}, bf16[128,512]{1,0:T(8,128)(2,1)S(1)}, u32[]{:S(2)}, u32[]{:S(2)}) collective-permute-start(bf16[128,512]{1,0:T(8,128)(2,1)S(1)} %get-tuple-element.50), channel_id=1, source_target_pairs={{4,0},{5,1},{6,4},{7,5},{2,6},{3,7},{0,2},{1,3},{12,8},{13,9},{14,... | collective-permute-start | bytes 393224 | tf_op jit(solution)/shard_map/ppermute | solution.py:361
  68.4 6.0 %collective-permute-start.20 = (bf16[128,512]{1,0:T(8,128)(2,1)S(1)}, bf16[128,512]{1,0:T(8,128)(2,1)S(1)}, u32[]{:S(2)}, u32[]{:S(2)}) collective-permute-start(bf16[128,512]{1,0:T(8,128)(2,1)S(1)} %get-tuple-element.48), channel_id=1, source_target_pairs={{4,0},{5,1},{6,4},{7,5},{2,6},{3,7},{0,2},{1,3},{12,8},{13,9},{14,... | collective-permute-start | bytes 393224 | tf_op jit(solution)/shard_map/ppermute | solution.py:361
  74.4 7.1 %collective-permute-start.8 = (bf16[128,512]{1,0:T(8,128)(2,1)S(1)}, bf16[128,512]{1,0:T(8,128)(2,1)S(1)}, u32[]{:S(2)}, u32[]{:S(2)}) collective-permute-start(bf16[128,512]{1,0:T(8,128)(2,1)S(1)} %get-tuple-element.49), channel_id=1, source_target_pairs={{0,2},{1,3},{2,0},{3,1},{4,6},{5,7},{6,4},{7,5},{8,10},{9,11},{10,... | collective-permute-start | bytes 393224 | tf_op jit(solution)/shard_map/ppermute | solution.py:361
  74.5 13.3 %collective-permute-start.19 = (bf16[128,512]{1,0:T(8,128)(2,1)S(1)}, bf16[128,512]{1,0:T(8,128)(2,1)S(1)}, u32[]{:S(2)}, u32[]{:S(2)}) collective-permute-start(bf16[128,512]{1,0:T(8,128)(2,1)S(1)} %get-tuple-element.47), channel_id=1, source_target_pairs={{0,2},{1,3},{2,0},{3,1},{4,6},{5,7},{6,4},{7,5},{8,10},{9,11},{10,... | collective-permute-start | bytes 393224 | tf_op jit(solution)/shard_map/ppermute | solution.py:361
  77.2 8.3 %collective-permute-start.10 = (bf16[128,512]{1,0:T(8,128)(2,1)S(1)}, bf16[128,512]{1,0:T(8,128)(2,1)S(1)}, u32[]{:S(2)}, u32[]{:S(2)}) collective-permute-start(bf16[128,512]{1,0:T(8,128)(2,1)S(1)} %fusion.2), channel_id=1, source_target_pairs={{0,6},{1,7},{6,0},{7,1},{2,4},{3,5},{4,2},{5,3},{8,14},{9,15},{14,... | collective-permute-start | bytes 393224 | tf_op jit(solution)/shard_map/ppermute | solution.py:361
  79.5 8.3 %collective-permute-start.21 = (bf16[128,512]{1,0:T(8,128)(2,1)S(1)}, bf16[128,512]{1,0:T(8,128)(2,1)S(1)}, u32[]{:S(2)}, u32[]{:S(2)}) collective-permute-start(bf16[128,512]{1,0:T(8,128)(2,1)S(1)} %fusion.6), channel_id=1, source_target_pairs={{0,6},{1,7},{6,0},{7,1},{2,4},{3,5},{4,2},{5,3},{8,14},{9,15},{14,... | collective-permute-start | bytes 393224 | tf_op jit(solution)/shard_map/ppermute | solution.py:361

commit v2 on v0

--- a/solution.py
+++ b/solution.py
@@ -1,11 +1,19 @@
+import functools
+
 import jax
 import jax.numpy as jnp
 from jax import lax
+from jax.experimental import pallas as pl
+from jax.experimental.pallas import tpu as pltpu
 from jax.sharding import PartitionSpec as P
 
 fact_share = 0.7
 counter_share = 0.3
 
+F32 = jnp.float32
+BF16 = jnp.bfloat16
+CODE_ROWS = 16
+VMEM_BYTES = 56 * 1024 * 1024
 
 def rounded(value):
     return lax.optimization_barrier(value.astype(jnp.bfloat16)).astype(jnp.float32)
@@ -115,9 +123,270 @@
     return (head_output, grad_tokens, grad_gate, grad_up, grad_down)
 
 
+def mm(left, right):
+    return jnp.dot(left, right, preferred_element_type=F32)
+
+
+def mm_nt(left, right):
+    return lax.dot_general(left, right, (((1,), (1,)), ((), ())), preferred_element_type=F32)
+
+
+def mm_tn(left, right):
+    return lax.dot_general(left, right, (((0,), (0,)), ((), ())), preferred_element_type=F32)
+
+
+def selections(code_tiles, arm, capacity):
+    count = code_tiles[0].shape[1]
+    named = [(tile.astype(F32) == arm).astype(F32) for tile in code_tiles]
+    before = lax.broadcasted_iota(jnp.int32, (count, count), 0)
+    after = lax.broadcasted_iota(jnp.int32, (count, count), 1)
+    ranks = mm(jnp.concatenate(named, axis=0).astype(BF16), (before < after).astype(BF16))
+    slot = lax.broadcasted_iota(jnp.int32, (capacity, count), 0).astype(F32)
+    pairs = []
+    for b, hit in enumerate(named):
+        rank = ranks[b * CODE_ROWS : b * CODE_ROWS + 1] + ranks[b * CODE_ROWS + 1 : b * CODE_ROWS + 2]
+        here = slot == rank
+        pairs.append((jnp.where(here, hit[0:1], 0.0), jnp.where(here, hit[1:2], 0.0)))
+    return pairs
+
+
+def pack_kernel(tokens_ref, cot_ref, codes_ref, out_ref):
+    count = tokens_ref.shape[0]
+    out_ref[0:count] = tokens_ref[...]
+    out_ref[count : 2 * count] = cot_ref[...]
+    out_ref[2 * count : 2 * count + CODE_ROWS] = jnp.zeros((CODE_ROWS, out_ref.shape[1]), BF16)
+    rows = lax.broadcasted_iota(jnp.int32, (CODE_ROWS, count), 0)
+    codes = codes_ref[...].astype(F32)
+    both = jnp.where(rows == 0, codes[0:1], jnp.where(rows == 1, codes[1:2], 0.0))
+    out_ref[2 * count : 2 * count + CODE_ROWS, 0:count] = both.astype(BF16)
+
+
+def arm_kernel(blocks, ins, outs_count, scalar_ref, *refs):
+    sources, refs = refs[:ins], refs[ins:]
+    outs, refs = refs[:outs_count], refs[outs_count:]
+    in_sems, out_sems, sel = refs[-3:]
+    staged, refs = refs[-3 - outs_count : -3], refs[: -3 - outs_count]
+    held, (gate_ref, up_ref, down_ref), saved = refs[0], refs[1:4], refs[4:]
+    keep_ref, give_ref = staged[:2]
+    rows, cots, hid, dgate, dup = saved[5:] if saved else staged[2:]
+    capacity, count = sel.shape[1], sel.shape[2] // 2
+    pieces = hid.shape[0]
+    targets = [held.at[b] for b in range(blocks)] + [gate_ref, up_ref, down_ref, *saved[:5]]
+    loads = [
+        pltpu.make_async_copy(source, target, in_sems.at[k])
+        for k, (source, target) in enumerate(zip(sources, targets))
+    ]
+    stores = [
+        pltpu.make_async_copy(source, target, out_sems.at[k])
+        for k, (source, target) in enumerate(zip(staged, outs))
+    ]
+    for load in loads:
+        load.start()
+    for load in loads[:blocks]:
+        load.wait()
+
+    tiles = [held[b, 2 * count : 2 * count + CODE_ROWS, 0:count] for b in range(blocks)]
+    pairs = selections(tiles, scalar_ref[0].astype(F32), capacity)
+    for b, (fact, counter) in enumerate(pairs):
+        at = slice(b * capacity, (b + 1) * capacity)
+        sel[b] = jnp.concatenate([fact, counter], axis=1).astype(BF16)
+        rows[at] = mm((fact + counter).astype(BF16), held[b, 0:count]).astype(BF16)
+        cot = held[b, count : 2 * count].astype(F32)
+        scaled = jnp.concatenate(
+            [(fact_share * cot).astype(BF16), (counter_share * cot).astype(BF16)], axis=0
+        )
+        cots[at] = mm(sel[b], scaled).astype(BF16)
+
+    for load in loads[blocks : blocks + 3]:
+        load.wait()
+    for k in range(pieces):
+        piece = hid.shape[2]
+        cut = slice(k * piece, (k + 1) * piece)
+        gate_pre = mm(rows[...], gate_ref[:, cut])
+        up_pre = mm(rows[...], up_ref[:, cut])
+        d_hidden = mm_nt(cots[...], down_ref[cut, :])
+        sig = 0.5 * jnp.tanh(0.5 * gate_pre) + 0.5
+        activated = gate_pre * sig
+        hid[k] = (activated * up_pre).astype(BF16)
+        dup[k] = (d_hidden * activated).astype(BF16)
+        dgate[k] = (d_hidden * up_pre * (sig + activated * (1.0 - sig))).astype(BF16)
+    if not saved:
+        for store in stores[2:]:
+            store.start()
+
+    total_out, total_in = None, None
+    for k in range(pieces):
+        cut = slice(k * piece, (k + 1) * piece)
+        out_part = mm(hid[k], down_ref[cut, :])
+        in_part = mm_nt(dgate[k], gate_ref[:, cut]) + mm_nt(dup[k], up_ref[:, cut])
+        total_out = out_part if k == 0 else total_out + out_part
+        total_in = in_part if k == 0 else total_in + in_part
+    for b in range(blocks):
+        at = slice(b * capacity, (b + 1) * capacity)
+        target = keep_ref if b < blocks // 2 else give_ref
+        placed = mm_tn(sel[b], total_out[at].astype(BF16))
+        target[b % (blocks // 2), 0] = (
+            fact_share * placed[:count] + counter_share * placed[count:]
+        ).astype(BF16)
+        placed = mm_tn(sel[b], total_in[at].astype(BF16))
+        target[b % (blocks // 2), 1] = (placed[:count] + placed[count:]).astype(BF16)
+    stores[0].start()
+    stores[1].start()
+
+    if saved:
+        for load in loads[blocks + 3 :]:
+            load.wait()
+        x_ref, y_ref, x_next_ref, y_next_ref, first_ref, second_ref = staged[2:]
+        all_rows = jnp.concatenate([saved[0][...], rows[...]], axis=0)
+        all_cots = jnp.concatenate([saved[1][...], cots[...]], axis=0)
+        half = all_rows.shape[1] // 2
+        quarters = (
+            (3, x_ref.at[0], y_ref.at[0], ()),
+            (1, x_ref.at[1], x_next_ref, (2, 4)),
+            (2, y_next_ref, y_ref.at[1], (5, 3)),
+            (0, first_ref, second_ref, (6, 7)),
+        )
+        for j, first, second, complete in quarters:
+            quarter = scalar_ref[1] ^ j
+            both = lambda old, new: jnp.concatenate([old[quarter], new[quarter]], axis=0)
+            for k, d_pre in enumerate((both(saved[3], dgate), both(saved[4], dup))):
+                part = mm_tn(all_rows, d_pre).astype(BF16)
+                first[k] = part[:half]
+                second[k] = part[half:]
+            part = mm_tn(both(saved[2], hid), all_cots).astype(BF16)
+            first[2] = part[:, :half]
+            second[2] = part[:, half:]
+            for k in complete:
+                stores[k].start()
+    for store in stores:
+        store.wait()
+
+
+def vmem():
+    return pl.BlockSpec(memory_space=pltpu.VMEM)
+
+
+def smem():
+    return pl.BlockSpec(memory_space=pltpu.SMEM)
+
+
+def run_pack(tokens, cotangent, codes):
+    count, width = tokens.shape
+    return pl.pallas_call(
+        pack_kernel,
+        in_specs=[vmem()] * 3,
+        out_specs=vmem(),
+        out_shape=jax.ShapeDtypeStruct((2 * count + CODE_ROWS, width), BF16),
+        name="pack",
+    )(tokens, cotangent, codes.T)
+
+
+def run_arm(scalars, parts, capacity, weights, piece, saved=()):
+    blocks = len(parts)
+    width, hidden_width = weights[0].shape
+    count = (parts[0].shape[0] - CODE_ROWS) // 2
+    rows = blocks * capacity
+    pieces = hidden_width // piece
+    one = (3, width // 2, piece)
+    made = [(rows, width)] * 2 + [(pieces, rows, piece)] * 3
+    outs = [(blocks // 2, 2, count, width)] * 2
+    outs += [(2,) + one] * 2 + [one] * 4 if saved else made
+    held = [(blocks,) + parts[0].shape] + [weight.shape for weight in weights]
+    held += [array.shape for array in saved] + made if saved else []
+    sources = (*parts, *weights, *saved)
+    anywhere = pl.BlockSpec(memory_space=pl.ANY)
+    return pl.pallas_call(
+        functools.partial(arm_kernel, blocks, len(sources), len(outs)),
+        in_specs=[smem()] + [anywhere] * len(sources),
+        out_specs=[anywhere] * len(outs),
+        out_shape=[jax.ShapeDtypeStruct(shape, BF16) for shape in outs],
+        scratch_shapes=[pltpu.VMEM(shape, BF16) for shape in held + outs]
+        + [
+            pltpu.SemaphoreType.DMA((len(sources),)),
+            pltpu.SemaphoreType.DMA((len(outs),)),
+            pltpu.VMEM((blocks, capacity, 2 * count), BF16),
+        ],
+        compiler_params=pltpu.CompilerParams(vmem_limit_bytes=VMEM_BYTES),
+        cost_estimate=pl.CostEstimate(
+            flops=(24 if saved else 12) * rows * width * hidden_width,
+            bytes_accessed=12 << 20,
+            transcendentals=0,
+        ),
+        name="arm_late" if saved else "arm_early",
+    )(scalars, *sources)
+
+
+def on_line(tokens, codes, cotangent, w_gate, w_up, w_down):
+    token_count, width = tokens.shape
+    arm_count = lax.axis_size("expert")
+    capacity = 4 * token_count // arm_count
+    w_gate, w_up, w_down = w_gate[0], w_up[0], w_down[0]
+    hidden_width = w_gate.shape[1]
+    chunk = hidden_width // lax.axis_size("dp")
+    expert = lax.axis_index("expert")
+    arm = jnp.reshape(expert, (1,)).astype(jnp.int32)
+    place = jnp.reshape(lax.axis_index("dp"), (1,)).astype(jnp.int32)
+    z = expert // 2
+    edge = (z == 0) | (z == 3)
+
+    def along(pairs):
+        return [(2 * s + c, 2 * d + c) for s, d in pairs for c in (0, 1)]
+
+    far = along([(0, 3), (3, 0), (1, 2), (2, 1)])
+    near = along([(0, 1), (1, 0), (2, 3), (3, 2)])
+    skip = along([(0, 2), (2, 3), (3, 1), (1, 0)])
+    skip_back = along([(2, 0), (3, 2), (1, 3), (0, 1)])
+    core = [(e, e ^ 1) for e in range(8)]
+    x_pair = [(i, i ^ 1) for i in range(4)]
+    y_pair = [(i, i ^ 2) for i in range(4)]
+    send = lambda value, pairs: lax.ppermute(value, "expert", pairs)
+    send_dp = lambda value, pairs: lax.ppermute(value, "dp", pairs)
+
+    own = run_pack(tokens, cotangent, codes)
+    add = lambda a, b: a.astype(F32) + b.astype(F32)
+    run = functools.partial(
+        run_arm,
+        jnp.concatenate([arm, place]),
+        capacity=capacity,
+        weights=(w_gate, w_up, w_down),
+        piece=chunk,
+    )
+    from_far = send(own, far)
+    from_near = send(own, near)
+    keep, give, *saved = run([own, from_near, send(own, core), send(from_near, core)])
+    from_skip = send(jnp.where(edge, own, from_far), skip)
+    from_skip, keep = lax.optimization_barrier((from_skip, keep))
+    got = send(give, core)
+    for_own = add(keep[0], got[0])
+    for_near = add(keep[1], got[1]).astype(BF16)
+    keep, give, x_part, y_part, x_next, y_next, k0, k1 = run(
+        [from_far, from_skip, send(from_far, core), send(from_skip, core)], saved=saved
+    )
+    got = send(give, core)
+    for_far = add(keep[0], got[0])
+    for_skip = add(keep[1], got[1]).astype(BF16)
+    from_x = send_dp(x_part, x_pair)
+    from_y = send_dp(y_part, y_pair)
+    from_skip = send(for_skip, skip_back).astype(F32)
+    from_near = send(for_near, near)
+    for_far = for_far + jnp.where(edge, 0.0, from_skip)
+    from_far = send(for_far.astype(BF16), far)
+    result = for_own + from_near + from_far + jnp.where(edge, from_skip, 0.0)
+    head_output, grad_tokens = result[0].astype(BF16), result[1].astype(BF16)
+    y_next = add(y_next, from_x[0]).astype(BF16)
+    x_next = add(x_next, from_y[0]).astype(BF16)
+    k0 = (add(k0, from_x[1]) + send_dp(y_next, y_pair)).astype(BF16)
+    k1 = (add(k1, from_y[1]) + send_dp(x_next, x_pair)).astype(BF16)
+    grad_gate = jnp.concatenate([k0[0], k1[0]], axis=0)[None]
+    grad_up = jnp.concatenate([k0[1], k1[1]], axis=0)[None]
+    grad_down = jnp.concatenate([k0[2], k1[2]], axis=1)[None]
+    return (head_output, grad_tokens, grad_gate, grad_up, grad_down)
+
+
 def solution(mesh):
+    on_square_of_lines = mesh.shape["dp"] == 4 and mesh.shape["expert"] == 8
     return jax.shard_map(
-        on_device,
+        on_line if on_square_of_lines else on_device,
         mesh=mesh,
         in_specs=(
             P(("dp", "expert"), None),

time: 139 us -> 75.8 us (0.55)
  matrix products: 27 us -> 0 us
  blocking collectives: 21.6 us -> 0 us
  local copies, waits for them, and re-layouts: 19.4 us -> 2.36 us
  Pallas kernels: 0 us -> 16.4 us
  between operations: 14.6 us -> 0.81 us
  other arithmetic: 15 us -> 5.1 us
  starting transfers between devices: 11.2 us -> 17.9 us
  waiting for transfers between devices: 29.3 us -> 33 us
    ppermute x0 -> x16, waiting for transfers between devices: none -> 33 us  [the longest x12 21.2 us: on_line(): send = lambda value, pairs: lax.ppermute(value, 'expert', pairs)]
    all_to_all x3 -> x0, waiting for transfers between devices: 29.2 us -> none  [the longest x1 12 us: on_device(): lax.all_to_all(out_rows, 'expert', split_axis=1, concat_axis=0, tiled=True)]
    dot_general x30 -> x0, matrix products: 27 us -> none  [the longest x5 5.34 us: arm_forward(): jnp.einsum('arc,ach->arh', rows_in, up_w, preferred_element_type=jnp.floa...]
    all_to_all x1 -> x0, blocking collectives: 21.6 us -> none  [on_device(): lax.all_to_all(send_tokens, 'expert', split_axis=0, concat_axis=1, tiled=...]
    ppermute x0 -> x16, starting transfers between devices: none -> 17.9 us  [the longest x12 11.8 us: on_line(): send = lambda value, pairs: lax.ppermute(value, 'expert', pairs)]
    pallas_call x0 -> x3, Pallas kernels: none -> 16.4 us  [the longest x2 14.7 us: run_arm(): pl.pallas_call(functools.partial(arm_kernel, blocks, len(sources), len(ou...]
    all_to_all x3 -> x0, starting transfers between devices: 11 us -> none  [the longest x1 3.78 us: on_device(): lax.all_to_all(out_rows, 'expert', split_axis=1, concat_axis=0, tiled=True)]
    unnamed x2 -> x0, other arithmetic: 8.43 us -> none
  transfers between devices with their start and end apart: 5 -> 16, of which waited for: 3 -> 8; matrix products, arithmetic and copies ran while one was open for 30% -> 5% of each run, Pallas kernels for 0% -> 8%
where the time goes in v2:
time: 75.8 us; the launch traced here: 75.6 us
  waiting for transfers between devices  33 us (44%)
  starting transfers between devices  17.9 us (24%)
  Pallas kernels  16.4 us (22%)
  other arithmetic  5.1 us (7%)
  local copies, waits for them, and re-layouts  2.36 us (3%)
  between operations  0.81 us (1%)
    ppermute x12, waiting for transfers between devices, on_line(): send = lambda value, pairs: lax.ppermute(value, 'expert', pairs)  21.2 us
    pallas_call x2, Pallas kernels, run_arm(): pl.pallas_call(functools.partial(arm_kernel, blocks, len(sources), len(ou...  14.7 us
    ppermute x4, waiting for transfers between devices, on_line(): send_dp = lambda value, pairs: lax.ppermute(value, 'dp', pairs)  11.8 us
    ppermute x12, starting transfers between devices, on_line(): send = lambda value, pairs: lax.ppermute(value, 'expert', pairs)  11.8 us
    ppermute x4, starting transfers between devices, on_line(): send_dp = lambda value, pairs: lax.ppermute(value, 'dp', pairs)  6.15 us
    pallas_call x1, Pallas kernels, run_pack(): pl.pallas_call(pack_kernel, in_specs=[vmem()] * 3, out_specs=vmem(), out_...  1.69 us
    unnamed x28, local copies, waits for them, and re-layouts  1.58 us
  transfers between devices with their start and end apart: 16, of which 8 were waited for; matrix products, arithmetic and copies ran while one was open for 5% of the time, Pallas kernels for 8%

profile of v2, /device:TPU:0, one launch (start us, length us, event | category | flops | bytes accessed | tf_op | source)
XLA Modules:
  0.0 75.6 jit_solution(16940002840206069669)
XLA Ops:
  0.6 1.7 %pack.1.refs_0_ = bf16[272,512]{1,0:T(8,128)(2,1)} custom-call(bf16[128,512]{1,0:T(8,128)(2,1)} %tokens_ref.1, bf16[128,512]{1,0:T(8,128)(2,1)} %cot_ref.1, s32[2,128]{1,0:T(2,128)} %bitcast.60), custom_call_target="tpu_custom_call" | custom-call | tf_op jit(solution)/shard_map/pack/pallas_call | solution.py:275
  2.3 3.0 %collective-permute-start.2 = (bf16[272,512]{1,0:T(8,128)(2,1)}, bf16[272,512]{1,0:T(8,128)(2,1)S(1)}, u32[]{:S(2)}, u32[]{:S(2)}) collective-permute-start(bf16[272,512]{1,0:T(8,128)(2,1)} %pack.1.refs_0_), channel_id=1, source_target_pairs={{0,2},{1,3},{2,0},{3,1},{4,6},{5,7},{6,4},{7,5},{8,10},{9,11},{10,... | collective-permute-start | bytes 835592 | tf_op jit(solution)/shard_map/ppermute | solution.py:342
  5.3 2.5 %collective-permute-start = (bf16[272,512]{1,0:T(8,128)(2,1)}, bf16[272,512]{1,0:T(8,128)(2,1)S(1)}, u32[]{:S(2)}, u32[]{:S(2)}) collective-permute-start(bf16[272,512]{1,0:T(8,128)(2,1)} %pack.1.refs_0_), channel_id=1, source_target_pairs={{0,6},{1,7},{6,0},{7,1},{2,4},{3,5},{4,2},{5,3},{8,14},{9,15},{14,... | collective-permute-start | bytes 835592 | tf_op jit(solution)/shard_map/ppermute | solution.py:342
  7.8 0.0 collective-permute-start.3
  7.8 4.9 %collective-permute-done.2.refs_1_ = bf16[272,512]{1,0:T(8,128)(2,1)S(1)} collective-permute-done((bf16[272,512]{1,0:T(8,128)(2,1)}, bf16[272,512]{1,0:T(8,128)(2,1)S(1)}, u32[]{:S(2)}, u32[]{:S(2)}) %collective-permute-start.2) | collective-permute-done | bytes 278560 | tf_op jit(solution)/shard_map/ppermute | solution.py:342
  12.7 0.0 collective-permute-start.4
  12.7 7.7 %collective-permute-done.refs_0_ = bf16[272,512]{1,0:T(8,128)(2,1)S(1)} collective-permute-done((bf16[272,512]{1,0:T(8,128)(2,1)}, bf16[272,512]{1,0:T(8,128)(2,1)S(1)}, u32[]{:S(2)}, u32[]{:S(2)}) %collective-permute-start) | collective-permute-done | bytes 278560 | tf_op jit(solution)/shard_map/ppermute | solution.py:342
  20.5 1.1 %broadcast_select_fusion = bf16[272,512]{1,0:T(8,128)(2,1)S(1)} fusion(bf16[272,512]{1,0:T(8,128)(2,1)} %pack.1.refs_0_, bf16[272,512]{1,0:T(8,128)(2,1)S(1)} %collective-permute-done.refs_0_, pred[]{:T(512)S(6)} %or.3), kind=kLoop, calls=%fused_computation.24 | loop fusion | flops 139264 | bytes 835585 | tf_op jit(solution)/shard_map/jit(_where)/select_n | solution.py:357
  21.6 0.8 collective-permute-start.1
  22.3 0.6 pad_add_fusion.scalar_ref
  22.9 0.0 collective-permute-start.7
  22.9 0.0 collective-permute-done.3.refs_2_
  22.9 0.0 collective-permute-done.4.refs_3_
  23.0 0.7 copy-done.9
  23.6 0.1 copy-done.12
  23.8 6.3 %arm_early.1 = (bf16[2,2,128,512]{3,2,1,0:T(8,128)(2,1)}, bf16[2,2,128,512]{3,2,1,0:T(8,128)(2,1)}, bf16[256,512]{1,0:T(8,128)(2,1)}, bf16[256,512]{1,0:T(8,128)...) custom-call(s32[2]{0:T(128)} %pad_add_fusion.scalar_ref, ...), custom_call_target="tpu_custom_call" | custom-call | flops 1610612736 | bytes 12582912 | tf_op jit(solution)/shard_map/arm_early/pallas_call | solution.py:298
  30.1 0.0 collective-permute-done.1.refs_1_
  30.1 0.6 collective-permute-start.8
  30.7 0.0 collective-permute-done.7.refs_2_
  30.7 1.2 %collective-permute-done.8.refs_3_ = bf16[272,512]{1,0:T(8,128)(2,1)S(1)} collective-permute-done((bf16[272,512]{1,0:T(8,128)(2,1)S(1)}, bf16[272,512]{1,0:T(8,128)(2,1)S(1)}, u32[]{:S(2)}, u32[]{:S(2)}) %collective-permute-start.8) | collective-permute-done | bytes 278560 | tf_op jit(solution)/shard_map/ppermute | solution.py:342
  31.9 0.7 copy-done.13
  32.6 8.4 %arm_late.1 = (bf16[2,2,128,512]{3,2,1,0:T(8,128)(2,1)}, bf16[2,2,128,512]{3,2,1,0:T(8,128)(2,1)}, bf16[2,3,256,256]{3,2,1,0:T(8,128)(2,1)}, bf16[2,3,256,256]{3...) custom-call(s32[2]{0:T(128)} %pad_add_fusion.scalar_ref, ...), custom_call_target="tpu_custom_call" | custom-call | flops 3221225472 | bytes 12582912 | tf_op jit(solution)/shard_map/arm_late/pallas_call | solution.py:298
  41.1 0.4 collective-permute-start.9
  41.5 0.1 collective-permute-start.5
  41.6 1.5 %collective-permute-start.12 = (bf16[2,3,256,256]{3,2,1,0:T(8,128)(2,1)}, bf16[2,3,256,256]{3,2,1,0:T(8,128)(2,1)S(1)}, u32[]{:S(2)}, u32[]{:S(2)}) collective-permute-start(bf16[2,3,256,256]{3,2,1,0:T(8,128)(2,1)} %get-tuple-element.34), channel_id=1, source_target_pairs={{0,8},{8,0},{16,24},{24,16},{1,9},{9,1},{17,25},{25,17},{2,10},{10... | collective-permute-start | bytes 2359304 | tf_op jit(solution)/shard_map/ppermute | solution.py:343
  43.1 1.5 %collective-permute-start.14 = (bf16[2,3,256,256]{3,2,1,0:T(8,128)(2,1)}, bf16[2,3,256,256]{3,2,1,0:T(8,128)(2,1)S(1)}, u32[]{:S(2)}, u32[]{:S(2)}) collective-permute-start(bf16[2,3,256,256]{3,2,1,0:T(8,128)(2,1)} %get-tuple-element.37), channel_id=1, source_target_pairs={{0,16},{8,24},{16,0},{24,8},{1,17},{9,25},{17,1},{25,9},{2,18},{10... | collective-permute-start | bytes 2359304 | tf_op jit(solution)/shard_map/ppermute | solution.py:343
  44.7 0.0 collective-permute-done.9
  44.7 1.0 %fusion.12 = bf16[2,128,512]{2,1,0:T(8,128)(2,1)S(1)} fusion(bf16[2,2,128,512]{3,2,1,0:T(8,128)(2,1)S(1)} %collective-permute-done.9, bf16[2,2,128,512]{3,2,1,0:T(8,128)(2,1)} %get-tuple-element.31), kind=kLoop, calls=%fused_computation.26 | loop fusion | flops 524288 | bytes 786432 | tf_op jit(solution)/shard_map/convert_element_type | solution.py:367
  45.7 1.4 %collective-permute-start.10 = (bf16[2,128,512]{2,1,0:T(8,128)(2,1)S(1)}, bf16[2,128,512]{2,1,0:T(8,128)(2,1)S(1)}, u32[]{:S(2)}, u32[]{:S(2)}) collective-permute-start(bf16[2,128,512]{2,1,0:T(8,128)(2,1)S(1)} %fusion.12), channel_id=1, source_target_pairs={{4,0},{5,1},{6,4},{7,5},{2,6},{3,7},{0,2},{1,3},{12,8},{13,9},{14,... | collective-permute-start | bytes 786440 | tf_op jit(solution)/shard_map/ppermute | solution.py:342
  47.1 0.1 fusion.11
  47.2 1.2 %collective-permute-start.6 = (bf16[2,128,512]{2,1,0:T(8,128)(2,1)S(1)}, bf16[2,128,512]{2,1,0:T(8,128)(2,1)S(1)}, u32[]{:S(2)}, u32[]{:S(2)}) collective-permute-start(bf16[2,128,512]{2,1,0:T(8,128)(2,1)S(1)} %fusion.11), channel_id=1, source_target_pairs={{0,2},{1,3},{2,0},{3,1},{4,6},{5,7},{6,4},{7,5},{8,10},{9,11},{10,... | collective-permute-start | bytes 786440 | tf_op jit(solution)/shard_map/ppermute | solution.py:342
  48.4 6.4 %collective-permute-done.10 = bf16[2,128,512]{2,1,0:T(8,128)(2,1)S(1)} collective-permute-done((bf16[2,128,512]{2,1,0:T(8,128)(2,1)S(1)}, bf16[2,128,512]{2,1,0:T(8,128)(2,1)S(1)}, u32[]{:S(2)}, u32[]{:S(2)}) %collective-permute-start.10) | collective-permute-done | bytes 262176 | tf_op jit(solution)/shard_map/ppermute | solution.py:342
  54.8 0.1 fusion.7
  54.9 1.8 %collective-permute-start.11 = (bf16[2,128,512]{2,1,0:T(8,128)(2,1)S(1)}, bf16[2,128,512]{2,1,0:T(8,128)(2,1)S(1)}, u32[]{:S(2)}, u32[]{:S(2)}) collective-permute-start(bf16[2,128,512]{2,1,0:T(8,128)(2,1)S(1)} %fusion.7), channel_id=1, source_target_pairs={{0,6},{1,7},{6,0},{7,1},{2,4},{3,5},{4,2},{5,3},{8,14},{9,15},{14,... | collective-permute-start | bytes 786440 | tf_op jit(solution)/shard_map/ppermute | solution.py:342
  56.6 5.0 %collective-permute-done.12 = bf16[2,3,256,256]{3,2,1,0:T(8,128)(2,1)S(1)} collective-permute-done((bf16[2,3,256,256]{3,2,1,0:T(8,128)(2,1)}, bf16[2,3,256,256]{3,2,1,0:T(8,128)(2,1)S(1)}, u32[]{:S(2)}, u32[]{:S(2)}) %collective-permute-start.12) | collective-permute-done | bytes 786464 | tf_op jit(solution)/shard_map/ppermute | solution.py:343
  61.7 0.1 fusion.3
  61.8 1.6 %collective-permute-start.13 = (bf16[3,256,256]{2,1,0:T(8,128)(2,1)S(1)}, bf16[3,256,256]{2,1,0:T(8,128)(2,1)S(1)}, u32[]{:S(2)}, u32[]{:S(2)}) collective-permute-start(bf16[3,256,256]{2,1,0:T(8,128)(2,1)S(1)} %fusion.3), channel_id=1, source_target_pairs={{0,16},{8,24},{16,0},{24,8},{1,17},{9,25},{17,1},{25,9},{2,18},{10... | collective-permute-start | bytes 1179656 | tf_op jit(solution)/shard_map/ppermute | solution.py:343
  63.4 0.1 fusion
  63.5 1.5 %collective-permute-start.15 = (bf16[3,256,256]{2,1,0:T(8,128)(2,1)S(1)}, bf16[3,256,256]{2,1,0:T(8,128)(2,1)S(1)}, u32[]{:S(2)}, u32[]{:S(2)}) collective-permute-start(bf16[3,256,256]{2,1,0:T(8,128)(2,1)S(1)} %fusion), channel_id=1, source_target_pairs={{0,8},{8,0},{16,24},{24,16},{1,9},{9,1},{17,25},{25,17},{2,10},{10... | collective-permute-start | bytes 1179656 | tf_op jit(solution)/shard_map/ppermute | solution.py:343
  65.0 1.0 %collective-permute-done.11 = bf16[2,128,512]{2,1,0:T(8,128)(2,1)S(1)} collective-permute-done((bf16[2,128,512]{2,1,0:T(8,128)(2,1)S(1)}, bf16[2,128,512]{2,1,0:T(8,128)(2,1)S(1)}, u32[]{:S(2)}, u32[]{:S(2)}) %collective-permute-start.11) | collective-permute-done | bytes 262176 | tf_op jit(solution)/shard_map/ppermute | solution.py:342
  66.0 0.2 fusion.9
  66.2 0.7 slice_bitcast_fusion.10
  66.9 5.5 %collective-permute-done.13 = bf16[3,256,256]{2,1,0:T(8,128)(2,1)S(1)} collective-permute-done((bf16[3,256,256]{2,1,0:T(8,128)(2,1)S(1)}, bf16[3,256,256]{2,1,0:T(8,128)(2,1)S(1)}, u32[]{:S(2)}, u32[]{:S(2)}) %collective-permute-start.13) | collective-permute-done | bytes 393248 | tf_op jit(solution)/shard_map/ppermute | solution.py:343
  72.4 0.1 fusion.5
  72.6 1.2 %collective-permute-done.15 = bf16[3,256,256]{2,1,0:T(8,128)(2,1)S(1)} collective-permute-done((bf16[3,256,256]{2,1,0:T(8,128)(2,1)S(1)}, bf16[3,256,256]{2,1,0:T(8,128)(2,1)S(1)}, u32[]{:S(2)}, u32[]{:S(2)}) %collective-permute-start.15) | collective-permute-done | bytes 393248 | tf_op jit(solution)/shard_map/ppermute | solution.py:343
  73.9 0.1 fusion.2
  74.0 0.7 maximum_bitcast_fusion.2
  74.8 0.8 %maximum_bitcast_fusion = (bf16[1,512,256]{2,1,0:T(8,128)(2,1)}, bf16[1,512,256]{2,1,0:T(8,128)(2,1)}) fusion(bf16[256,256]{1,0:T(8,128)(2,1)S(1)} %get-tuple-element.44, bf16[256,256]{1,0:T(8,128)(2,1)S(1)} %get-tuple-element.41, bf16[256,256]{1,0:T(8,128)(2,1)S(1)} %get-tuple-element.43, bf16[256,256]{1,0:T(8,128)(2,1)S(1)} %get-tuple-element.40), kind=kLoop, calls=%fused_computation.27 | loop fusion | flops 1048576 | bytes 1048576 | tf_op jit(solution)/shard_map/broadcast_in_dim | solution.py:380
  (30 shorter events, 0.1 us)
Async XLA Ops:
  2.3 10.4 %collective-permute-start.2 = (bf16[272,512]{1,0:T(8,128)(2,1)}, bf16[272,512]{1,0:T(8,128)(2,1)S(1)}, u32[]{:S(2)}, u32[]{:S(2)}) collective-permute-start(bf16[272,512]{1,0:T(8,128)(2,1)} %pack.1.refs_0_), channel_id=1, source_target_pairs={{0,2},{1,3},{2,0},{3,1},{4,6},{5,7},{6,4},{7,5},{8,10},{9,11},{10,... | collective-permute-start | bytes 835592 | tf_op jit(solution)/shard_map/ppermute | solution.py:342
  5.3 15.1 %collective-permute-start = (bf16[272,512]{1,0:T(8,128)(2,1)}, bf16[272,512]{1,0:T(8,128)(2,1)S(1)}, u32[]{:S(2)}, u32[]{:S(2)}) collective-permute-start(bf16[272,512]{1,0:T(8,128)(2,1)} %pack.1.refs_0_), channel_id=1, source_target_pairs={{0,6},{1,7},{6,0},{7,1},{2,4},{3,5},{4,2},{5,3},{8,14},{9,15},{14,... | collective-permute-start | bytes 835592 | tf_op jit(solution)/shard_map/ppermute | solution.py:342
  7.8 15.1 %collective-permute-start.3 = (bf16[272,512]{1,0:T(8,128)(2,1)}, bf16[272,512]{1,0:T(8,128)(2,1)S(1)}, u32[]{:S(2)}, u32[]{:S(2)}) collective-permute-start(bf16[272,512]{1,0:T(8,128)(2,1)} %pack.1.refs_0_), channel_id=1, source_target_pairs={{0,1},{1,0},{2,3},{3,2},{4,5},{5,4},{6,7},{7,6},{8,9},{9,8},{10,11... | collective-permute-start | bytes 835592 | tf_op jit(solution)/shard_map/ppermute | solution.py:342
  12.7 8.8 %copy-start.8 = (bf16[272,512]{1,0:T(8,128)(2,1)}, bf16[272,512]{1,0:T(8,128)(2,1)S(1)}, u32[]{:S(2)}) copy-start(bf16[272,512]{1,0:T(8,128)(2,1)S(1)} %collective-permute-done.2.refs_1_) | copy-start | bytes 835588
  12.7 10.2 %collective-permute-start.4 = (bf16[272,512]{1,0:T(8,128)(2,1)S(1)}, bf16[272,512]{1,0:T(8,128)(2,1)S(1)}, u32[]{:S(2)}, u32[]{:S(2)}) collective-permute-start(bf16[272,512]{1,0:T(8,128)(2,1)S(1)} %collective-permute-done.2.refs_1_), channel_id=1, source_target_pairs={{0,1},{1,0},{2,3},{3,2},{4,5},{5,4},{6,7},{7,6},{8,9},{9,8},{10,11... | collective-permute-start | bytes 835592 | tf_op jit(solution)/shard_map/ppermute | solution.py:342
  20.5 2.4 %copy-start.6 = (bf16[272,512]{1,0:T(8,128)(2,1)}, bf16[272,512]{1,0:T(8,128)(2,1)S(1)}, u32[]{:S(2)}) copy-start(bf16[272,512]{1,0:T(8,128)(2,1)S(1)} %collective-permute-done.refs_0_) | copy-start | bytes 835588
  21.6 8.5 %collective-permute-start.1 = (bf16[272,512]{1,0:T(8,128)(2,1)S(1)}, bf16[272,512]{1,0:T(8,128)(2,1)S(1)}, u32[]{:S(2)}, u32[]{:S(2)}) collective-permute-start(bf16[272,512]{1,0:T(8,128)(2,1)S(1)} %broadcast_select_fusion), channel_id=1, source_target_pairs={{0,4},{1,5},{4,6},{5,7},{6,2},{7,3},{2,0},{3,1},{8,12},{9,13},{12,... | collective-permute-start | bytes 835592 | tf_op jit(solution)/shard_map/ppermute | solution.py:342
  22.9 7.7 %collective-permute-start.7 = (bf16[272,512]{1,0:T(8,128)(2,1)S(1)}, bf16[272,512]{1,0:T(8,128)(2,1)S(1)}, u32[]{:S(2)}, u32[]{:S(2)}) collective-permute-start(bf16[272,512]{1,0:T(8,128)(2,1)S(1)} %collective-permute-done.refs_0_), channel_id=1, source_target_pairs={{0,1},{1,0},{2,3},{3,2},{4,5},{5,4},{6,7},{7,6},{8,9},{9,8},{10,11... | collective-permute-start | bytes 835592 | tf_op jit(solution)/shard_map/ppermute | solution.py:342
  22.9 0.7 copy-start.9
  23.0 0.8 %copy-start.12 = (bf16[272,512]{1,0:T(8,128)(2,1)}, bf16[272,512]{1,0:T(8,128)(2,1)S(1)}, u32[]{:S(2)}) copy-start(bf16[272,512]{1,0:T(8,128)(2,1)S(1)} %collective-permute-done.4.refs_3_) | copy-start | bytes 835588
  30.1 1.8 %copy-start.10 = (bf16[272,512]{1,0:T(8,128)(2,1)}, bf16[272,512]{1,0:T(8,128)(2,1)S(1)}, u32[]{:S(2)}) copy-start(bf16[272,512]{1,0:T(8,128)(2,1)S(1)} %collective-permute-done.1.refs_1_) | copy-start | bytes 835588
  30.1 1.8 %collective-permute-start.8 = (bf16[272,512]{1,0:T(8,128)(2,1)S(1)}, bf16[272,512]{1,0:T(8,128)(2,1)S(1)}, u32[]{:S(2)}, u32[]{:S(2)}) collective-permute-start(bf16[272,512]{1,0:T(8,128)(2,1)S(1)} %collective-permute-done.1.refs_1_), channel_id=1, source_target_pairs={{0,1},{1,0},{2,3},{3,2},{4,5},{5,4},{6,7},{7,6},{8,9},{9,8},{10,11... | collective-permute-start | bytes 835592 | tf_op jit(solution)/shard_map/ppermute | solution.py:342
  30.7 1.2 %copy-start.11 = (bf16[272,512]{1,0:T(8,128)(2,1)}, bf16[272,512]{1,0:T(8,128)(2,1)S(1)}, u32[]{:S(2)}) copy-start(bf16[272,512]{1,0:T(8,128)(2,1)S(1)} %collective-permute-done.7.refs_2_) | copy-start | bytes 835588
  31.9 0.8 copy-start.13
  32.6 8.9 %copy-start.7 = (bf16[2,2,128,512]{3,2,1,0:T(8,128)(2,1)S(1)}, bf16[2,2,128,512]{3,2,1,0:T(8,128)(2,1)}, u32[]{:S(2)}) copy-start(bf16[2,2,128,512]{3,2,1,0:T(8,128)(2,1)} %get-tuple-element.24) | copy-start | bytes 1572868
  41.0 6.0 %copy-start = (bf16[2,2,128,512]{3,2,1,0:T(8,128)(2,1)S(1)}, bf16[2,2,128,512]{3,2,1,0:T(8,128)(2,1)}, u32[]{:S(2)}) copy-start(bf16[2,2,128,512]{3,2,1,0:T(8,128)(2,1)} %get-tuple-element.23) | copy-start | bytes 1572868
  41.1 3.6 %collective-permute-start.9 = (bf16[2,2,128,512]{3,2,1,0:T(8,128)(2,1)}, bf16[2,2,128,512]{3,2,1,0:T(8,128)(2,1)S(1)}, u32[]{:S(2)}, u32[]{:S(2)}) collective-permute-start(bf16[2,2,128,512]{3,2,1,0:T(8,128)(2,1)} %get-tuple-element.32), channel_id=1, source_target_pairs={{0,1},{1,0},{2,3},{3,2},{4,5},{5,4},{6,7},{7,6},{8,9},{9,8},{10,11... | collective-permute-start | bytes 1572872 | tf_op jit(solution)/shard_map/ppermute | solution.py:342
  41.5 5.6 %collective-permute-start.5 = (bf16[2,2,128,512]{3,2,1,0:T(8,128)(2,1)S(1)}, bf16[2,2,128,512]{3,2,1,0:T(8,128)(2,1)S(1)}, u32[]{:S(2)}, u32[]{:S(2)}) collective-permute-start(bf16[2,2,128,512]{3,2,1,0:T(8,128)(2,1)S(1)} %copy-done.7), channel_id=1, source_target_pairs={{0,1},{1,0},{2,3},{3,2},{4,5},{5,4},{6,7},{7,6},{8,9},{9,8},{10,11... | collective-permute-start | bytes 1572872 | tf_op jit(solution)/shard_map/ppermute | solution.py:342
  41.6 20.0 %collective-permute-start.12 = (bf16[2,3,256,256]{3,2,1,0:T(8,128)(2,1)}, bf16[2,3,256,256]{3,2,1,0:T(8,128)(2,1)S(1)}, u32[]{:S(2)}, u32[]{:S(2)}) collective-permute-start(bf16[2,3,256,256]{3,2,1,0:T(8,128)(2,1)} %get-tuple-element.34), channel_id=1, source_target_pairs={{0,8},{8,0},{16,24},{24,16},{1,9},{9,1},{17,25},{25,17},{2,10},{10... | collective-permute-start | bytes 2359304 | tf_op jit(solution)/shard_map/ppermute | solution.py:343
  43.1 20.2 %collective-permute-start.14 = (bf16[2,3,256,256]{3,2,1,0:T(8,128)(2,1)}, bf16[2,3,256,256]{3,2,1,0:T(8,128)(2,1)S(1)}, u32[]{:S(2)}, u32[]{:S(2)}) collective-permute-start(bf16[2,3,256,256]{3,2,1,0:T(8,128)(2,1)} %get-tuple-element.37), channel_id=1, source_target_pairs={{0,16},{8,24},{16,0},{24,8},{1,17},{9,25},{17,1},{25,9},{2,18},{10... | collective-permute-start | bytes 2359304 | tf_op jit(solution)/shard_map/ppermute | solution.py:343
  45.7 9.1 %copy-start.1 = (bf16[2,2,128,512]{3,2,1,0:T(8,128)(2,1)S(1)}, bf16[2,2,128,512]{3,2,1,0:T(8,128)(2,1)}, u32[]{:S(2)}) copy-start(bf16[2,2,128,512]{3,2,1,0:T(8,128)(2,1)} %get-tuple-element.31) | copy-start | bytes 1572868
  45.7 9.1 %collective-permute-start.10 = (bf16[2,128,512]{2,1,0:T(8,128)(2,1)S(1)}, bf16[2,128,512]{2,1,0:T(8,128)(2,1)S(1)}, u32[]{:S(2)}, u32[]{:S(2)}) collective-permute-start(bf16[2,128,512]{2,1,0:T(8,128)(2,1)S(1)} %fusion.12), channel_id=1, source_target_pairs={{4,0},{5,1},{6,4},{7,5},{2,6},{3,7},{0,2},{1,3},{12,8},{13,9},{14,... | collective-permute-start | bytes 786440 | tf_op jit(solution)/shard_map/ppermute | solution.py:342
  47.2 14.5 %copy-start.5 = (bf16[3,256,256]{2,1,0:T(8,128)(2,1)S(1)}, bf16[3,256,256]{2,1,0:T(8,128)(2,1)}, u32[]{:S(2)}) copy-start(bf16[3,256,256]{2,1,0:T(8,128)(2,1)} %get-tuple-element.35) | copy-start | bytes 1179652
  47.2 17.9 %collective-permute-start.6 = (bf16[2,128,512]{2,1,0:T(8,128)(2,1)S(1)}, bf16[2,128,512]{2,1,0:T(8,128)(2,1)S(1)}, u32[]{:S(2)}, u32[]{:S(2)}) collective-permute-start(bf16[2,128,512]{2,1,0:T(8,128)(2,1)S(1)} %fusion.11), channel_id=1, source_target_pairs={{0,2},{1,3},{2,0},{3,1},{4,6},{5,7},{6,4},{7,5},{8,10},{9,11},{10,... | collective-permute-start | bytes 786440 | tf_op jit(solution)/shard_map/ppermute | solution.py:342
  54.9 11.1 %collective-permute-start.11 = (bf16[2,128,512]{2,1,0:T(8,128)(2,1)S(1)}, bf16[2,128,512]{2,1,0:T(8,128)(2,1)S(1)}, u32[]{:S(2)}, u32[]{:S(2)}) collective-permute-start(bf16[2,128,512]{2,1,0:T(8,128)(2,1)S(1)} %fusion.7), channel_id=1, source_target_pairs={{0,6},{1,7},{6,0},{7,1},{2,4},{3,5},{4,2},{5,3},{8,14},{9,15},{14,... | collective-permute-start | bytes 786440 | tf_op jit(solution)/shard_map/ppermute | solution.py:342
  61.7 1.7 %copy-start.4 = (bf16[3,256,256]{2,1,0:T(8,128)(2,1)S(1)}, bf16[3,256,256]{2,1,0:T(8,128)(2,1)}, u32[]{:S(2)}) copy-start(bf16[3,256,256]{2,1,0:T(8,128)(2,1)} %get-tuple-element.38) | copy-start | bytes 1179652
  61.8 10.6 %collective-permute-start.13 = (bf16[3,256,256]{2,1,0:T(8,128)(2,1)S(1)}, bf16[3,256,256]{2,1,0:T(8,128)(2,1)S(1)}, u32[]{:S(2)}, u32[]{:S(2)}) collective-permute-start(bf16[3,256,256]{2,1,0:T(8,128)(2,1)S(1)} %fusion.3), channel_id=1, source_target_pairs={{0,16},{8,24},{16,0},{24,8},{1,17},{9,25},{17,1},{25,9},{2,18},{10... | collective-permute-start | bytes 1179656 | tf_op jit(solution)/shard_map/ppermute | solution.py:343
  63.5 10.4 %collective-permute-start.15 = (bf16[3,256,256]{2,1,0:T(8,128)(2,1)S(1)}, bf16[3,256,256]{2,1,0:T(8,128)(2,1)S(1)}, u32[]{:S(2)}, u32[]{:S(2)}) collective-permute-start(bf16[3,256,256]{2,1,0:T(8,128)(2,1)S(1)} %fusion), channel_id=1, source_target_pairs={{0,8},{8,0},{16,24},{24,16},{1,9},{9,1},{17,25},{25,17},{2,10},{10... | collective-permute-start | bytes 1179656 | tf_op jit(solution)/shard_map/ppermute | solution.py:343
  66.2 6.3 %copy-start.3 = (bf16[3,256,256]{2,1,0:T(8,128)(2,1)S(1)}, bf16[3,256,256]{2,1,0:T(8,128)(2,1)}, u32[]{:S(2)}) copy-start(bf16[3,256,256]{2,1,0:T(8,128)(2,1)} %get-tuple-element.33) | copy-start | bytes 1179652
  72.6 1.3 %copy-start.2 = (bf16[3,256,256]{2,1,0:T(8,128)(2,1)S(1)}, bf16[3,256,256]{2,1,0:T(8,128)(2,1)}, u32[]{:S(2)}) copy-start(bf16[3,256,256]{2,1,0:T(8,128)(2,1)} %get-tuple-element.36) | copy-start | bytes 1179652

commit v3 on v2

--- a/solution.py
+++ b/solution.py
@@ -142,12 +142,14 @@
     after = lax.broadcasted_iota(jnp.int32, (count, count), 1)
     ranks = mm(jnp.concatenate(named, axis=0).astype(BF16), (before < after).astype(BF16))
     slot = lax.broadcasted_iota(jnp.int32, (capacity, count), 0).astype(F32)
-    pairs = []
+    chosen, shares = [], []
     for b, hit in enumerate(named):
         rank = ranks[b * CODE_ROWS : b * CODE_ROWS + 1] + ranks[b * CODE_ROWS + 1 : b * CODE_ROWS + 2]
-        here = slot == rank
-        pairs.append((jnp.where(here, hit[0:1], 0.0), jnp.where(here, hit[1:2], 0.0)))
-    return pairs
+        here = jnp.where(slot == rank, hit[0:1] + hit[1:2], 0.0)
+        share = fact_share * hit[0:1] + counter_share * hit[1:2]
+        chosen.append(here.astype(BF16))
+        shares.append(jnp.sum(here * share, axis=1, keepdims=True))
+    return chosen, shares
 
 
 def pack_kernel(tokens_ref, cot_ref, codes_ref, out_ref):
@@ -161,15 +163,15 @@
     out_ref[2 * count : 2 * count + CODE_ROWS, 0:count] = both.astype(BF16)
 
 
-def arm_kernel(blocks, ins, outs_count, scalar_ref, *refs):
+def arm_kernel(blocks, ins, outs_count, *refs):
     sources, refs = refs[:ins], refs[ins:]
     outs, refs = refs[:outs_count], refs[outs_count:]
-    in_sems, out_sems, sel = refs[-3:]
-    staged, refs = refs[-3 - outs_count : -3], refs[: -3 - outs_count]
+    in_sems, out_sems = refs[-2:]
+    staged, refs = refs[-2 - outs_count : -2], refs[: -2 - outs_count]
     held, (gate_ref, up_ref, down_ref), saved = refs[0], refs[1:4], refs[4:]
     keep_ref, give_ref = staged[:2]
     rows, cots, hid, dgate, dup = saved[5:] if saved else staged[2:]
-    capacity, count = sel.shape[1], sel.shape[2] // 2
+    capacity, count = rows.shape[0] // blocks, keep_ref.shape[2]
     pieces = hid.shape[0]
     targets = [held.at[b] for b in range(blocks)] + [gate_ref, up_ref, down_ref, *saved[:5]]
     loads = [
@@ -182,20 +184,16 @@
     ]
     for load in loads:
         load.start()
+    arm, place = lax.axis_index("expert"), lax.axis_index("dp")
     for load in loads[:blocks]:
         load.wait()
 
     tiles = [held[b, 2 * count : 2 * count + CODE_ROWS, 0:count] for b in range(blocks)]
-    pairs = selections(tiles, scalar_ref[0].astype(F32), capacity)
-    for b, (fact, counter) in enumerate(pairs):
+    chosen, shares = selections(tiles, arm.astype(F32), capacity)
+    for b in range(blocks):
         at = slice(b * capacity, (b + 1) * capacity)
-        sel[b] = jnp.concatenate([fact, counter], axis=1).astype(BF16)
-        rows[at] = mm((fact + counter).astype(BF16), held[b, 0:count]).astype(BF16)
-        cot = held[b, count : 2 * count].astype(F32)
-        scaled = jnp.concatenate(
-            [(fact_share * cot).astype(BF16), (counter_share * cot).astype(BF16)], axis=0
-        )
-        cots[at] = mm(sel[b], scaled).astype(BF16)
+        rows[at] = mm(chosen[b], held[b, 0:count]).astype(BF16)
+        cots[at] = (mm(chosen[b], held[b, count : 2 * count]) * shares[b]).astype(BF16)
 
     for load in loads[blocks : blocks + 3]:
         load.wait()
@@ -224,30 +222,29 @@
     for b in range(blocks):
         at = slice(b * capacity, (b + 1) * capacity)
         target = keep_ref if b < blocks // 2 else give_ref
-        placed = mm_tn(sel[b], total_out[at].astype(BF16))
-        target[b % (blocks // 2), 0] = (
-            fact_share * placed[:count] + counter_share * placed[count:]
-        ).astype(BF16)
-        placed = mm_tn(sel[b], total_in[at].astype(BF16))
-        target[b % (blocks // 2), 1] = (placed[:count] + placed[count:]).astype(BF16)
+        out_rows = (total_out[at].astype(BF16).astype(F32) * shares[b]).astype(BF16)
+        target[b % (blocks // 2), 0] = mm_tn(chosen[b], out_rows).astype(BF16)
+        in_rows = total_in[at].astype(BF16)
+        target[b % (blocks // 2), 1] = mm_tn(chosen[b], in_rows).astype(BF16)
     stores[0].start()
     stores[1].start()
 
     if saved:
         for load in loads[blocks + 3 :]:
             load.wait()
-        x_ref, y_ref, x_next_ref, y_next_ref, first_ref, second_ref = staged[2:]
+        parts = staged[2:]
         all_rows = jnp.concatenate([saved[0][...], rows[...]], axis=0)
         all_cots = jnp.concatenate([saved[1][...], cots[...]], axis=0)
         half = all_rows.shape[1] // 2
-        quarters = (
+        x_ref, y_ref, x_next_ref, y_next_ref, first_ref, second_ref = parts
+        plan = (
             (3, x_ref.at[0], y_ref.at[0], ()),
-            (1, x_ref.at[1], x_next_ref, (2, 4)),
-            (2, y_next_ref, y_ref.at[1], (5, 3)),
-            (0, first_ref, second_ref, (6, 7)),
-        )
-        for j, first, second, complete in quarters:
-            quarter = scalar_ref[1] ^ j
+            (1, x_ref.at[1], x_next_ref, (0, 2)),
+            (2, y_next_ref, y_ref.at[1], (1, 3)),
+            (0, first_ref, second_ref, (4, 5)),
+        )
+        for j, first, second, complete in plan:
+            quarter = place ^ j
             both = lambda old, new: jnp.concatenate([old[quarter], new[quarter]], axis=0)
             for k, d_pre in enumerate((both(saved[3], dgate), both(saved[4], dup))):
                 part = mm_tn(all_rows, d_pre).astype(BF16)
@@ -256,18 +253,27 @@
             part = mm_tn(both(saved[2], hid), all_cots).astype(BF16)
             first[2] = part[:, :half]
             second[2] = part[:, half:]
-            for k in complete:
-                stores[k].start()
+            for n in complete:
+                stores[2 + n].start()
     for store in stores:
         store.wait()
 
 
+def finish_kernel(*refs):
+    gate_ref, up_ref, down_ref = refs[6:]
+    half = gate_ref.shape[0] // 2
+    for k in (0, 1):
+        mine, got, late = refs[3 * k : 3 * k + 3]
+        total = mine[...].astype(F32) + got[1].astype(F32) + late[...].astype(F32)
+        total = total.astype(BF16)
+        at = slice(k * half, (k + 1) * half)
+        gate_ref[at] = total[0]
+        up_ref[at] = total[1]
+        down_ref[:, at] = total[2]
+
+
 def vmem():
     return pl.BlockSpec(memory_space=pltpu.VMEM)
-
-
-def smem():
-    return pl.BlockSpec(memory_space=pltpu.SMEM)
 
 
 def run_pack(tokens, cotangent, codes):
@@ -281,7 +287,7 @@
     )(tokens, cotangent, codes.T)
 
 
-def run_arm(scalars, parts, capacity, weights, piece, saved=()):
+def run_arm(parts, capacity, weights, piece, saved=()):
     blocks = len(parts)
     width, hidden_width = weights[0].shape
     count = (parts[0].shape[0] - CODE_ROWS) // 2
@@ -297,14 +303,13 @@
     anywhere = pl.BlockSpec(memory_space=pl.ANY)
     return pl.pallas_call(
         functools.partial(arm_kernel, blocks, len(sources), len(outs)),
-        in_specs=[smem()] + [anywhere] * len(sources),
+        in_specs=[anywhere] * len(sources),
         out_specs=[anywhere] * len(outs),
         out_shape=[jax.ShapeDtypeStruct(shape, BF16) for shape in outs],
         scratch_shapes=[pltpu.VMEM(shape, BF16) for shape in held + outs]
         + [
             pltpu.SemaphoreType.DMA((len(sources),)),
             pltpu.SemaphoreType.DMA((len(outs),)),
-            pltpu.VMEM((blocks, capacity, 2 * count), BF16),
         ],
         compiler_params=pltpu.CompilerParams(vmem_limit_bytes=VMEM_BYTES),
         cost_estimate=pl.CostEstimate(
@@ -313,7 +318,21 @@
             transcendentals=0,
         ),
         name="arm_late" if saved else "arm_early",
-    )(scalars, *sources)
+    )(*sources)
+
+
+def run_finish(*parts):
+    _, half, share = parts[0].shape
+    width = 2 * half
+    outs = [(width, share), (width, share), (share, width)]
+    return pl.pallas_call(
+        finish_kernel,
+        in_specs=[vmem()] * 6,
+        out_specs=[vmem()] * 3,
+        out_shape=[jax.ShapeDtypeStruct(shape, BF16) for shape in outs],
+        compiler_params=pltpu.CompilerParams(vmem_limit_bytes=8 * 1024 * 1024),
+        name="finish",
+    )(*parts)
 
 
 def on_line(tokens, codes, cotangent, w_gate, w_up, w_down):
@@ -323,10 +342,7 @@
     w_gate, w_up, w_down = w_gate[0], w_up[0], w_down[0]
     hidden_width = w_gate.shape[1]
     chunk = hidden_width // lax.axis_size("dp")
-    expert = lax.axis_index("expert")
-    arm = jnp.reshape(expert, (1,)).astype(jnp.int32)
-    place = jnp.reshape(lax.axis_index("dp"), (1,)).astype(jnp.int32)
-    z = expert // 2
+    z = lax.axis_index("expert") // 2
     edge = (z == 0) | (z == 3)
 
     def along(pairs):
@@ -346,7 +362,6 @@
     add = lambda a, b: a.astype(F32) + b.astype(F32)
     run = functools.partial(
         run_arm,
-        jnp.concatenate([arm, place]),
         capacity=capacity,
         weights=(w_gate, w_up, w_down),
         piece=chunk,
@@ -365,21 +380,20 @@
     got = send(give, core)
     for_far = add(keep[0], got[0])
     for_skip = add(keep[1], got[1]).astype(BF16)
-    from_x = send_dp(x_part, x_pair)
-    from_y = send_dp(y_part, y_pair)
+    from_x, from_y = send_dp(x_part, x_pair), send_dp(y_part, y_pair)
     from_skip = send(for_skip, skip_back).astype(F32)
     from_near = send(for_near, near)
     for_far = for_far + jnp.where(edge, 0.0, from_skip)
     from_far = send(for_far.astype(BF16), far)
     result = for_own + from_near + from_far + jnp.where(edge, from_skip, 0.0)
     head_output, grad_tokens = result[0].astype(BF16), result[1].astype(BF16)
+
     y_next = add(y_next, from_x[0]).astype(BF16)
     x_next = add(x_next, from_y[0]).astype(BF16)
-    k0 = (add(k0, from_x[1]) + send_dp(y_next, y_pair)).astype(BF16)
-    k1 = (add(k1, from_y[1]) + send_dp(x_next, x_pair)).astype(BF16)
-    grad_gate = jnp.concatenate([k0[0], k1[0]], axis=0)[None]
-    grad_up = jnp.concatenate([k0[1], k1[1]], axis=0)[None]
-    grad_down = jnp.concatenate([k0[2], k1[2]], axis=1)[None]
+    grads = run_finish(
+        k0, from_x, send_dp(y_next, y_pair), k1, from_y, send_dp(x_next, x_pair)
+    )
+    grad_gate, grad_up, grad_down = (part[None] for part in grads)
     return (head_output, grad_tokens, grad_gate, grad_up, grad_down)
 
 

time: 75.8 us -> 72.4 us (0.955)
  other arithmetic: 5.1 us -> 2.65 us
  waiting for transfers between devices: 33 us -> 30.7 us
  starting transfers between devices: 17.9 us -> 20.1 us
    ppermute x12, starting transfers between devices: 11.8 us -> 13.9 us  [on_line(): send = lambda value, pairs: lax.ppermute(value, 'expert', pairs)]
    ppermute x4, waiting for transfers between devices: 11.8 us -> 9.72 us  [on_line(): send_dp = lambda value, pairs: lax.ppermute(value, 'dp', pairs)]
    pallas_call x2, Pallas kernels: 14.7 us -> 12.9 us  [run_arm(): pl.pallas_call(functools.partial(arm_kernel, blocks, len(sources), len(ou...]
    broadcast_in_dim x2 -> x0, other arithmetic: 1.54 us -> none  [the longest x1 0.82 us: on_line(): grad_gate = jnp.concatenate([k0[0], k1[0]], axis=0)[None]]
    pallas_call x0 -> x1, Pallas kernels: none -> 1.09 us  [run_finish(): pl.pallas_call(finish_kernel, in_specs=[vmem()] * 6, out_specs=[vmem()] *...]
  transfers between devices with their start and end apart: 16 -> 16, of which waited for: 8 -> 9; matrix products, arithmetic and copies ran while one was open for 5% -> 5% of each run, Pallas kernels for 8% -> 8%
where the time goes in v3:
time: 72.4 us; the launch traced here: 72.2 us
  waiting for transfers between devices  30.7 us (42%)
  starting transfers between devices  20.1 us (28%)
  Pallas kernels  15.7 us (22%)
  other arithmetic  2.65 us (4%)
  local copies, waits for them, and re-layouts  2.3 us (3%)
  between operations  0.77 us (1%)
    ppermute x12, waiting for transfers between devices, on_line(): send = lambda value, pairs: lax.ppermute(value, 'expert', pairs)  21 us
    ppermute x12, starting transfers between devices, on_line(): send = lambda value, pairs: lax.ppermute(value, 'expert', pairs)  13.9 us
    pallas_call x2, Pallas kernels, run_arm(): pl.pallas_call(functools.partial(arm_kernel, blocks, len(sources), len(ou...  12.9 us
    ppermute x4, waiting for transfers between devices, on_line(): send_dp = lambda value, pairs: lax.ppermute(value, 'dp', pairs)  9.72 us
    ppermute x4, starting transfers between devices, on_line(): send_dp = lambda value, pairs: lax.ppermute(value, 'dp', pairs)  6.16 us
    pallas_call x1, Pallas kernels, run_pack(): pl.pallas_call(pack_kernel, in_specs=[vmem()] * 3, out_specs=vmem(), out_...  1.7 us
    unnamed x28, local copies, waits for them, and re-layouts  1.59 us
  transfers between devices with their start and end apart: 16, of which 9 were waited for; matrix products, arithmetic and copies ran while one was open for 5% of the time, Pallas kernels for 8%

profile of v3, /device:TPU:0, one launch (start us, length us, event | category | flops | bytes accessed | tf_op | source)
XLA Modules:
  0.0 72.2 jit_solution(14700348814657798625)
XLA Ops:
  0.6 1.7 %pack.1.refs_0_ = bf16[272,512]{1,0:T(8,128)(2,1)} custom-call(bf16[128,512]{1,0:T(8,128)(2,1)} %tokens_ref.1, bf16[128,512]{1,0:T(8,128)(2,1)} %cot_ref.1, s32[2,128]{1,0:T(2,128)} %bitcast.33), custom_call_target="tpu_custom_call" | custom-call | tf_op jit(solution)/shard_map/pack/pallas_call | solution.py:281
  2.3 3.0 %collective-permute-start.2 = (bf16[272,512]{1,0:T(8,128)(2,1)}, bf16[272,512]{1,0:T(8,128)(2,1)S(1)}, u32[]{:S(2)}, u32[]{:S(2)}) collective-permute-start(bf16[272,512]{1,0:T(8,128)(2,1)} %pack.1.refs_0_), channel_id=1, source_target_pairs={{0,2},{1,3},{2,0},{3,1},{4,6},{5,7},{6,4},{7,5},{8,10},{9,11},{10,... | collective-permute-start | bytes 835592 | tf_op jit(solution)/shard_map/ppermute | solution.py:358
  5.4 2.5 %collective-permute-start = (bf16[272,512]{1,0:T(8,128)(2,1)}, bf16[272,512]{1,0:T(8,128)(2,1)S(1)}, u32[]{:S(2)}, u32[]{:S(2)}) collective-permute-start(bf16[272,512]{1,0:T(8,128)(2,1)} %pack.1.refs_0_), channel_id=1, source_target_pairs={{0,6},{1,7},{6,0},{7,1},{2,4},{3,5},{4,2},{5,3},{8,14},{9,15},{14,... | collective-permute-start | bytes 835592 | tf_op jit(solution)/shard_map/ppermute | solution.py:358
  7.8 0.0 collective-permute-start.3
  7.8 4.9 %collective-permute-done.2.refs_1_ = bf16[272,512]{1,0:T(8,128)(2,1)S(1)} collective-permute-done((bf16[272,512]{1,0:T(8,128)(2,1)}, bf16[272,512]{1,0:T(8,128)(2,1)S(1)}, u32[]{:S(2)}, u32[]{:S(2)}) %collective-permute-start.2) | collective-permute-done | bytes 278560 | tf_op jit(solution)/shard_map/ppermute | solution.py:358
  12.7 0.0 collective-permute-start.4
  12.7 7.7 %collective-permute-done.refs_0_ = bf16[272,512]{1,0:T(8,128)(2,1)S(1)} collective-permute-done((bf16[272,512]{1,0:T(8,128)(2,1)}, bf16[272,512]{1,0:T(8,128)(2,1)S(1)}, u32[]{:S(2)}, u32[]{:S(2)}) %collective-permute-start) | collective-permute-done | bytes 278560 | tf_op jit(solution)/shard_map/ppermute | solution.py:358
  20.5 1.1 %broadcast_select_fusion = bf16[272,512]{1,0:T(8,128)(2,1)S(1)} fusion(bf16[272,512]{1,0:T(8,128)(2,1)} %pack.1.refs_0_, bf16[272,512]{1,0:T(8,128)(2,1)S(1)} %collective-permute-done.refs_0_, pred[]{:T(512)S(6)} %or.3), kind=kLoop, calls=%fused_computation.16 | loop fusion | flops 139264 | bytes 835585 | tf_op jit(solution)/shard_map/jit(_where)/select_n | solution.py:372
  21.6 0.8 %collective-permute-start.1 = (bf16[272,512]{1,0:T(8,128)(2,1)S(1)}, bf16[272,512]{1,0:T(8,128)(2,1)S(1)}, u32[]{:S(2)}, u32[]{:S(2)}) collective-permute-start(bf16[272,512]{1,0:T(8,128)(2,1)S(1)} %broadcast_select_fusion), channel_id=1, source_target_pairs={{0,4},{1,5},{4,6},{5,7},{6,2},{7,3},{2,0},{3,1},{8,12},{9,13},{12,... | collective-permute-start | bytes 835592 | tf_op jit(solution)/shard_map/ppermute | solution.py:358
  22.3 0.0 copy-done.6
  22.3 0.0 collective-permute-start.7
  22.3 0.0 collective-permute-done.3.refs_2_
  22.4 0.0 collective-permute-done.4.refs_3_
  22.4 0.7 copy-done.9
  23.1 0.1 copy-done.12
  23.2 5.5 %arm_early.1 = (bf16[2,2,128,512]{3,2,1,0:T(8,128)(2,1)}, bf16[2,2,128,512]{3,2,1,0:T(8,128)(2,1)}, bf16[256,512]{1,0:T(8,128)(2,1)}, bf16[256,512]{1,0:T(8,128)...) custom-call(bf16[272,512]{1,0:T(8,128)(2,1)} %pack.1.refs_0_, ...), custom_call_target="tpu_custom_call" | custom-call | flops 1610612736 | bytes 12582912 | tf_op jit(solution)/shard_map/arm_early/pallas_call | solution.py:304
  28.6 0.5 collective-permute-done.1.refs_1_
  29.1 0.1 collective-permute-start.8
  29.2 0.0 collective-permute-done.7.refs_2_
  29.2 1.4 %collective-permute-done.8.refs_3_ = bf16[272,512]{1,0:T(8,128)(2,1)S(1)} collective-permute-done((bf16[272,512]{1,0:T(8,128)(2,1)S(1)}, bf16[272,512]{1,0:T(8,128)(2,1)S(1)}, u32[]{:S(2)}, u32[]{:S(2)}) %collective-permute-start.8) | collective-permute-done | bytes 278560 | tf_op jit(solution)/shard_map/ppermute | solution.py:358
  30.7 0.8 %copy-done.13 = bf16[272,512]{1,0:T(8,128)(2,1)} copy-done((bf16[272,512]{1,0:T(8,128)(2,1)}, bf16[272,512]{1,0:T(8,128)(2,1)S(1)}, u32[]{:S(2)}) %copy-start.13) | copy-done | bytes 278552
  31.4 7.5 %arm_late.1 = (bf16[2,2,128,512]{3,2,1,0:T(8,128)(2,1)}, bf16[2,2,128,512]{3,2,1,0:T(8,128)(2,1)}, bf16[2,3,256,256]{3,2,1,0:T(8,128)(2,1)}, bf16[2,3,256,256]{3...) custom-call(bf16[272,512]{1,0:T(8,128)(2,1)} %copy-done.6, ...), custom_call_target="tpu_custom_call" | custom-call | flops 3221225472 | bytes 12582912 | tf_op jit(solution)/shard_map/arm_late/pallas_call | solution.py:304
  38.9 0.2 collective-permute-start.9
  39.1 0.4 collective-permute-start.5
  39.5 1.5 %collective-permute-start.14 = (bf16[2,3,256,256]{3,2,1,0:T(8,128)(2,1)}, bf16[2,3,256,256]{3,2,1,0:T(8,128)(2,1)S(1)}, u32[]{:S(2)}, u32[]{:S(2)}) collective-permute-start(bf16[2,3,256,256]{3,2,1,0:T(8,128)(2,1)} %get-tuple-element.40), channel_id=1, source_target_pairs={{0,16},{8,24},{16,0},{24,8},{1,17},{9,25},{17,1},{25,9},{2,18},{10... | collective-permute-start | bytes 2359304 | tf_op jit(solution)/shard_map/ppermute | solution.py:359
  41.0 1.5 %collective-permute-start.12 = (bf16[2,3,256,256]{3,2,1,0:T(8,128)(2,1)}, bf16[2,3,256,256]{3,2,1,0:T(8,128)(2,1)S(1)}, u32[]{:S(2)}, u32[]{:S(2)}) collective-permute-start(bf16[2,3,256,256]{3,2,1,0:T(8,128)(2,1)} %get-tuple-element.37), channel_id=1, source_target_pairs={{0,8},{8,0},{16,24},{24,16},{1,9},{9,1},{17,25},{25,17},{2,10},{10... | collective-permute-start | bytes 2359304 | tf_op jit(solution)/shard_map/ppermute | solution.py:359
  42.5 0.0 collective-permute-done.9
  42.5 1.0 %fusion.8 = bf16[2,128,512]{2,1,0:T(8,128)(2,1)S(1)} fusion(bf16[2,2,128,512]{3,2,1,0:T(8,128)(2,1)S(1)} %collective-permute-done.9, bf16[2,2,128,512]{3,2,1,0:T(8,128)(2,1)} %get-tuple-element.34), kind=kLoop, calls=%fused_computation.18 | loop fusion | flops 524288 | bytes 786432 | tf_op jit(solution)/shard_map/convert_element_type | solution.py:382
  43.6 1.9 %collective-permute-start.10 = (bf16[2,128,512]{2,1,0:T(8,128)(2,1)S(1)}, bf16[2,128,512]{2,1,0:T(8,128)(2,1)S(1)}, u32[]{:S(2)}, u32[]{:S(2)}) collective-permute-start(bf16[2,128,512]{2,1,0:T(8,128)(2,1)S(1)} %fusion.8), channel_id=1, source_target_pairs={{4,0},{5,1},{6,4},{7,5},{2,6},{3,7},{0,2},{1,3},{12,8},{13,9},{14,... | collective-permute-start | bytes 786440 | tf_op jit(solution)/shard_map/ppermute | solution.py:358
  45.5 0.0 collective-permute-done.5
  45.5 0.1 fusion.7
  45.6 1.8 %collective-permute-start.6 = (bf16[2,128,512]{2,1,0:T(8,128)(2,1)S(1)}, bf16[2,128,512]{2,1,0:T(8,128)(2,1)S(1)}, u32[]{:S(2)}, u32[]{:S(2)}) collective-permute-start(bf16[2,128,512]{2,1,0:T(8,128)(2,1)S(1)} %fusion.7), channel_id=1, source_target_pairs={{0,2},{1,3},{2,0},{3,1},{4,6},{5,7},{6,4},{7,5},{8,10},{9,11},{10,... | collective-permute-start | bytes 786440 | tf_op jit(solution)/shard_map/ppermute | solution.py:358
  47.4 5.0 %collective-permute-done.10 = bf16[2,128,512]{2,1,0:T(8,128)(2,1)S(1)} collective-permute-done((bf16[2,128,512]{2,1,0:T(8,128)(2,1)S(1)}, bf16[2,128,512]{2,1,0:T(8,128)(2,1)S(1)}, u32[]{:S(2)}, u32[]{:S(2)}) %collective-permute-start.10) | collective-permute-done | bytes 262176 | tf_op jit(solution)/shard_map/ppermute | solution.py:358
  52.4 0.1 fusion.3
  52.5 3.2 %collective-permute-start.11 = (bf16[2,128,512]{2,1,0:T(8,128)(2,1)S(1)}, bf16[2,128,512]{2,1,0:T(8,128)(2,1)S(1)}, u32[]{:S(2)}, u32[]{:S(2)}) collective-permute-start(bf16[2,128,512]{2,1,0:T(8,128)(2,1)S(1)} %fusion.3), channel_id=1, source_target_pairs={{0,6},{1,7},{6,0},{7,1},{2,4},{3,5},{4,2},{5,3},{8,14},{9,15},{14,... | collective-permute-start | bytes 786440 | tf_op jit(solution)/shard_map/ppermute | solution.py:358
  55.7 3.6 %collective-permute-done.14.refs_4_ = bf16[2,3,256,256]{3,2,1,0:T(8,128)(2,1)S(1)} collective-permute-done((bf16[2,3,256,256]{3,2,1,0:T(8,128)(2,1)}, bf16[2,3,256,256]{3,2,1,0:T(8,128)(2,1)S(1)}, u32[]{:S(2)}, u32[]{:S(2)}) %collective-permute-start.14) | collective-permute-done | bytes 786464 | tf_op jit(solution)/shard_map/ppermute | solution.py:359
  59.3 0.1 fusion
  59.4 1.6 %collective-permute-start.15 = (bf16[3,256,256]{2,1,0:T(8,128)(2,1)S(1)}, bf16[3,256,256]{2,1,0:T(8,128)(2,1)S(1)}, u32[]{:S(2)}, u32[]{:S(2)}) collective-permute-start(bf16[3,256,256]{2,1,0:T(8,128)(2,1)S(1)} %fusion), channel_id=1, source_target_pairs={{0,8},{8,0},{16,24},{24,16},{1,9},{9,1},{17,25},{25,17},{2,10},{10... | collective-permute-start | bytes 1179656 | tf_op jit(solution)/shard_map/ppermute | solution.py:359
  61.0 0.0 collective-permute-done.12.refs_1_
  61.0 0.1 fusion.1
  61.1 1.6 %collective-permute-start.13 = (bf16[3,256,256]{2,1,0:T(8,128)(2,1)S(1)}, bf16[3,256,256]{2,1,0:T(8,128)(2,1)S(1)}, u32[]{:S(2)}, u32[]{:S(2)}) collective-permute-start(bf16[3,256,256]{2,1,0:T(8,128)(2,1)S(1)} %fusion.1), channel_id=1, source_target_pairs={{0,16},{8,24},{16,0},{24,8},{1,17},{9,25},{17,1},{25,9},{2,18},{10... | collective-permute-start | bytes 1179656 | tf_op jit(solution)/shard_map/ppermute | solution.py:359
  62.6 0.0 collective-permute-done.6
  62.6 1.5 %collective-permute-done.11 = bf16[2,128,512]{2,1,0:T(8,128)(2,1)S(1)} collective-permute-done((bf16[2,128,512]{2,1,0:T(8,128)(2,1)S(1)}, bf16[2,128,512]{2,1,0:T(8,128)(2,1)S(1)}, u32[]{:S(2)}, u32[]{:S(2)}) %collective-permute-start.11) | collective-permute-done | bytes 262176 | tf_op jit(solution)/shard_map/ppermute | solution.py:358
  64.1 0.2 fusion.5
  64.3 0.7 slice_bitcast_fusion.2
  65.0 4.8 %collective-permute-done.15.refs_5_ = bf16[3,256,256]{2,1,0:T(8,128)(2,1)S(1)} collective-permute-done((bf16[3,256,256]{2,1,0:T(8,128)(2,1)S(1)}, bf16[3,256,256]{2,1,0:T(8,128)(2,1)S(1)}, u32[]{:S(2)}, u32[]{:S(2)}) %collective-permute-start.15) | collective-permute-done | bytes 393248 | tf_op jit(solution)/shard_map/ppermute | solution.py:359
  69.8 1.3 %collective-permute-done.13.refs_2_ = bf16[3,256,256]{2,1,0:T(8,128)(2,1)S(1)} collective-permute-done((bf16[3,256,256]{2,1,0:T(8,128)(2,1)S(1)}, bf16[3,256,256]{2,1,0:T(8,128)(2,1)S(1)}, u32[]{:S(2)}, u32[]{:S(2)}) %collective-permute-start.13) | collective-permute-done | bytes 393248 | tf_op jit(solution)/shard_map/ppermute | solution.py:359
  71.2 1.1 %finish.1 = (bf16[512,256]{1,0:T(8,128)(2,1)}, bf16[512,256]{1,0:T(8,128)(2,1)}, bf16[256,512]{1,0:T(8,128)(2,1)}) custom-call(bf16[3,256,256]{2,1,0:T(8,128)(2,1)S(1)} %copy-done, bf16[2,3,256,256]{3,2,1,0:T(8,128)(2,1)S(1)} %collective-permute-done.12.refs_1_, bf16[3,256,256]{2,1,0:T(8,128)(2,1)S(1)} %collective-permute-done.13.refs_2_, ...), custom_call_target="tpu_custom_call" | custom-call | tf_op jit(solution)/shard_map/finish/pallas_call | solution.py:328
  (24 shorter events, 0.0 us)
Async XLA Ops:
  2.3 10.4 %collective-permute-start.2 = (bf16[272,512]{1,0:T(8,128)(2,1)}, bf16[272,512]{1,0:T(8,128)(2,1)S(1)}, u32[]{:S(2)}, u32[]{:S(2)}) collective-permute-start(bf16[272,512]{1,0:T(8,128)(2,1)} %pack.1.refs_0_), channel_id=1, source_target_pairs={{0,2},{1,3},{2,0},{3,1},{4,6},{5,7},{6,4},{7,5},{8,10},{9,11},{10,... | collective-permute-start | bytes 835592 | tf_op jit(solution)/shard_map/ppermute | solution.py:358
  5.4 15.1 %collective-permute-start = (bf16[272,512]{1,0:T(8,128)(2,1)}, bf16[272,512]{1,0:T(8,128)(2,1)S(1)}, u32[]{:S(2)}, u32[]{:S(2)}) collective-permute-start(bf16[272,512]{1,0:T(8,128)(2,1)} %pack.1.refs_0_), channel_id=1, source_target_pairs={{0,6},{1,7},{6,0},{7,1},{2,4},{3,5},{4,2},{5,3},{8,14},{9,15},{14,... | collective-permute-start | bytes 835592 | tf_op jit(solution)/shard_map/ppermute | solution.py:358
  7.8 14.5 %collective-permute-start.3 = (bf16[272,512]{1,0:T(8,128)(2,1)}, bf16[272,512]{1,0:T(8,128)(2,1)S(1)}, u32[]{:S(2)}, u32[]{:S(2)}) collective-permute-start(bf16[272,512]{1,0:T(8,128)(2,1)} %pack.1.refs_0_), channel_id=1, source_target_pairs={{0,1},{1,0},{2,3},{3,2},{4,5},{5,4},{6,7},{7,6},{8,9},{9,8},{10,11... | collective-permute-start | bytes 835592 | tf_op jit(solution)/shard_map/ppermute | solution.py:358
  12.7 8.8 %copy-start.8 = (bf16[272,512]{1,0:T(8,128)(2,1)}, bf16[272,512]{1,0:T(8,128)(2,1)S(1)}, u32[]{:S(2)}) copy-start(bf16[272,512]{1,0:T(8,128)(2,1)S(1)} %collective-permute-done.2.refs_1_) | copy-start | bytes 835588
  12.7 9.6 %collective-permute-start.4 = (bf16[272,512]{1,0:T(8,128)(2,1)S(1)}, bf16[272,512]{1,0:T(8,128)(2,1)S(1)}, u32[]{:S(2)}, u32[]{:S(2)}) collective-permute-start(bf16[272,512]{1,0:T(8,128)(2,1)S(1)} %collective-permute-done.2.refs_1_), channel_id=1, source_target_pairs={{0,1},{1,0},{2,3},{3,2},{4,5},{5,4},{6,7},{7,6},{8,9},{9,8},{10,11... | collective-permute-start | bytes 835592 | tf_op jit(solution)/shard_map/ppermute | solution.py:358
  20.5 1.9 %copy-start.6 = (bf16[272,512]{1,0:T(8,128)(2,1)}, bf16[272,512]{1,0:T(8,128)(2,1)S(1)}, u32[]{:S(2)}) copy-start(bf16[272,512]{1,0:T(8,128)(2,1)S(1)} %collective-permute-done.refs_0_) | copy-start | bytes 835588
  21.6 7.5 %collective-permute-start.1 = (bf16[272,512]{1,0:T(8,128)(2,1)S(1)}, bf16[272,512]{1,0:T(8,128)(2,1)S(1)}, u32[]{:S(2)}, u32[]{:S(2)}) collective-permute-start(bf16[272,512]{1,0:T(8,128)(2,1)S(1)} %broadcast_select_fusion), channel_id=1, source_target_pairs={{0,4},{1,5},{4,6},{5,7},{6,2},{7,3},{2,0},{3,1},{8,12},{9,13},{12,... | collective-permute-start | bytes 835592 | tf_op jit(solution)/shard_map/ppermute | solution.py:358
  22.3 6.9 %collective-permute-start.7 = (bf16[272,512]{1,0:T(8,128)(2,1)S(1)}, bf16[272,512]{1,0:T(8,128)(2,1)S(1)}, u32[]{:S(2)}, u32[]{:S(2)}) collective-permute-start(bf16[272,512]{1,0:T(8,128)(2,1)S(1)} %collective-permute-done.refs_0_), channel_id=1, source_target_pairs={{0,1},{1,0},{2,3},{3,2},{4,5},{5,4},{6,7},{7,6},{8,9},{9,8},{10,11... | collective-permute-start | bytes 835592 | tf_op jit(solution)/shard_map/ppermute | solution.py:358
  22.4 0.7 copy-start.9
  22.4 0.8 %copy-start.12 = (bf16[272,512]{1,0:T(8,128)(2,1)}, bf16[272,512]{1,0:T(8,128)(2,1)S(1)}, u32[]{:S(2)}) copy-start(bf16[272,512]{1,0:T(8,128)(2,1)S(1)} %collective-permute-done.4.refs_3_) | copy-start | bytes 835588
  29.1 1.6 %copy-start.10 = (bf16[272,512]{1,0:T(8,128)(2,1)}, bf16[272,512]{1,0:T(8,128)(2,1)S(1)}, u32[]{:S(2)}) copy-start(bf16[272,512]{1,0:T(8,128)(2,1)S(1)} %collective-permute-done.1.refs_1_) | copy-start | bytes 835588
  29.1 1.6 %collective-permute-start.8 = (bf16[272,512]{1,0:T(8,128)(2,1)S(1)}, bf16[272,512]{1,0:T(8,128)(2,1)S(1)}, u32[]{:S(2)}, u32[]{:S(2)}) collective-permute-start(bf16[272,512]{1,0:T(8,128)(2,1)S(1)} %collective-permute-done.1.refs_1_), channel_id=1, source_target_pairs={{0,1},{1,0},{2,3},{3,2},{4,5},{5,4},{6,7},{7,6},{8,9},{9,8},{10,11... | collective-permute-start | bytes 835592 | tf_op jit(solution)/shard_map/ppermute | solution.py:358
  29.2 1.4 %copy-start.11 = (bf16[272,512]{1,0:T(8,128)(2,1)}, bf16[272,512]{1,0:T(8,128)(2,1)S(1)}, u32[]{:S(2)}) copy-start(bf16[272,512]{1,0:T(8,128)(2,1)S(1)} %collective-permute-done.7.refs_2_) | copy-start | bytes 835588
  30.7 0.8 %copy-start.13 = (bf16[272,512]{1,0:T(8,128)(2,1)}, bf16[272,512]{1,0:T(8,128)(2,1)S(1)}, u32[]{:S(2)}) copy-start(bf16[272,512]{1,0:T(8,128)(2,1)S(1)} %collective-permute-done.8.refs_3_) | copy-start | bytes 835588
  31.4 7.7 %copy-start.7 = (bf16[2,2,128,512]{3,2,1,0:T(8,128)(2,1)S(1)}, bf16[2,2,128,512]{3,2,1,0:T(8,128)(2,1)}, u32[]{:S(2)}) copy-start(bf16[2,2,128,512]{3,2,1,0:T(8,128)(2,1)} %get-tuple-element.27) | copy-start | bytes 1572868
  38.9 6.6 %copy-start.2 = (bf16[2,2,128,512]{3,2,1,0:T(8,128)(2,1)S(1)}, bf16[2,2,128,512]{3,2,1,0:T(8,128)(2,1)}, u32[]{:S(2)}) copy-start(bf16[2,2,128,512]{3,2,1,0:T(8,128)(2,1)} %get-tuple-element.26) | copy-start | bytes 1572868
  38.9 3.6 %collective-permute-start.9 = (bf16[2,2,128,512]{3,2,1,0:T(8,128)(2,1)}, bf16[2,2,128,512]{3,2,1,0:T(8,128)(2,1)S(1)}, u32[]{:S(2)}, u32[]{:S(2)}) collective-permute-start(bf16[2,2,128,512]{3,2,1,0:T(8,128)(2,1)} %get-tuple-element.35), channel_id=1, source_target_pairs={{0,1},{1,0},{2,3},{3,2},{4,5},{5,4},{6,7},{7,6},{8,9},{9,8},{10,11... | collective-permute-start | bytes 1572872 | tf_op jit(solution)/shard_map/ppermute | solution.py:358
  39.1 6.4 %collective-permute-start.5 = (bf16[2,2,128,512]{3,2,1,0:T(8,128)(2,1)S(1)}, bf16[2,2,128,512]{3,2,1,0:T(8,128)(2,1)S(1)}, u32[]{:S(2)}, u32[]{:S(2)}) collective-permute-start(bf16[2,2,128,512]{3,2,1,0:T(8,128)(2,1)S(1)} %copy-done.7), channel_id=1, source_target_pairs={{0,1},{1,0},{2,3},{3,2},{4,5},{5,4},{6,7},{7,6},{8,9},{9,8},{10,11... | collective-permute-start | bytes 1572872 | tf_op jit(solution)/shard_map/ppermute | solution.py:358
  39.5 19.8 %collective-permute-start.14 = (bf16[2,3,256,256]{3,2,1,0:T(8,128)(2,1)}, bf16[2,3,256,256]{3,2,1,0:T(8,128)(2,1)S(1)}, u32[]{:S(2)}, u32[]{:S(2)}) collective-permute-start(bf16[2,3,256,256]{3,2,1,0:T(8,128)(2,1)} %get-tuple-element.40), channel_id=1, source_target_pairs={{0,16},{8,24},{16,0},{24,8},{1,17},{9,25},{17,1},{25,9},{2,18},{10... | collective-permute-start | bytes 2359304 | tf_op jit(solution)/shard_map/ppermute | solution.py:359
  41.0 19.9 %collective-permute-start.12 = (bf16[2,3,256,256]{3,2,1,0:T(8,128)(2,1)}, bf16[2,3,256,256]{3,2,1,0:T(8,128)(2,1)S(1)}, u32[]{:S(2)}, u32[]{:S(2)}) collective-permute-start(bf16[2,3,256,256]{3,2,1,0:T(8,128)(2,1)} %get-tuple-element.37), channel_id=1, source_target_pairs={{0,8},{8,0},{16,24},{24,16},{1,9},{9,1},{17,25},{25,17},{2,10},{10... | collective-permute-start | bytes 2359304 | tf_op jit(solution)/shard_map/ppermute | solution.py:359
  43.5 8.8 %copy-start.3 = (bf16[2,2,128,512]{3,2,1,0:T(8,128)(2,1)S(1)}, bf16[2,2,128,512]{3,2,1,0:T(8,128)(2,1)}, u32[]{:S(2)}) copy-start(bf16[2,2,128,512]{3,2,1,0:T(8,128)(2,1)} %get-tuple-element.34) | copy-start | bytes 1572868
  43.6 8.8 %collective-permute-start.10 = (bf16[2,128,512]{2,1,0:T(8,128)(2,1)S(1)}, bf16[2,128,512]{2,1,0:T(8,128)(2,1)S(1)}, u32[]{:S(2)}, u32[]{:S(2)}) collective-permute-start(bf16[2,128,512]{2,1,0:T(8,128)(2,1)S(1)} %fusion.8), channel_id=1, source_target_pairs={{4,0},{5,1},{6,4},{7,5},{2,6},{3,7},{0,2},{1,3},{12,8},{13,9},{14,... | collective-permute-start | bytes 786440 | tf_op jit(solution)/shard_map/ppermute | solution.py:358
  45.6 13.7 %copy-start.5 = (bf16[3,256,256]{2,1,0:T(8,128)(2,1)S(1)}, bf16[3,256,256]{2,1,0:T(8,128)(2,1)}, u32[]{:S(2)}) copy-start(bf16[3,256,256]{2,1,0:T(8,128)(2,1)} %get-tuple-element.41) | copy-start | bytes 1179652
  45.6 17.0 %collective-permute-start.6 = (bf16[2,128,512]{2,1,0:T(8,128)(2,1)S(1)}, bf16[2,128,512]{2,1,0:T(8,128)(2,1)S(1)}, u32[]{:S(2)}, u32[]{:S(2)}) collective-permute-start(bf16[2,128,512]{2,1,0:T(8,128)(2,1)S(1)} %fusion.7), channel_id=1, source_target_pairs={{0,2},{1,3},{2,0},{3,1},{4,6},{5,7},{6,4},{7,5},{8,10},{9,11},{10,... | collective-permute-start | bytes 786440 | tf_op jit(solution)/shard_map/ppermute | solution.py:358
  52.5 11.6 %collective-permute-start.11 = (bf16[2,128,512]{2,1,0:T(8,128)(2,1)S(1)}, bf16[2,128,512]{2,1,0:T(8,128)(2,1)S(1)}, u32[]{:S(2)}, u32[]{:S(2)}) collective-permute-start(bf16[2,128,512]{2,1,0:T(8,128)(2,1)S(1)} %fusion.3), channel_id=1, source_target_pairs={{0,6},{1,7},{6,0},{7,1},{2,4},{3,5},{4,2},{5,3},{8,14},{9,15},{14,... | collective-permute-start | bytes 786440 | tf_op jit(solution)/shard_map/ppermute | solution.py:358
  59.3 1.7 %copy-start.4 = (bf16[3,256,256]{2,1,0:T(8,128)(2,1)S(1)}, bf16[3,256,256]{2,1,0:T(8,128)(2,1)}, u32[]{:S(2)}) copy-start(bf16[3,256,256]{2,1,0:T(8,128)(2,1)} %get-tuple-element.38) | copy-start | bytes 1179652
  59.4 10.4 %collective-permute-start.15 = (bf16[3,256,256]{2,1,0:T(8,128)(2,1)S(1)}, bf16[3,256,256]{2,1,0:T(8,128)(2,1)S(1)}, u32[]{:S(2)}, u32[]{:S(2)}) collective-permute-start(bf16[3,256,256]{2,1,0:T(8,128)(2,1)S(1)} %fusion), channel_id=1, source_target_pairs={{0,8},{8,0},{16,24},{24,16},{1,9},{9,1},{17,25},{25,17},{2,10},{10... | collective-permute-start | bytes 1179656 | tf_op jit(solution)/shard_map/ppermute | solution.py:359
  61.1 10.1 %collective-permute-start.13 = (bf16[3,256,256]{2,1,0:T(8,128)(2,1)S(1)}, bf16[3,256,256]{2,1,0:T(8,128)(2,1)S(1)}, u32[]{:S(2)}, u32[]{:S(2)}) collective-permute-start(bf16[3,256,256]{2,1,0:T(8,128)(2,1)S(1)} %fusion.1), channel_id=1, source_target_pairs={{0,16},{8,24},{16,0},{24,8},{1,17},{9,25},{17,1},{25,9},{2,18},{10... | collective-permute-start | bytes 1179656 | tf_op jit(solution)/shard_map/ppermute | solution.py:359
  64.1 7.0 %copy-start.1 = (bf16[3,256,256]{2,1,0:T(8,128)(2,1)S(1)}, bf16[3,256,256]{2,1,0:T(8,128)(2,1)}, u32[]{:S(2)}) copy-start(bf16[3,256,256]{2,1,0:T(8,128)(2,1)} %get-tuple-element.39.refs_3_) | copy-start | bytes 1179652
  64.3 6.9 %copy-start = (bf16[3,256,256]{2,1,0:T(8,128)(2,1)S(1)}, bf16[3,256,256]{2,1,0:T(8,128)(2,1)}, u32[]{:S(2)}) copy-start(bf16[3,256,256]{2,1,0:T(8,128)(2,1)} %get-tuple-element.36.refs_0_) | copy-start | bytes 1179652

commit v4 on v3

--- a/solution.py
+++ b/solution.py
@@ -13,7 +13,7 @@
 F32 = jnp.float32
 BF16 = jnp.bfloat16
 CODE_ROWS = 16
-VMEM_BYTES = 56 * 1024 * 1024
+VMEM_BYTES = 16 * 1024 * 1024
 
 def rounded(value):
     return lax.optimization_barrier(value.astype(jnp.bfloat16)).astype(jnp.float32)
@@ -163,40 +163,25 @@
     out_ref[2 * count : 2 * count + CODE_ROWS, 0:count] = both.astype(BF16)
 
 
-def arm_kernel(blocks, ins, outs_count, *refs):
-    sources, refs = refs[:ins], refs[ins:]
-    outs, refs = refs[:outs_count], refs[outs_count:]
-    in_sems, out_sems = refs[-2:]
-    staged, refs = refs[-2 - outs_count : -2], refs[: -2 - outs_count]
-    held, (gate_ref, up_ref, down_ref), saved = refs[0], refs[1:4], refs[4:]
+def arm_kernel(blocks, outs_count, *refs):
+    held, refs = refs[:blocks], refs[blocks:]
+    (gate_ref, up_ref, down_ref), refs = refs[:3], refs[3:]
+    saved, refs = (refs[:5], refs[5:]) if outs_count == 8 else ((), refs)
+    staged, made = refs[:outs_count], refs[outs_count:]
     keep_ref, give_ref = staged[:2]
-    rows, cots, hid, dgate, dup = saved[5:] if saved else staged[2:]
+    rows, cots, hid, dgate, dup = made if saved else staged[2:]
     capacity, count = rows.shape[0] // blocks, keep_ref.shape[2]
     pieces = hid.shape[0]
-    targets = [held.at[b] for b in range(blocks)] + [gate_ref, up_ref, down_ref, *saved[:5]]
-    loads = [
-        pltpu.make_async_copy(source, target, in_sems.at[k])
-        for k, (source, target) in enumerate(zip(sources, targets))
-    ]
-    stores = [
-        pltpu.make_async_copy(source, target, out_sems.at[k])
-        for k, (source, target) in enumerate(zip(staged, outs))
-    ]
-    for load in loads:
-        load.start()
     arm, place = lax.axis_index("expert"), lax.axis_index("dp")
-    for load in loads[:blocks]:
-        load.wait()
-
-    tiles = [held[b, 2 * count : 2 * count + CODE_ROWS, 0:count] for b in range(blocks)]
+
+    tiles = [ref[2 * count : 2 * count + CODE_ROWS, 0:count] for ref in held]
     chosen, shares = selections(tiles, arm.astype(F32), capacity)
     for b in range(blocks):
         at = slice(b * capacity, (b + 1) * capacity)
-        rows[at] = mm(chosen[b], held[b, 0:count]).astype(BF16)
-        cots[at] = (mm(chosen[b], held[b, count : 2 * count]) * shares[b]).astype(BF16)
-
-    for load in loads[blocks : blocks + 3]:
-        load.wait()
+        rows[at] = mm(chosen[b], held[b][0:count]).astype(BF16)
+        picked = mm(chosen[b], held[b][count : 2 * count])
+        cots[at] = (picked * shares[b]).astype(BF16)
+
     for k in range(pieces):
         piece = hid.shape[2]
         cut = slice(k * piece, (k + 1) * piece)
@@ -208,9 +193,6 @@
         hid[k] = (activated * up_pre).astype(BF16)
         dup[k] = (d_hidden * activated).astype(BF16)
         dgate[k] = (d_hidden * up_pre * (sig + activated * (1.0 - sig))).astype(BF16)
-    if not saved:
-        for store in stores[2:]:
-            store.start()
 
     total_out, total_in = None, None
     for k in range(pieces):
@@ -226,24 +208,20 @@
         target[b % (blocks // 2), 0] = mm_tn(chosen[b], out_rows).astype(BF16)
         in_rows = total_in[at].astype(BF16)
         target[b % (blocks // 2), 1] = mm_tn(chosen[b], in_rows).astype(BF16)
-    stores[0].start()
-    stores[1].start()
 
     if saved:
-        for load in loads[blocks + 3 :]:
-            load.wait()
         parts = staged[2:]
         all_rows = jnp.concatenate([saved[0][...], rows[...]], axis=0)
         all_cots = jnp.concatenate([saved[1][...], cots[...]], axis=0)
         half = all_rows.shape[1] // 2
         x_ref, y_ref, x_next_ref, y_next_ref, first_ref, second_ref = parts
         plan = (
-            (3, x_ref.at[0], y_ref.at[0], ()),
-            (1, x_ref.at[1], x_next_ref, (0, 2)),
-            (2, y_next_ref, y_ref.at[1], (1, 3)),
-            (0, first_ref, second_ref, (4, 5)),
-        )
-        for j, first, second, complete in plan:
+            (3, x_ref.at[0], y_ref.at[0]),
+            (1, x_ref.at[1], x_next_ref),
+            (2, y_next_ref, y_ref.at[1]),
+            (0, first_ref, second_ref),
+        )
+        for j, first, second in plan:
             quarter = place ^ j
             both = lambda old, new: jnp.concatenate([old[quarter], new[quarter]], axis=0)
             for k, d_pre in enumerate((both(saved[3], dgate), both(saved[4], dup))):
@@ -253,10 +231,6 @@
             part = mm_tn(both(saved[2], hid), all_cots).astype(BF16)
             first[2] = part[:, :half]
             second[2] = part[:, half:]
-            for n in complete:
-                stores[2 + n].start()
-    for store in stores:
-        store.wait()
 
 
 def finish_kernel(*refs):
@@ -283,6 +257,7 @@
         in_specs=[vmem()] * 3,
         out_specs=vmem(),
         out_shape=jax.ShapeDtypeStruct((2 * count + CODE_ROWS, width), BF16),
+        compiler_params=pltpu.CompilerParams(vmem_limit_bytes=4 * 1024 * 1024),
         name="pack",
     )(tokens, cotangent, codes.T)
 
@@ -297,20 +272,13 @@
     made = [(rows, width)] * 2 + [(pieces, rows, piece)] * 3
     outs = [(blocks // 2, 2, count, width)] * 2
     outs += [(2,) + one] * 2 + [one] * 4 if saved else made
-    held = [(blocks,) + parts[0].shape] + [weight.shape for weight in weights]
-    held += [array.shape for array in saved] + made if saved else []
-    sources = (*parts, *weights, *saved)
-    anywhere = pl.BlockSpec(memory_space=pl.ANY)
+    ins = (*parts, *weights, *saved)
     return pl.pallas_call(
-        functools.partial(arm_kernel, blocks, len(sources), len(outs)),
-        in_specs=[anywhere] * len(sources),
-        out_specs=[anywhere] * len(outs),
+        functools.partial(arm_kernel, blocks, len(outs)),
+        in_specs=[vmem()] * len(ins),
+        out_specs=[vmem()] * len(outs),
         out_shape=[jax.ShapeDtypeStruct(shape, BF16) for shape in outs],
-        scratch_shapes=[pltpu.VMEM(shape, BF16) for shape in held + outs]
-        + [
-            pltpu.SemaphoreType.DMA((len(sources),)),
-            pltpu.SemaphoreType.DMA((len(outs),)),
-        ],
+        scratch_shapes=[pltpu.VMEM(shape, BF16) for shape in made] if saved else [],
         compiler_params=pltpu.CompilerParams(vmem_limit_bytes=VMEM_BYTES),
         cost_estimate=pl.CostEstimate(
             flops=(24 if saved else 12) * rows * width * hidden_width,
@@ -318,7 +286,7 @@
             transcendentals=0,
         ),
         name="arm_late" if saved else "arm_early",
-    )(*sources)
+    )(*ins)
 
 
 def run_finish(*parts):

time: 72.4 us -> 67.8 us (0.936)
  Pallas kernels: 15.7 us -> 7.98 us
  local copies, waits for them, and re-layouts: 2.3 us -> 5.65 us
  other arithmetic: 2.65 us -> 0.64 us
  waiting for transfers between devices: 30.7 us -> 31.6 us
  starting transfers between devices: 20.1 us -> 21 us
    pallas_call x2, Pallas kernels: 12.9 us -> 6.87 us  [run_arm(): pl.pallas_call(functools.partial(arm_kernel, blocks, len(outs)), in_specs...]
    unnamed x28 -> x16, local copies, waits for them, and re-layouts: 1.59 us -> 4.93 us
    pallas_call x1, Pallas kernels: 1.7 us -> 0.02 us  [run_pack(): pl.pallas_call(pack_kernel, in_specs=[vmem()] * 3, out_specs=vmem(), out_...]
    ppermute x4, waiting for transfers between devices: 9.72 us -> 11.3 us  [on_line(): send_dp = lambda value, pairs: lax.ppermute(value, 'dp', pairs)]
    select_n x1, other arithmetic: 1.09 us -> 0.03 us  [on_line(): from_skip = send(jnp.where(edge, own, from_far), skip)]
    convert_element_type x1, other arithmetic: 1.02 us -> 0.07 us  [on_line(): for_skip = add(keep[1], got[1]).astype(BF16)]
    ppermute x12, starting transfers between devices: 13.9 us -> 14.9 us  [on_line(): send = lambda value, pairs: lax.ppermute(value, 'expert', pairs)]
  transfers between devices with their start and end apart: 16 -> 16, of which waited for: 9 -> 9; matrix products, arithmetic and copies ran while one was open for 5% -> 2% of each run, Pallas kernels for 8% -> 4%
where the time goes in v4:
time: 67.8 us; the launch traced here: 67.6 us
  waiting for transfers between devices  31.6 us (47%)
  starting transfers between devices  21 us (31%)
  Pallas kernels  7.98 us (12%)
  local copies, waits for them, and re-layouts  5.65 us (8%)
  between operations  0.73 us (1%)
    ppermute x12, waiting for transfers between devices, on_line(): send = lambda value, pairs: lax.ppermute(value, 'expert', pairs)  20.3 us
    ppermute x12, starting transfers between devices, on_line(): send = lambda value, pairs: lax.ppermute(value, 'expert', pairs)  14.9 us
    ppermute x4, waiting for transfers between devices, on_line(): send_dp = lambda value, pairs: lax.ppermute(value, 'dp', pairs)  11.3 us
    pallas_call x2, Pallas kernels, run_arm(): pl.pallas_call(functools.partial(arm_kernel, blocks, len(outs)), in_specs...  6.87 us
    ppermute x4, starting transfers between devices, on_line(): send_dp = lambda value, pairs: lax.ppermute(value, 'dp', pairs)  6.15 us
    unnamed x16, local copies, waits for them, and re-layouts  4.93 us
  transfers between devices with their start and end apart: 16, of which 9 were waited for; matrix products, arithmetic and copies ran while one was open for 2% of the time, Pallas kernels for 4%

profile of v4, /device:TPU:0, one launch (start us, length us, event | category | flops | bytes accessed | tf_op | source)
XLA Modules:
  0.0 67.6 jit_solution(16575739825642611688)
XLA Ops:
  0.6 0.7 copy-done.2
  1.3 0.9 %copy-done = bf16[128,512]{1,0:T(8,128)(2,1)S(1)} copy-done((bf16[128,512]{1,0:T(8,128)(2,1)S(1)}, bf16[128,512]{1,0:T(8,128)(2,1)}, u32[]{:S(2)}) %copy-start) | copy-done | bytes 131096
  2.2 0.9 %copy-done.1 = bf16[128,512]{1,0:T(8,128)(2,1)S(1)} copy-done((bf16[128,512]{1,0:T(8,128)(2,1)S(1)}, bf16[128,512]{1,0:T(8,128)(2,1)}, u32[]{:S(2)}) %copy-start.1) | copy-done | bytes 131096
  3.1 3.1 %collective-permute-start.2 = (bf16[272,512]{1,0:T(8,128)(2,1)S(1)}, bf16[272,512]{1,0:T(8,128)(2,1)S(1)}, u32[]{:S(2)}, u32[]{:S(2)}) collective-permute-start(bf16[272,512]{1,0:T(8,128)(2,1)S(1)} %pack.1.refs_0_), channel_id=1, source_target_pairs={{0,2},{1,3},{2,0},{3,1},{4,6},{5,7},{6,4},{7,5},{8,10},{9,11},{10,... | collective-permute-start | bytes 835592 | tf_op jit(solution)/shard_map/ppermute | solution.py:326
  6.2 2.5 %collective-permute-start = (bf16[272,512]{1,0:T(8,128)(2,1)S(1)}, bf16[272,512]{1,0:T(8,128)(2,1)S(1)}, u32[]{:S(2)}, u32[]{:S(2)}) collective-permute-start(bf16[272,512]{1,0:T(8,128)(2,1)S(1)} %pack.1.refs_0_), channel_id=1, source_target_pairs={{0,6},{1,7},{6,0},{7,1},{2,4},{3,5},{4,2},{5,3},{8,14},{9,15},{14,... | collective-permute-start | bytes 835592 | tf_op jit(solution)/shard_map/ppermute | solution.py:326
  8.7 0.0 collective-permute-start.3
  8.7 4.6 %collective-permute-done.2.refs_1_ = bf16[272,512]{1,0:T(8,128)(2,1)S(1)} collective-permute-done((bf16[272,512]{1,0:T(8,128)(2,1)S(1)}, bf16[272,512]{1,0:T(8,128)(2,1)S(1)}, u32[]{:S(2)}, u32[]{:S(2)}) %collective-permute-start.2) | collective-permute-done | bytes 278560 | tf_op jit(solution)/shard_map/ppermute | solution.py:326
  13.3 0.0 collective-permute-start.4
  13.3 7.9 %collective-permute-done.refs_0_ = bf16[272,512]{1,0:T(8,128)(2,1)S(1)} collective-permute-done((bf16[272,512]{1,0:T(8,128)(2,1)S(1)}, bf16[272,512]{1,0:T(8,128)(2,1)S(1)}, u32[]{:S(2)}, u32[]{:S(2)}) %collective-permute-start) | collective-permute-done | bytes 278560 | tf_op jit(solution)/shard_map/ppermute | solution.py:326
  21.2 1.8 %collective-permute-start.1 = (bf16[272,512]{1,0:T(8,128)(2,1)S(1)}, bf16[272,512]{1,0:T(8,128)(2,1)S(1)}, u32[]{:S(2)}, u32[]{:S(2)}) collective-permute-start(bf16[272,512]{1,0:T(8,128)(2,1)S(1)} %broadcast_select_fusion), channel_id=1, source_target_pairs={{0,4},{1,5},{4,6},{5,7},{6,2},{7,3},{2,0},{3,1},{8,12},{9,13},{12,... | collective-permute-start | bytes 835592 | tf_op jit(solution)/shard_map/ppermute | solution.py:326
  23.0 0.0 collective-permute-start.7
  23.0 0.0 collective-permute-done.3.refs_2_
  23.0 0.0 collective-permute-done.4.refs_3_
  23.0 0.0 copy-start.4
  23.0 1.2 %copy-done.4 = bf16[1,512,1024]{2,1,0:T(8,128)(2,1)S(1)} copy-done((bf16[1,512,1024]{2,1,0:T(8,128)(2,1)S(1)}, bf16[1,512,1024]{2,1,0:T(8,128)(2,1)}, u32[]{:S(2)}) %copy-start.4) | copy-done | bytes 1048600
  24.3 1.2 %copy-done.6 = bf16[1,1024,512]{2,1,0:T(8,128)(2,1)S(1)} copy-done((bf16[1,1024,512]{2,1,0:T(8,128)(2,1)S(1)}, bf16[1,1024,512]{2,1,0:T(8,128)(2,1)}, u32[]{:S(2)}) %copy-start.6) | copy-done | bytes 1048600
  25.5 2.6 %arm_early.1 = (bf16[2,2,128,512]{3,2,1,0:T(8,128)(2,1)S(1)}, bf16[2,2,128,512]{3,2,1,0:T(8,128)(2,1)S(1)}, bf16[256,512]{1,0:T(8,128)(2,1)S(1)}, bf16[256,512]{...) custom-call(bf16[272,512]{1,0:T(8,128)(2,1)S(1)} %pack.1.refs_0_, ...), custom_call_target="tpu_custom_call" | custom-call | flops 1610612736 | bytes 12582912 | tf_op jit(solution)/shard_map/arm_early/pallas_call | solution.py:276
  28.1 0.6 collective-permute-done.1.refs_1_
  28.7 0.0 collective-permute-start.8
  28.7 0.0 collective-permute-done.7.refs_2_
  28.7 1.6 %collective-permute-done.8.refs_3_ = bf16[272,512]{1,0:T(8,128)(2,1)S(1)} collective-permute-done((bf16[272,512]{1,0:T(8,128)(2,1)S(1)}, bf16[272,512]{1,0:T(8,128)(2,1)S(1)}, u32[]{:S(2)}, u32[]{:S(2)}) %collective-permute-start.8) | collective-permute-done | bytes 278560 | tf_op jit(solution)/shard_map/ppermute | solution.py:326
  30.3 4.2 %arm_late.1 = (bf16[2,2,128,512]{3,2,1,0:T(8,128)(2,1)S(1)}, bf16[2,2,128,512]{3,2,1,0:T(8,128)(2,1)S(1)}, bf16[2,3,256,256]{3,2,1,0:T(8,128)(2,1)S(1)}, bf16[2,...) custom-call(bf16[272,512]{1,0:T(8,128)(2,1)S(1)} %collective-permute, ...), custom_call_target="tpu_custom_call" | custom-call | flops 3221225472 | bytes 12582912 | tf_op jit(solution)/shard_map/arm_late/pallas_call | solution.py:276
  34.5 0.2 collective-permute-start.9
  34.7 0.4 collective-permute-start.5
  35.1 1.5 %collective-permute-start.14 = (bf16[2,3,256,256]{3,2,1,0:T(8,128)(2,1)S(1)}, bf16[2,3,256,256]{3,2,1,0:T(8,128)(2,1)S(1)}, u32[]{:S(2)}, u32[]{:S(2)}) collective-permute-start(bf16[2,3,256,256]{3,2,1,0:T(8,128)(2,1)S(1)} %get-tuple-element.40), channel_id=1, source_target_pairs={{0,16},{8,24},{16,0},{24,8},{1,17},{9,25},{17,1},{25,9},{2,18},{10... | collective-permute-start | bytes 2359304 | tf_op jit(solution)/shard_map/ppermute | solution.py:327
  36.6 1.5 %collective-permute-start.12 = (bf16[2,3,256,256]{3,2,1,0:T(8,128)(2,1)S(1)}, bf16[2,3,256,256]{3,2,1,0:T(8,128)(2,1)S(1)}, u32[]{:S(2)}, u32[]{:S(2)}) collective-permute-start(bf16[2,3,256,256]{3,2,1,0:T(8,128)(2,1)S(1)} %get-tuple-element.37), channel_id=1, source_target_pairs={{0,8},{8,0},{16,24},{24,16},{1,9},{9,1},{17,25},{25,17},{2,10},{10... | collective-permute-start | bytes 2359304 | tf_op jit(solution)/shard_map/ppermute | solution.py:327
  38.1 0.0 collective-permute-done.9
  38.1 0.1 fusion.8
  38.2 2.0 %collective-permute-start.10 = (bf16[2,128,512]{2,1,0:T(8,128)(2,1)S(1)}, bf16[2,128,512]{2,1,0:T(8,128)(2,1)S(1)}, u32[]{:S(2)}, u32[]{:S(2)}) collective-permute-start(bf16[2,128,512]{2,1,0:T(8,128)(2,1)S(1)} %fusion.8), channel_id=1, source_target_pairs={{4,0},{5,1},{6,4},{7,5},{2,6},{3,7},{0,2},{1,3},{12,8},{13,9},{14,... | collective-permute-start | bytes 786440 | tf_op jit(solution)/shard_map/ppermute | solution.py:326
  40.1 0.0 collective-permute-done.5
  40.1 0.1 fusion.7
  40.2 1.8 %collective-permute-start.6 = (bf16[2,128,512]{2,1,0:T(8,128)(2,1)S(1)}, bf16[2,128,512]{2,1,0:T(8,128)(2,1)S(1)}, u32[]{:S(2)}, u32[]{:S(2)}) collective-permute-start(bf16[2,128,512]{2,1,0:T(8,128)(2,1)S(1)} %fusion.7), channel_id=1, source_target_pairs={{0,2},{1,3},{2,0},{3,1},{4,6},{5,7},{6,4},{7,5},{8,10},{9,11},{10,... | collective-permute-start | bytes 786440 | tf_op jit(solution)/shard_map/ppermute | solution.py:326
  42.0 5.0 %collective-permute-done.10 = bf16[2,128,512]{2,1,0:T(8,128)(2,1)S(1)} collective-permute-done((bf16[2,128,512]{2,1,0:T(8,128)(2,1)S(1)}, bf16[2,128,512]{2,1,0:T(8,128)(2,1)S(1)}, u32[]{:S(2)}, u32[]{:S(2)}) %collective-permute-start.10) | collective-permute-done | bytes 262176 | tf_op jit(solution)/shard_map/ppermute | solution.py:326
  47.0 0.1 fusion.3
  47.1 3.2 %collective-permute-start.11 = (bf16[2,128,512]{2,1,0:T(8,128)(2,1)S(1)}, bf16[2,128,512]{2,1,0:T(8,128)(2,1)S(1)}, u32[]{:S(2)}, u32[]{:S(2)}) collective-permute-start(bf16[2,128,512]{2,1,0:T(8,128)(2,1)S(1)} %fusion.3), channel_id=1, source_target_pairs={{0,6},{1,7},{6,0},{7,1},{2,4},{3,5},{4,2},{5,3},{8,14},{9,15},{14,... | collective-permute-start | bytes 786440 | tf_op jit(solution)/shard_map/ppermute | solution.py:326
  50.3 4.4 %collective-permute-done.14.refs_4_ = bf16[2,3,256,256]{3,2,1,0:T(8,128)(2,1)S(1)} collective-permute-done((bf16[2,3,256,256]{3,2,1,0:T(8,128)(2,1)S(1)}, bf16[2,3,256,256]{3,2,1,0:T(8,128)(2,1)S(1)}, u32[]{:S(2)}, u32[]{:S(2)}) %collective-permute-start.14) | collective-permute-done | bytes 786464 | tf_op jit(solution)/shard_map/ppermute | solution.py:327
  54.7 0.1 fusion
  54.8 1.6 %collective-permute-start.15 = (bf16[3,256,256]{2,1,0:T(8,128)(2,1)S(1)}, bf16[3,256,256]{2,1,0:T(8,128)(2,1)S(1)}, u32[]{:S(2)}, u32[]{:S(2)}) collective-permute-start(bf16[3,256,256]{2,1,0:T(8,128)(2,1)S(1)} %fusion), channel_id=1, source_target_pairs={{0,8},{8,0},{16,24},{24,16},{1,9},{9,1},{17,25},{25,17},{2,10},{10... | collective-permute-start | bytes 1179656 | tf_op jit(solution)/shard_map/ppermute | solution.py:327
  56.3 0.0 collective-permute-done.12.refs_1_
  56.3 0.1 fusion.1
  56.4 1.6 %collective-permute-start.13 = (bf16[3,256,256]{2,1,0:T(8,128)(2,1)S(1)}, bf16[3,256,256]{2,1,0:T(8,128)(2,1)S(1)}, u32[]{:S(2)}, u32[]{:S(2)}) collective-permute-start(bf16[3,256,256]{2,1,0:T(8,128)(2,1)S(1)} %fusion.1), channel_id=1, source_target_pairs={{0,16},{8,24},{16,0},{24,8},{1,17},{9,25},{17,1},{25,9},{2,18},{10... | collective-permute-start | bytes 1179656 | tf_op jit(solution)/shard_map/ppermute | solution.py:327
  58.0 0.0 collective-permute-done.6
  58.0 0.7 %collective-permute-done.11 = bf16[2,128,512]{2,1,0:T(8,128)(2,1)S(1)} collective-permute-done((bf16[2,128,512]{2,1,0:T(8,128)(2,1)S(1)}, bf16[2,128,512]{2,1,0:T(8,128)(2,1)S(1)}, u32[]{:S(2)}, u32[]{:S(2)}) %collective-permute-start.11) | collective-permute-done | bytes 262176 | tf_op jit(solution)/shard_map/ppermute | solution.py:326
  58.7 0.2 fusion.5
  58.9 0.7 %slice_bitcast_fusion.2 = (bf16[128,512]{1,0:T(8,128)(2,1)}, bf16[128,512]{1,0:T(8,128)(2,1)}) fusion(bf16[2,128,512]{2,1,0:T(8,128)(2,1)S(1)} %fusion.5), kind=kLoop, calls=%fused_computation.19 | loop fusion | bytes 524288 | tf_op jit(solution)/shard_map/convert_element_type | solution.py:357
  59.6 5.5 %collective-permute-done.15.refs_5_ = bf16[3,256,256]{2,1,0:T(8,128)(2,1)S(1)} collective-permute-done((bf16[3,256,256]{2,1,0:T(8,128)(2,1)S(1)}, bf16[3,256,256]{2,1,0:T(8,128)(2,1)S(1)}, u32[]{:S(2)}, u32[]{:S(2)}) %collective-permute-start.15) | collective-permute-done | bytes 393248 | tf_op jit(solution)/shard_map/ppermute | solution.py:327
  65.2 1.4 %collective-permute-done.13.refs_2_ = bf16[3,256,256]{2,1,0:T(8,128)(2,1)S(1)} collective-permute-done((bf16[3,256,256]{2,1,0:T(8,128)(2,1)S(1)}, bf16[3,256,256]{2,1,0:T(8,128)(2,1)S(1)}, u32[]{:S(2)}, u32[]{:S(2)}) %collective-permute-start.13) | collective-permute-done | bytes 393248 | tf_op jit(solution)/shard_map/ppermute | solution.py:327
  66.5 1.1 %finish.1 = (bf16[512,256]{1,0:T(8,128)(2,1)}, bf16[512,256]{1,0:T(8,128)(2,1)}, bf16[256,512]{1,0:T(8,128)(2,1)}) custom-call(bf16[3,256,256]{2,1,0:T(8,128)(2,1)S(1)} %get-tuple-element.36.refs_0_, bf16[2,3,256,256]{3,2,1,0:T(8,128)(2,1)S(1)} %collective-permute-done.12.refs_1_, bf16[3,256,256]{2,1,0:T(8,128)(2,1)S(1)} %collective-permute-done.13.refs_2_, ...), custom_call_target="tpu_custom_call" | custom-call | tf_op jit(solution)/shard_map/finish/pallas_call | solution.py:296
  (12 shorter events, 0.1 us)
Async XLA Ops:
  0.6 0.7 %copy-start.2 = (s32[128,2]{0,1:T(2,128)S(1)}, s32[128,2]{0,1:T(2,128)}, u32[]{:S(2)}) copy-start(s32[128,2]{0,1:T(2,128)} %param.7) | copy-start | bytes 3076
  1.3 0.9 %copy-start = (bf16[128,512]{1,0:T(8,128)(2,1)S(1)}, bf16[128,512]{1,0:T(8,128)(2,1)}, u32[]{:S(2)}) copy-start(bf16[128,512]{1,0:T(8,128)(2,1)} %tokens_ref.1) | copy-start | bytes 393220
  2.2 0.9 %copy-start.1 = (bf16[128,512]{1,0:T(8,128)(2,1)S(1)}, bf16[128,512]{1,0:T(8,128)(2,1)}, u32[]{:S(2)}) copy-start(bf16[128,512]{1,0:T(8,128)(2,1)} %cot_ref.1) | copy-start | bytes 393220
  3.1 19.9 %copy-start.3 = (bf16[1,512,1024]{2,1,0:T(8,128)(2,1)S(1)}, bf16[1,512,1024]{2,1,0:T(8,128)(2,1)}, u32[]{:S(2)}) copy-start(bf16[1,512,1024]{2,1,0:T(8,128)(2,1)} %param.9) | copy-start | bytes 3145732
  3.1 10.2 %collective-permute-start.2 = (bf16[272,512]{1,0:T(8,128)(2,1)S(1)}, bf16[272,512]{1,0:T(8,128)(2,1)S(1)}, u32[]{:S(2)}, u32[]{:S(2)}) collective-permute-start(bf16[272,512]{1,0:T(8,128)(2,1)S(1)} %pack.1.refs_0_), channel_id=1, source_target_pairs={{0,2},{1,3},{2,0},{3,1},{4,6},{5,7},{6,4},{7,5},{8,10},{9,11},{10,... | collective-permute-start | bytes 835592 | tf_op jit(solution)/shard_map/ppermute | solution.py:326
  6.2 14.9 %collective-permute-start = (bf16[272,512]{1,0:T(8,128)(2,1)S(1)}, bf16[272,512]{1,0:T(8,128)(2,1)S(1)}, u32[]{:S(2)}, u32[]{:S(2)}) collective-permute-start(bf16[272,512]{1,0:T(8,128)(2,1)S(1)} %pack.1.refs_0_), channel_id=1, source_target_pairs={{0,6},{1,7},{6,0},{7,1},{2,4},{3,5},{4,2},{5,3},{8,14},{9,15},{14,... | collective-permute-start | bytes 835592 | tf_op jit(solution)/shard_map/ppermute | solution.py:326
  8.7 14.3 %collective-permute-start.3 = (bf16[272,512]{1,0:T(8,128)(2,1)S(1)}, bf16[272,512]{1,0:T(8,128)(2,1)S(1)}, u32[]{:S(2)}, u32[]{:S(2)}) collective-permute-start(bf16[272,512]{1,0:T(8,128)(2,1)S(1)} %pack.1.refs_0_), channel_id=1, source_target_pairs={{0,1},{1,0},{2,3},{3,2},{4,5},{5,4},{6,7},{7,6},{8,9},{9,8},{10,11... | collective-permute-start | bytes 835592 | tf_op jit(solution)/shard_map/ppermute | solution.py:326
  13.3 9.7 %collective-permute-start.4 = (bf16[272,512]{1,0:T(8,128)(2,1)S(1)}, bf16[272,512]{1,0:T(8,128)(2,1)S(1)}, u32[]{:S(2)}, u32[]{:S(2)}) collective-permute-start(bf16[272,512]{1,0:T(8,128)(2,1)S(1)} %collective-permute-done.2.refs_1_), channel_id=1, source_target_pairs={{0,1},{1,0},{2,3},{3,2},{4,5},{5,4},{6,7},{7,6},{8,9},{9,8},{10,11... | collective-permute-start | bytes 835592 | tf_op jit(solution)/shard_map/ppermute | solution.py:326
  21.2 7.5 %collective-permute-start.1 = (bf16[272,512]{1,0:T(8,128)(2,1)S(1)}, bf16[272,512]{1,0:T(8,128)(2,1)S(1)}, u32[]{:S(2)}, u32[]{:S(2)}) collective-permute-start(bf16[272,512]{1,0:T(8,128)(2,1)S(1)} %broadcast_select_fusion), channel_id=1, source_target_pairs={{0,4},{1,5},{4,6},{5,7},{6,2},{7,3},{2,0},{3,1},{8,12},{9,13},{12,... | collective-permute-start | bytes 835592 | tf_op jit(solution)/shard_map/ppermute | solution.py:326
  23.0 5.7 %collective-permute-start.7 = (bf16[272,512]{1,0:T(8,128)(2,1)S(1)}, bf16[272,512]{1,0:T(8,128)(2,1)S(1)}, u32[]{:S(2)}, u32[]{:S(2)}) collective-permute-start(bf16[272,512]{1,0:T(8,128)(2,1)S(1)} %collective-permute-done.refs_0_), channel_id=1, source_target_pairs={{0,1},{1,0},{2,3},{3,2},{4,5},{5,4},{6,7},{7,6},{8,9},{9,8},{10,11... | collective-permute-start | bytes 835592 | tf_op jit(solution)/shard_map/ppermute | solution.py:326
  23.0 1.2 %copy-start.4 = (bf16[1,512,1024]{2,1,0:T(8,128)(2,1)S(1)}, bf16[1,512,1024]{2,1,0:T(8,128)(2,1)}, u32[]{:S(2)}) copy-start(bf16[1,512,1024]{2,1,0:T(8,128)(2,1)} %param.10) | copy-start | bytes 3145732
  24.3 1.2 %copy-start.6 = (bf16[1,1024,512]{2,1,0:T(8,128)(2,1)S(1)}, bf16[1,1024,512]{2,1,0:T(8,128)(2,1)}, u32[]{:S(2)}) copy-start(bf16[1,1024,512]{2,1,0:T(8,128)(2,1)} %param.11) | copy-start | bytes 3145732
  25.5 4.8 %copy-start.5 = (bf16[1,512,1024]{2,1,0:T(8,128)(2,1)S(1)}, bf16[1,512,1024]{2,1,0:T(8,128)(2,1)}, u32[]{:S(2)}) copy-start(bf16[1,512,1024]{2,1,0:T(8,128)(2,1)} %param.10) | copy-start | bytes 3145732
  25.5 4.8 %copy-start.7 = (bf16[1,1024,512]{2,1,0:T(8,128)(2,1)S(1)}, bf16[1,1024,512]{2,1,0:T(8,128)(2,1)}, u32[]{:S(2)}) copy-start(bf16[1,1024,512]{2,1,0:T(8,128)(2,1)} %param.11) | copy-start | bytes 3145732
  28.7 1.6 %collective-permute-start.8 = (bf16[272,512]{1,0:T(8,128)(2,1)S(1)}, bf16[272,512]{1,0:T(8,128)(2,1)S(1)}, u32[]{:S(2)}, u32[]{:S(2)}) collective-permute-start(bf16[272,512]{1,0:T(8,128)(2,1)S(1)} %collective-permute-done.1.refs_1_), channel_id=1, source_target_pairs={{0,1},{1,0},{2,3},{3,2},{4,5},{5,4},{6,7},{7,6},{8,9},{9,8},{10,11... | collective-permute-start | bytes 835592 | tf_op jit(solution)/shard_map/ppermute | solution.py:326
  34.5 3.6 %collective-permute-start.9 = (bf16[2,2,128,512]{3,2,1,0:T(8,128)(2,1)S(1)}, bf16[2,2,128,512]{3,2,1,0:T(8,128)(2,1)S(1)}, u32[]{:S(2)}, u32[]{:S(2)}) collective-permute-start(bf16[2,2,128,512]{3,2,1,0:T(8,128)(2,1)S(1)} %get-tuple-element.35), channel_id=1, source_target_pairs={{0,1},{1,0},{2,3},{3,2},{4,5},{5,4},{6,7},{7,6},{8,9},{9,8},{10,11... | collective-permute-start | bytes 1572872 | tf_op jit(solution)/shard_map/ppermute | solution.py:326
  34.7 5.4 %collective-permute-start.5 = (bf16[2,2,128,512]{3,2,1,0:T(8,128)(2,1)S(1)}, bf16[2,2,128,512]{3,2,1,0:T(8,128)(2,1)S(1)}, u32[]{:S(2)}, u32[]{:S(2)}) collective-permute-start(bf16[2,2,128,512]{3,2,1,0:T(8,128)(2,1)S(1)} %get-tuple-element.27), channel_id=1, source_target_pairs={{0,1},{1,0},{2,3},{3,2},{4,5},{5,4},{6,7},{7,6},{8,9},{9,8},{10,11... | collective-permute-start | bytes 1572872 | tf_op jit(solution)/shard_map/ppermute | solution.py:326
  35.1 19.6 %collective-permute-start.14 = (bf16[2,3,256,256]{3,2,1,0:T(8,128)(2,1)S(1)}, bf16[2,3,256,256]{3,2,1,0:T(8,128)(2,1)S(1)}, u32[]{:S(2)}, u32[]{:S(2)}) collective-permute-start(bf16[2,3,256,256]{3,2,1,0:T(8,128)(2,1)S(1)} %get-tuple-element.40), channel_id=1, source_target_pairs={{0,16},{8,24},{16,0},{24,8},{1,17},{9,25},{17,1},{25,9},{2,18},{10... | collective-permute-start | bytes 2359304 | tf_op jit(solution)/shard_map/ppermute | solution.py:327
  36.6 19.7 %collective-permute-start.12 = (bf16[2,3,256,256]{3,2,1,0:T(8,128)(2,1)S(1)}, bf16[2,3,256,256]{3,2,1,0:T(8,128)(2,1)S(1)}, u32[]{:S(2)}, u32[]{:S(2)}) collective-permute-start(bf16[2,3,256,256]{3,2,1,0:T(8,128)(2,1)S(1)} %get-tuple-element.37), channel_id=1, source_target_pairs={{0,8},{8,0},{16,24},{24,16},{1,9},{9,1},{17,25},{25,17},{2,10},{10... | collective-permute-start | bytes 2359304 | tf_op jit(solution)/shard_map/ppermute | solution.py:327
  38.2 8.8 %collective-permute-start.10 = (bf16[2,128,512]{2,1,0:T(8,128)(2,1)S(1)}, bf16[2,128,512]{2,1,0:T(8,128)(2,1)S(1)}, u32[]{:S(2)}, u32[]{:S(2)}) collective-permute-start(bf16[2,128,512]{2,1,0:T(8,128)(2,1)S(1)} %fusion.8), channel_id=1, source_target_pairs={{4,0},{5,1},{6,4},{7,5},{2,6},{3,7},{0,2},{1,3},{12,8},{13,9},{14,... | collective-permute-start | bytes 786440 | tf_op jit(solution)/shard_map/ppermute | solution.py:326
  40.2 17.8 %collective-permute-start.6 = (bf16[2,128,512]{2,1,0:T(8,128)(2,1)S(1)}, bf16[2,128,512]{2,1,0:T(8,128)(2,1)S(1)}, u32[]{:S(2)}, u32[]{:S(2)}) collective-permute-start(bf16[2,128,512]{2,1,0:T(8,128)(2,1)S(1)} %fusion.7), channel_id=1, source_target_pairs={{0,2},{1,3},{2,0},{3,1},{4,6},{5,7},{6,4},{7,5},{8,10},{9,11},{10,... | collective-permute-start | bytes 786440 | tf_op jit(solution)/shard_map/ppermute | solution.py:326
  47.1 11.6 %collective-permute-start.11 = (bf16[2,128,512]{2,1,0:T(8,128)(2,1)S(1)}, bf16[2,128,512]{2,1,0:T(8,128)(2,1)S(1)}, u32[]{:S(2)}, u32[]{:S(2)}) collective-permute-start(bf16[2,128,512]{2,1,0:T(8,128)(2,1)S(1)} %fusion.3), channel_id=1, source_target_pairs={{0,6},{1,7},{6,0},{7,1},{2,4},{3,5},{4,2},{5,3},{8,14},{9,15},{14,... | collective-permute-start | bytes 786440 | tf_op jit(solution)/shard_map/ppermute | solution.py:326
  54.8 10.4 %collective-permute-start.15 = (bf16[3,256,256]{2,1,0:T(8,128)(2,1)S(1)}, bf16[3,256,256]{2,1,0:T(8,128)(2,1)S(1)}, u32[]{:S(2)}, u32[]{:S(2)}) collective-permute-start(bf16[3,256,256]{2,1,0:T(8,128)(2,1)S(1)} %fusion), channel_id=1, source_target_pairs={{0,8},{8,0},{16,24},{24,16},{1,9},{9,1},{17,25},{25,17},{2,10},{10... | collective-permute-start | bytes 1179656 | tf_op jit(solution)/shard_map/ppermute | solution.py:327
  56.4 10.1 %collective-permute-start.13 = (bf16[3,256,256]{2,1,0:T(8,128)(2,1)S(1)}, bf16[3,256,256]{2,1,0:T(8,128)(2,1)S(1)}, u32[]{:S(2)}, u32[]{:S(2)}) collective-permute-start(bf16[3,256,256]{2,1,0:T(8,128)(2,1)S(1)} %fusion.1), channel_id=1, source_target_pairs={{0,16},{8,24},{16,0},{24,8},{1,17},{9,25},{17,1},{25,9},{2,18},{10... | collective-permute-start | bytes 1179656 | tf_op jit(solution)/shard_map/ppermute | solution.py:327

commit v5 on v4

--- a/solution.py
+++ b/solution.py
@@ -166,7 +166,7 @@
 def arm_kernel(blocks, outs_count, *refs):
     held, refs = refs[:blocks], refs[blocks:]
     (gate_ref, up_ref, down_ref), refs = refs[:3], refs[3:]
-    saved, refs = (refs[:5], refs[5:]) if outs_count == 8 else ((), refs)
+    saved, refs = (refs[:5], refs[5:]) if outs_count == 10 else ((), refs)
     staged, made = refs[:outs_count], refs[outs_count:]
     keep_ref, give_ref = staged[:2]
     rows, cots, hid, dgate, dup = made if saved else staged[2:]
@@ -214,14 +214,8 @@
         all_rows = jnp.concatenate([saved[0][...], rows[...]], axis=0)
         all_cots = jnp.concatenate([saved[1][...], cots[...]], axis=0)
         half = all_rows.shape[1] // 2
-        x_ref, y_ref, x_next_ref, y_next_ref, first_ref, second_ref = parts
-        plan = (
-            (3, x_ref.at[0], y_ref.at[0]),
-            (1, x_ref.at[1], x_next_ref),
-            (2, y_next_ref, y_ref.at[1]),
-            (0, first_ref, second_ref),
-        )
-        for j, first, second in plan:
+        for n, j in enumerate((3, 1, 2, 0)):
+            first, second = parts[2 * n : 2 * n + 2]
             quarter = place ^ j
             both = lambda old, new: jnp.concatenate([old[quarter], new[quarter]], axis=0)
             for k, d_pre in enumerate((both(saved[3], dgate), both(saved[4], dup))):
@@ -237,9 +231,8 @@
     gate_ref, up_ref, down_ref = refs[6:]
     half = gate_ref.shape[0] // 2
     for k in (0, 1):
-        mine, got, late = refs[3 * k : 3 * k + 3]
-        total = mine[...].astype(F32) + got[1].astype(F32) + late[...].astype(F32)
-        total = total.astype(BF16)
+        mine, got, late = (ref[...].astype(F32) for ref in refs[3 * k : 3 * k + 3])
+        total = (mine + got + late).astype(BF16)
         at = slice(k * half, (k + 1) * half)
         gate_ref[at] = total[0]
         up_ref[at] = total[1]
@@ -271,7 +264,7 @@
     one = (3, width // 2, piece)
     made = [(rows, width)] * 2 + [(pieces, rows, piece)] * 3
     outs = [(blocks // 2, 2, count, width)] * 2
-    outs += [(2,) + one] * 2 + [one] * 4 if saved else made
+    outs += [one] * 8 if saved else made
     ins = (*parts, *weights, *saved)
     return pl.pallas_call(
         functools.partial(arm_kernel, blocks, len(outs)),
@@ -342,25 +335,25 @@
     got = send(give, core)
     for_own = add(keep[0], got[0])
     for_near = add(keep[1], got[1]).astype(BF16)
-    keep, give, x_part, y_part, x_next, y_next, k0, k1 = run(
+    keep, give, d0, d1, x0, x1, y0, y1, k0, k1 = run(
         [from_far, from_skip, send(from_far, core), send(from_skip, core)], saved=saved
     )
     got = send(give, core)
     for_far = add(keep[0], got[0])
     for_skip = add(keep[1], got[1]).astype(BF16)
-    from_x, from_y = send_dp(x_part, x_pair), send_dp(y_part, y_pair)
-    from_skip = send(for_skip, skip_back).astype(F32)
+    from_x, from_y = send_dp(d0, x_pair), send_dp(d1, y_pair)
+    for_near, x0, y1 = lax.optimization_barrier((for_near, x0, y1))
+    last_x, last_y = send_dp(x0, x_pair), send_dp(y1, y_pair)
+    from_skip = send(for_skip, skip_back)
+    from_skip, from_x, from_y = lax.optimization_barrier((from_skip, from_x, from_y))
     from_near = send(for_near, near)
-    for_far = for_far + jnp.where(edge, 0.0, from_skip)
+    for_far = for_far + jnp.where(edge, 0.0, from_skip.astype(F32))
     from_far = send(for_far.astype(BF16), far)
-    result = for_own + from_near + from_far + jnp.where(edge, from_skip, 0.0)
+    y0, x1 = add(y0, from_x).astype(BF16), add(x1, from_y).astype(BF16)
+    y0, x1 = send_dp(y0, y_pair), send_dp(x1, x_pair)
+    result = for_own + from_near + from_far + jnp.where(edge, from_skip.astype(F32), 0.0)
     head_output, grad_tokens = result[0].astype(BF16), result[1].astype(BF16)
-
-    y_next = add(y_next, from_x[0]).astype(BF16)
-    x_next = add(x_next, from_y[0]).astype(BF16)
-    grads = run_finish(
-        k0, from_x, send_dp(y_next, y_pair), k1, from_y, send_dp(x_next, x_pair)
-    )
+    grads = run_finish(k0, last_x, y0, k1, last_y, x1)
     grad_gate, grad_up, grad_down = (part[None] for part in grads)
     return (head_output, grad_tokens, grad_gate, grad_up, grad_down)
 

time: 67.8 us -> 65.6 us (0.968)
  waiting for transfers between devices: 31.6 us -> 29.2 us
    ppermute x4 -> x6, waiting for transfers between devices: 11.3 us -> 7.97 us  [on_line(): send_dp = lambda value, pairs: lax.ppermute(value, 'dp', pairs)]
    ppermute x12, waiting for transfers between devices: 20.3 us -> 21.2 us  [on_line(): send = lambda value, pairs: lax.ppermute(value, 'expert', pairs)]
    ppermute x4 -> x6, starting transfers between devices: 6.15 us -> 6.6 us  [on_line(): send_dp = lambda value, pairs: lax.ppermute(value, 'dp', pairs)]
  transfers between devices with their start and end apart: 16 -> 18, of which waited for: 9 -> 9; matrix products, arithmetic and copies ran while one was open for 2% -> 2% of each run, Pallas kernels for 4% -> 4%
where the time goes in v5:
time: 65.6 us; the launch traced here: 65.4 us
  waiting for transfers between devices  29.2 us (45%)
  starting transfers between devices  21.2 us (32%)
  Pallas kernels  7.98 us (12%)
  local copies, waits for them, and re-layouts  5.65 us (9%)
  between operations  0.73 us (1%)
    ppermute x12, waiting for transfers between devices, on_line(): send = lambda value, pairs: lax.ppermute(value, 'expert', pairs)  21.2 us
    ppermute x12, starting transfers between devices, on_line(): send = lambda value, pairs: lax.ppermute(value, 'expert', pairs)  14.6 us
    ppermute x6, waiting for transfers between devices, on_line(): send_dp = lambda value, pairs: lax.ppermute(value, 'dp', pairs)  7.97 us
    pallas_call x2, Pallas kernels, run_arm(): pl.pallas_call(functools.partial(arm_kernel, blocks, len(outs)), in_specs...  6.87 us
    ppermute x6, starting transfers between devices, on_line(): send_dp = lambda value, pairs: lax.ppermute(value, 'dp', pairs)  6.6 us
    unnamed x16, local copies, waits for them, and re-layouts  4.93 us
  transfers between devices with their start and end apart: 18, of which 9 were waited for; matrix products, arithmetic and copies ran while one was open for 2% of the time, Pallas kernels for 4%

profile of v5, /device:TPU:0, one launch (start us, length us, event | category | flops | bytes accessed | tf_op | source)
XLA Modules:
  0.0 65.4 jit_solution(2432486128487117986)
XLA Ops:
  0.6 0.7 %copy-done.2 = s32[128,2]{0,1:T(2,128)S(1)} copy-done((s32[128,2]{0,1:T(2,128)S(1)}, s32[128,2]{0,1:T(2,128)}, u32[]{:S(2)}) %copy-start.2) | copy-done | bytes 1048
  1.3 0.9 %copy-done = bf16[128,512]{1,0:T(8,128)(2,1)S(1)} copy-done((bf16[128,512]{1,0:T(8,128)(2,1)S(1)}, bf16[128,512]{1,0:T(8,128)(2,1)}, u32[]{:S(2)}) %copy-start) | copy-done | bytes 131096
  2.2 0.9 %copy-done.1 = bf16[128,512]{1,0:T(8,128)(2,1)S(1)} copy-done((bf16[128,512]{1,0:T(8,128)(2,1)S(1)}, bf16[128,512]{1,0:T(8,128)(2,1)}, u32[]{:S(2)}) %copy-start.1) | copy-done | bytes 131096
  3.1 3.1 %collective-permute-start.2 = (bf16[272,512]{1,0:T(8,128)(2,1)S(1)}, bf16[272,512]{1,0:T(8,128)(2,1)S(1)}, u32[]{:S(2)}, u32[]{:S(2)}) collective-permute-start(bf16[272,512]{1,0:T(8,128)(2,1)S(1)} %pack.1.refs_0_), channel_id=1, source_target_pairs={{0,2},{1,3},{2,0},{3,1},{4,6},{5,7},{6,4},{7,5},{8,10},{9,11},{10,... | collective-permute-start | bytes 835592 | tf_op jit(solution)/shard_map/ppermute | solution.py:319
  6.2 2.5 %collective-permute-start = (bf16[272,512]{1,0:T(8,128)(2,1)S(1)}, bf16[272,512]{1,0:T(8,128)(2,1)S(1)}, u32[]{:S(2)}, u32[]{:S(2)}) collective-permute-start(bf16[272,512]{1,0:T(8,128)(2,1)S(1)} %pack.1.refs_0_), channel_id=1, source_target_pairs={{0,6},{1,7},{6,0},{7,1},{2,4},{3,5},{4,2},{5,3},{8,14},{9,15},{14,... | collective-permute-start | bytes 835592 | tf_op jit(solution)/shard_map/ppermute | solution.py:319
  8.7 0.0 collective-permute-start.3
  8.7 4.6 %collective-permute-done.2.refs_1_ = bf16[272,512]{1,0:T(8,128)(2,1)S(1)} collective-permute-done((bf16[272,512]{1,0:T(8,128)(2,1)S(1)}, bf16[272,512]{1,0:T(8,128)(2,1)S(1)}, u32[]{:S(2)}, u32[]{:S(2)}) %collective-permute-start.2) | collective-permute-done | bytes 278560 | tf_op jit(solution)/shard_map/ppermute | solution.py:319
  13.3 0.0 collective-permute-start.4
  13.3 7.9 %collective-permute-done.refs_0_ = bf16[272,512]{1,0:T(8,128)(2,1)S(1)} collective-permute-done((bf16[272,512]{1,0:T(8,128)(2,1)S(1)}, bf16[272,512]{1,0:T(8,128)(2,1)S(1)}, u32[]{:S(2)}, u32[]{:S(2)}) %collective-permute-start) | collective-permute-done | bytes 278560 | tf_op jit(solution)/shard_map/ppermute | solution.py:319
  21.2 1.8 %collective-permute-start.1 = (bf16[272,512]{1,0:T(8,128)(2,1)S(1)}, bf16[272,512]{1,0:T(8,128)(2,1)S(1)}, u32[]{:S(2)}, u32[]{:S(2)}) collective-permute-start(bf16[272,512]{1,0:T(8,128)(2,1)S(1)} %broadcast_select_fusion), channel_id=1, source_target_pairs={{0,4},{1,5},{4,6},{5,7},{6,2},{7,3},{2,0},{3,1},{8,12},{9,13},{12,... | collective-permute-start | bytes 835592 | tf_op jit(solution)/shard_map/ppermute | solution.py:319
  23.0 0.0 collective-permute-start.6
  23.0 0.0 collective-permute-done.3.refs_2_
  23.0 0.0 collective-permute-done.4.refs_3_
  23.0 0.0 copy-start.4
  23.0 1.2 %copy-done.4 = bf16[1,512,1024]{2,1,0:T(8,128)(2,1)S(1)} copy-done((bf16[1,512,1024]{2,1,0:T(8,128)(2,1)S(1)}, bf16[1,512,1024]{2,1,0:T(8,128)(2,1)}, u32[]{:S(2)}) %copy-start.4) | copy-done | bytes 1048600
  24.3 1.2 %copy-done.6 = bf16[1,1024,512]{2,1,0:T(8,128)(2,1)S(1)} copy-done((bf16[1,1024,512]{2,1,0:T(8,128)(2,1)S(1)}, bf16[1,1024,512]{2,1,0:T(8,128)(2,1)}, u32[]{:S(2)}) %copy-start.6) | copy-done | bytes 1048600
  25.5 2.6 %arm_early.1 = (bf16[2,2,128,512]{3,2,1,0:T(8,128)(2,1)S(1)}, bf16[2,2,128,512]{3,2,1,0:T(8,128)(2,1)S(1)}, bf16[256,512]{1,0:T(8,128)(2,1)S(1)}, bf16[256,512]{...) custom-call(bf16[272,512]{1,0:T(8,128)(2,1)S(1)} %pack.1.refs_0_, ...), custom_call_target="tpu_custom_call" | custom-call | flops 1610612736 | bytes 12582912 | tf_op jit(solution)/shard_map/arm_early/pallas_call | solution.py:269
  28.1 0.6 collective-permute-done.1.refs_1_
  28.7 0.0 collective-permute-start.7
  28.7 0.0 collective-permute-done.6.refs_2_
  28.7 1.6 %collective-permute-done.7.refs_3_ = bf16[272,512]{1,0:T(8,128)(2,1)S(1)} collective-permute-done((bf16[272,512]{1,0:T(8,128)(2,1)S(1)}, bf16[272,512]{1,0:T(8,128)(2,1)S(1)}, u32[]{:S(2)}, u32[]{:S(2)}) %collective-permute-start.7) | collective-permute-done | bytes 278560 | tf_op jit(solution)/shard_map/ppermute | solution.py:319
  30.3 4.2 %arm_late.1 = (bf16[2,2,128,512]{3,2,1,0:T(8,128)(2,1)S(1)}, bf16[2,2,128,512]{3,2,1,0:T(8,128)(2,1)S(1)}, bf16[3,256,256]{2,1,0:T(8,128)(2,1)S(1)}, bf16[3,256,...) custom-call(bf16[272,512]{1,0:T(8,128)(2,1)S(1)} %collective-permute, ...), custom_call_target="tpu_custom_call" | custom-call | flops 3221225472 | bytes 12582912 | tf_op jit(solution)/shard_map/arm_late/pallas_call | solution.py:269
  34.5 0.2 collective-permute-start.9
  34.7 0.4 collective-permute-start.5
  35.1 1.5 %collective-permute-start.11 = (bf16[3,256,256]{2,1,0:T(8,128)(2,1)S(1)}, bf16[3,256,256]{2,1,0:T(8,128)(2,1)S(1)}, u32[]{:S(2)}, u32[]{:S(2)}) collective-permute-start(bf16[3,256,256]{2,1,0:T(8,128)(2,1)S(1)} %get-tuple-element.47), channel_id=1, source_target_pairs={{0,8},{8,0},{16,24},{24,16},{1,9},{9,1},{17,25},{25,17},{2,10},{10... | collective-permute-start | bytes 1179656 | tf_op jit(solution)/shard_map/ppermute | solution.py:320
  36.6 1.5 %collective-permute-start.12 = (bf16[3,256,256]{2,1,0:T(8,128)(2,1)S(1)}, bf16[3,256,256]{2,1,0:T(8,128)(2,1)S(1)}, u32[]{:S(2)}, u32[]{:S(2)}) collective-permute-start(bf16[3,256,256]{2,1,0:T(8,128)(2,1)S(1)} %get-tuple-element.48), channel_id=1, source_target_pairs={{0,16},{8,24},{16,0},{24,8},{1,17},{9,25},{17,1},{25,9},{2,18},{10... | collective-permute-start | bytes 1179656 | tf_op jit(solution)/shard_map/ppermute | solution.py:320
  38.1 0.1 fusion.6
  38.2 2.0 %collective-permute-start.10 = (bf16[2,128,512]{2,1,0:T(8,128)(2,1)S(1)}, bf16[2,128,512]{2,1,0:T(8,128)(2,1)S(1)}, u32[]{:S(2)}, u32[]{:S(2)}) collective-permute-start(bf16[2,128,512]{2,1,0:T(8,128)(2,1)S(1)} %fusion.6), channel_id=1, source_target_pairs={{4,0},{5,1},{6,4},{7,5},{2,6},{3,7},{0,2},{1,3},{12,8},{13,9},{14,... | collective-permute-start | bytes 786440 | tf_op jit(solution)/shard_map/ppermute | solution.py:319
  40.1 0.1 fusion.5
  40.2 0.6 collective-permute-start.14
  40.8 0.8 %collective-permute-start.16 = (bf16[3,256,256]{2,1,0:T(8,128)(2,1)S(1)}, bf16[3,256,256]{2,1,0:T(8,128)(2,1)S(1)}, u32[]{:S(2)}, u32[]{:S(2)}) collective-permute-start(bf16[3,256,256]{2,1,0:T(8,128)(2,1)S(1)} %get-tuple-element.55), channel_id=1, source_target_pairs={{0,16},{8,24},{16,0},{24,8},{1,17},{9,25},{17,1},{25,9},{2,18},{10... | collective-permute-start | bytes 1179656 | tf_op jit(solution)/shard_map/ppermute | solution.py:320
  41.7 5.4 %collective-permute-done.11 = bf16[3,256,256]{2,1,0:T(8,128)(2,1)S(1)} collective-permute-done((bf16[3,256,256]{2,1,0:T(8,128)(2,1)S(1)}, bf16[3,256,256]{2,1,0:T(8,128)(2,1)S(1)}, u32[]{:S(2)}, u32[]{:S(2)}) %collective-permute-start.11) | collective-permute-done | bytes 393248 | tf_op jit(solution)/shard_map/ppermute | solution.py:320
  47.1 1.9 %collective-permute-start.8 = (bf16[2,128,512]{2,1,0:T(8,128)(2,1)S(1)}, bf16[2,128,512]{2,1,0:T(8,128)(2,1)S(1)}, u32[]{:S(2)}, u32[]{:S(2)}) collective-permute-start(bf16[2,128,512]{2,1,0:T(8,128)(2,1)S(1)} %fusion.5), channel_id=1, source_target_pairs={{0,2},{1,3},{2,0},{3,1},{4,6},{5,7},{6,4},{7,5},{8,10},{9,11},{10,... | collective-permute-start | bytes 786440 | tf_op jit(solution)/shard_map/ppermute | solution.py:319
  49.0 0.0 collective-permute-done.12
  49.0 0.0 collective-permute-done.10
  49.0 0.1 fusion.1
  49.1 2.8 %collective-permute-start.13 = (bf16[2,128,512]{2,1,0:T(8,128)(2,1)S(1)}, bf16[2,128,512]{2,1,0:T(8,128)(2,1)S(1)}, u32[]{:S(2)}, u32[]{:S(2)}) collective-permute-start(bf16[2,128,512]{2,1,0:T(8,128)(2,1)S(1)} %fusion.1), channel_id=1, source_target_pairs={{0,6},{1,7},{6,0},{7,1},{2,4},{3,5},{4,2},{5,3},{8,14},{9,15},{14,... | collective-permute-start | bytes 786440 | tf_op jit(solution)/shard_map/ppermute | solution.py:319
  51.9 0.1 add_convert_fusion
  52.0 0.6 collective-permute-start.17
  52.6 0.1 add_convert_fusion.1
  52.7 3.1 %collective-permute-done.8 = bf16[2,128,512]{2,1,0:T(8,128)(2,1)S(1)} collective-permute-done((bf16[2,128,512]{2,1,0:T(8,128)(2,1)S(1)}, bf16[2,128,512]{2,1,0:T(8,128)(2,1)S(1)}, u32[]{:S(2)}, u32[]{:S(2)}) %collective-permute-start.8) | collective-permute-done | bytes 262176 | tf_op jit(solution)/shard_map/ppermute | solution.py:319
  55.7 1.5 %collective-permute-start.15 = (bf16[3,256,256]{2,1,0:T(8,128)(2,1)S(1)}, bf16[3,256,256]{2,1,0:T(8,128)(2,1)S(1)}, u32[]{:S(2)}, u32[]{:S(2)}) collective-permute-start(bf16[3,256,256]{2,1,0:T(8,128)(2,1)S(1)} %add_convert_fusion.1), channel_id=1, source_target_pairs={{0,16},{8,24},{16,0},{24,8},{1,17},{9,25},{17,1},{25,9},{2,18},{10... | collective-permute-start | bytes 1179656 | tf_op jit(solution)/shard_map/ppermute | solution.py:320
  57.3 3.6 %collective-permute-done.13 = bf16[2,128,512]{2,1,0:T(8,128)(2,1)S(1)} collective-permute-done((bf16[2,128,512]{2,1,0:T(8,128)(2,1)S(1)}, bf16[2,128,512]{2,1,0:T(8,128)(2,1)S(1)}, u32[]{:S(2)}, u32[]{:S(2)}) %collective-permute-start.13) | collective-permute-done | bytes 262176 | tf_op jit(solution)/shard_map/ppermute | solution.py:319
  60.8 0.2 fusion.3
  61.0 0.7 %slice_bitcast_fusion = (bf16[128,512]{1,0:T(8,128)(2,1)}, bf16[128,512]{1,0:T(8,128)(2,1)}) fusion(bf16[2,128,512]{2,1,0:T(8,128)(2,1)S(1)} %fusion.3), kind=kLoop, calls=%fused_computation.15 | loop fusion | bytes 524288 | tf_op jit(solution)/shard_map/convert_element_type | solution.py:355
  61.7 1.4 %collective-permute-done.17.refs_5_ = bf16[3,256,256]{2,1,0:T(8,128)(2,1)S(1)} collective-permute-done((bf16[3,256,256]{2,1,0:T(8,128)(2,1)S(1)}, bf16[3,256,256]{2,1,0:T(8,128)(2,1)S(1)}, u32[]{:S(2)}, u32[]{:S(2)}) %collective-permute-start.17) | collective-permute-done | bytes 393248 | tf_op jit(solution)/shard_map/ppermute | solution.py:320
  63.1 1.2 %collective-permute-done.15.refs_2_ = bf16[3,256,256]{2,1,0:T(8,128)(2,1)S(1)} collective-permute-done((bf16[3,256,256]{2,1,0:T(8,128)(2,1)S(1)}, bf16[3,256,256]{2,1,0:T(8,128)(2,1)S(1)}, u32[]{:S(2)}, u32[]{:S(2)}) %collective-permute-start.15) | collective-permute-done | bytes 393248 | tf_op jit(solution)/shard_map/ppermute | solution.py:320
  64.3 1.1 %finish.1 = (bf16[512,256]{1,0:T(8,128)(2,1)}, bf16[512,256]{1,0:T(8,128)(2,1)}, bf16[256,512]{1,0:T(8,128)(2,1)}) custom-call(bf16[3,256,256]{2,1,0:T(8,128)(2,1)S(1)} %get-tuple-element.50.refs_0_, bf16[3,256,256]{2,1,0:T(8,128)(2,1)S(1)} %collective-permute-done.14.refs_1_, bf16[3,256,256]{2,1,0:T(8,128)(2,1)S(1)} %collective-permute-done.15.refs_2_, ...), custom_call_target="tpu_custom_call" | custom-call | tf_op jit(solution)/shard_map/finish/pallas_call | solution.py:289
  (16 shorter events, 0.1 us)
Async XLA Ops:
  0.6 0.7 %copy-start.2 = (s32[128,2]{0,1:T(2,128)S(1)}, s32[128,2]{0,1:T(2,128)}, u32[]{:S(2)}) copy-start(s32[128,2]{0,1:T(2,128)} %param.7) | copy-start | bytes 3076
  1.3 0.9 %copy-start = (bf16[128,512]{1,0:T(8,128)(2,1)S(1)}, bf16[128,512]{1,0:T(8,128)(2,1)}, u32[]{:S(2)}) copy-start(bf16[128,512]{1,0:T(8,128)(2,1)} %tokens_ref.1) | copy-start | bytes 393220
  2.2 0.9 %copy-start.1 = (bf16[128,512]{1,0:T(8,128)(2,1)S(1)}, bf16[128,512]{1,0:T(8,128)(2,1)}, u32[]{:S(2)}) copy-start(bf16[128,512]{1,0:T(8,128)(2,1)} %cot_ref.1) | copy-start | bytes 393220
  3.1 19.9 %copy-start.3 = (bf16[1,512,1024]{2,1,0:T(8,128)(2,1)S(1)}, bf16[1,512,1024]{2,1,0:T(8,128)(2,1)}, u32[]{:S(2)}) copy-start(bf16[1,512,1024]{2,1,0:T(8,128)(2,1)} %param.9) | copy-start | bytes 3145732
  3.1 10.2 %collective-permute-start.2 = (bf16[272,512]{1,0:T(8,128)(2,1)S(1)}, bf16[272,512]{1,0:T(8,128)(2,1)S(1)}, u32[]{:S(2)}, u32[]{:S(2)}) collective-permute-start(bf16[272,512]{1,0:T(8,128)(2,1)S(1)} %pack.1.refs_0_), channel_id=1, source_target_pairs={{0,2},{1,3},{2,0},{3,1},{4,6},{5,7},{6,4},{7,5},{8,10},{9,11},{10,... | collective-permute-start | bytes 835592 | tf_op jit(solution)/shard_map/ppermute | solution.py:319
  6.2 14.9 %collective-permute-start = (bf16[272,512]{1,0:T(8,128)(2,1)S(1)}, bf16[272,512]{1,0:T(8,128)(2,1)S(1)}, u32[]{:S(2)}, u32[]{:S(2)}) collective-permute-start(bf16[272,512]{1,0:T(8,128)(2,1)S(1)} %pack.1.refs_0_), channel_id=1, source_target_pairs={{0,6},{1,7},{6,0},{7,1},{2,4},{3,5},{4,2},{5,3},{8,14},{9,15},{14,... | collective-permute-start | bytes 835592 | tf_op jit(solution)/shard_map/ppermute | solution.py:319
  8.7 14.3 %collective-permute-start.3 = (bf16[272,512]{1,0:T(8,128)(2,1)S(1)}, bf16[272,512]{1,0:T(8,128)(2,1)S(1)}, u32[]{:S(2)}, u32[]{:S(2)}) collective-permute-start(bf16[272,512]{1,0:T(8,128)(2,1)S(1)} %pack.1.refs_0_), channel_id=1, source_target_pairs={{0,1},{1,0},{2,3},{3,2},{4,5},{5,4},{6,7},{7,6},{8,9},{9,8},{10,11... | collective-permute-start | bytes 835592 | tf_op jit(solution)/shard_map/ppermute | solution.py:319
  13.3 9.7 %collective-permute-start.4 = (bf16[272,512]{1,0:T(8,128)(2,1)S(1)}, bf16[272,512]{1,0:T(8,128)(2,1)S(1)}, u32[]{:S(2)}, u32[]{:S(2)}) collective-permute-start(bf16[272,512]{1,0:T(8,128)(2,1)S(1)} %collective-permute-done.2.refs_1_), channel_id=1, source_target_pairs={{0,1},{1,0},{2,3},{3,2},{4,5},{5,4},{6,7},{7,6},{8,9},{9,8},{10,11... | collective-permute-start | bytes 835592 | tf_op jit(solution)/shard_map/ppermute | solution.py:319
  21.2 7.5 %collective-permute-start.1 = (bf16[272,512]{1,0:T(8,128)(2,1)S(1)}, bf16[272,512]{1,0:T(8,128)(2,1)S(1)}, u32[]{:S(2)}, u32[]{:S(2)}) collective-permute-start(bf16[272,512]{1,0:T(8,128)(2,1)S(1)} %broadcast_select_fusion), channel_id=1, source_target_pairs={{0,4},{1,5},{4,6},{5,7},{6,2},{7,3},{2,0},{3,1},{8,12},{9,13},{12,... | collective-permute-start | bytes 835592 | tf_op jit(solution)/shard_map/ppermute | solution.py:319
  23.0 5.7 %collective-permute-start.6 = (bf16[272,512]{1,0:T(8,128)(2,1)S(1)}, bf16[272,512]{1,0:T(8,128)(2,1)S(1)}, u32[]{:S(2)}, u32[]{:S(2)}) collective-permute-start(bf16[272,512]{1,0:T(8,128)(2,1)S(1)} %collective-permute-done.refs_0_), channel_id=1, source_target_pairs={{0,1},{1,0},{2,3},{3,2},{4,5},{5,4},{6,7},{7,6},{8,9},{9,8},{10,11... | collective-permute-start | bytes 835592 | tf_op jit(solution)/shard_map/ppermute | solution.py:319
  23.0 1.2 %copy-start.4 = (bf16[1,512,1024]{2,1,0:T(8,128)(2,1)S(1)}, bf16[1,512,1024]{2,1,0:T(8,128)(2,1)}, u32[]{:S(2)}) copy-start(bf16[1,512,1024]{2,1,0:T(8,128)(2,1)} %param.10) | copy-start | bytes 3145732
  24.3 1.2 %copy-start.6 = (bf16[1,1024,512]{2,1,0:T(8,128)(2,1)S(1)}, bf16[1,1024,512]{2,1,0:T(8,128)(2,1)}, u32[]{:S(2)}) copy-start(bf16[1,1024,512]{2,1,0:T(8,128)(2,1)} %param.11) | copy-start | bytes 3145732
  25.5 4.8 %copy-start.5 = (bf16[1,512,1024]{2,1,0:T(8,128)(2,1)S(1)}, bf16[1,512,1024]{2,1,0:T(8,128)(2,1)}, u32[]{:S(2)}) copy-start(bf16[1,512,1024]{2,1,0:T(8,128)(2,1)} %param.10) | copy-start | bytes 3145732
  25.5 4.8 %copy-start.7 = (bf16[1,1024,512]{2,1,0:T(8,128)(2,1)S(1)}, bf16[1,1024,512]{2,1,0:T(8,128)(2,1)}, u32[]{:S(2)}) copy-start(bf16[1,1024,512]{2,1,0:T(8,128)(2,1)} %param.11) | copy-start | bytes 3145732
  28.7 1.6 %collective-permute-start.7 = (bf16[272,512]{1,0:T(8,128)(2,1)S(1)}, bf16[272,512]{1,0:T(8,128)(2,1)S(1)}, u32[]{:S(2)}, u32[]{:S(2)}) collective-permute-start(bf16[272,512]{1,0:T(8,128)(2,1)S(1)} %collective-permute-done.1.refs_1_), channel_id=1, source_target_pairs={{0,1},{1,0},{2,3},{3,2},{4,5},{5,4},{6,7},{7,6},{8,9},{9,8},{10,11... | collective-permute-start | bytes 835592 | tf_op jit(solution)/shard_map/ppermute | solution.py:319
  34.5 3.6 %collective-permute-start.9 = (bf16[2,2,128,512]{3,2,1,0:T(8,128)(2,1)S(1)}, bf16[2,2,128,512]{3,2,1,0:T(8,128)(2,1)S(1)}, u32[]{:S(2)}, u32[]{:S(2)}) collective-permute-start(bf16[2,2,128,512]{3,2,1,0:T(8,128)(2,1)S(1)} %get-tuple-element.46), channel_id=1, source_target_pairs={{0,1},{1,0},{2,3},{3,2},{4,5},{5,4},{6,7},{7,6},{8,9},{9,8},{10,11... | collective-permute-start | bytes 1572872 | tf_op jit(solution)/shard_map/ppermute | solution.py:319
  34.7 5.4 %collective-permute-start.5 = (bf16[2,2,128,512]{3,2,1,0:T(8,128)(2,1)S(1)}, bf16[2,2,128,512]{3,2,1,0:T(8,128)(2,1)S(1)}, u32[]{:S(2)}, u32[]{:S(2)}) collective-permute-start(bf16[2,2,128,512]{3,2,1,0:T(8,128)(2,1)S(1)} %get-tuple-element.35), channel_id=1, source_target_pairs={{0,1},{1,0},{2,3},{3,2},{4,5},{5,4},{6,7},{7,6},{8,9},{9,8},{10,11... | collective-permute-start | bytes 1572872 | tf_op jit(solution)/shard_map/ppermute | solution.py:319
  35.1 12.0 %collective-permute-start.11 = (bf16[3,256,256]{2,1,0:T(8,128)(2,1)S(1)}, bf16[3,256,256]{2,1,0:T(8,128)(2,1)S(1)}, u32[]{:S(2)}, u32[]{:S(2)}) collective-permute-start(bf16[3,256,256]{2,1,0:T(8,128)(2,1)S(1)} %get-tuple-element.47), channel_id=1, source_target_pairs={{0,8},{8,0},{16,24},{24,16},{1,9},{9,1},{17,25},{25,17},{2,10},{10... | collective-permute-start | bytes 1179656 | tf_op jit(solution)/shard_map/ppermute | solution.py:320
  36.6 12.4 %collective-permute-start.12 = (bf16[3,256,256]{2,1,0:T(8,128)(2,1)S(1)}, bf16[3,256,256]{2,1,0:T(8,128)(2,1)S(1)}, u32[]{:S(2)}, u32[]{:S(2)}) collective-permute-start(bf16[3,256,256]{2,1,0:T(8,128)(2,1)S(1)} %get-tuple-element.48), channel_id=1, source_target_pairs={{0,16},{8,24},{16,0},{24,8},{1,17},{9,25},{17,1},{25,9},{2,18},{10... | collective-permute-start | bytes 1179656 | tf_op jit(solution)/shard_map/ppermute | solution.py:320
  38.2 10.8 %collective-permute-start.10 = (bf16[2,128,512]{2,1,0:T(8,128)(2,1)S(1)}, bf16[2,128,512]{2,1,0:T(8,128)(2,1)S(1)}, u32[]{:S(2)}, u32[]{:S(2)}) collective-permute-start(bf16[2,128,512]{2,1,0:T(8,128)(2,1)S(1)} %fusion.6), channel_id=1, source_target_pairs={{4,0},{5,1},{6,4},{7,5},{2,6},{3,7},{0,2},{1,3},{12,8},{13,9},{14,... | collective-permute-start | bytes 786440 | tf_op jit(solution)/shard_map/ppermute | solution.py:319
  40.2 21.5 %collective-permute-start.14 = (bf16[3,256,256]{2,1,0:T(8,128)(2,1)S(1)}, bf16[3,256,256]{2,1,0:T(8,128)(2,1)S(1)}, u32[]{:S(2)}, u32[]{:S(2)}) collective-permute-start(bf16[3,256,256]{2,1,0:T(8,128)(2,1)S(1)} %get-tuple-element.51), channel_id=1, source_target_pairs={{0,8},{8,0},{16,24},{24,16},{1,9},{9,1},{17,25},{25,17},{2,10},{10... | collective-permute-start | bytes 1179656 | tf_op jit(solution)/shard_map/ppermute | solution.py:320
  40.8 20.9 %collective-permute-start.16 = (bf16[3,256,256]{2,1,0:T(8,128)(2,1)S(1)}, bf16[3,256,256]{2,1,0:T(8,128)(2,1)S(1)}, u32[]{:S(2)}, u32[]{:S(2)}) collective-permute-start(bf16[3,256,256]{2,1,0:T(8,128)(2,1)S(1)} %get-tuple-element.55), channel_id=1, source_target_pairs={{0,16},{8,24},{16,0},{24,8},{1,17},{9,25},{17,1},{25,9},{2,18},{10... | collective-permute-start | bytes 1179656 | tf_op jit(solution)/shard_map/ppermute | solution.py:320
  47.1 8.7 %collective-permute-start.8 = (bf16[2,128,512]{2,1,0:T(8,128)(2,1)S(1)}, bf16[2,128,512]{2,1,0:T(8,128)(2,1)S(1)}, u32[]{:S(2)}, u32[]{:S(2)}) collective-permute-start(bf16[2,128,512]{2,1,0:T(8,128)(2,1)S(1)} %fusion.5), channel_id=1, source_target_pairs={{0,2},{1,3},{2,0},{3,1},{4,6},{5,7},{6,4},{7,5},{8,10},{9,11},{10,... | collective-permute-start | bytes 786440 | tf_op jit(solution)/shard_map/ppermute | solution.py:319
  49.1 11.7 %collective-permute-start.13 = (bf16[2,128,512]{2,1,0:T(8,128)(2,1)S(1)}, bf16[2,128,512]{2,1,0:T(8,128)(2,1)S(1)}, u32[]{:S(2)}, u32[]{:S(2)}) collective-permute-start(bf16[2,128,512]{2,1,0:T(8,128)(2,1)S(1)} %fusion.1), channel_id=1, source_target_pairs={{0,6},{1,7},{6,0},{7,1},{2,4},{3,5},{4,2},{5,3},{8,14},{9,15},{14,... | collective-permute-start | bytes 786440 | tf_op jit(solution)/shard_map/ppermute | solution.py:319
  52.0 11.1 %collective-permute-start.17 = (bf16[3,256,256]{2,1,0:T(8,128)(2,1)S(1)}, bf16[3,256,256]{2,1,0:T(8,128)(2,1)S(1)}, u32[]{:S(2)}, u32[]{:S(2)}) collective-permute-start(bf16[3,256,256]{2,1,0:T(8,128)(2,1)S(1)} %add_convert_fusion), channel_id=1, source_target_pairs={{0,8},{8,0},{16,24},{24,16},{1,9},{9,1},{17,25},{25,17},{2,10},{10... | collective-permute-start | bytes 1179656 | tf_op jit(solution)/shard_map/ppermute | solution.py:320
  55.7 8.6 %collective-permute-start.15 = (bf16[3,256,256]{2,1,0:T(8,128)(2,1)S(1)}, bf16[3,256,256]{2,1,0:T(8,128)(2,1)S(1)}, u32[]{:S(2)}, u32[]{:S(2)}) collective-permute-start(bf16[3,256,256]{2,1,0:T(8,128)(2,1)S(1)} %add_convert_fusion.1), channel_id=1, source_target_pairs={{0,16},{8,24},{16,0},{24,8},{1,17},{9,25},{17,1},{25,9},{2,18},{10... | collective-permute-start | bytes 1179656 | tf_op jit(solution)/shard_map/ppermute | solution.py:320

commit v6 on v5

--- a/solution.py
+++ b/solution.py
@@ -218,10 +218,12 @@
             first, second = parts[2 * n : 2 * n + 2]
             quarter = place ^ j
             both = lambda old, new: jnp.concatenate([old[quarter], new[quarter]], axis=0)
-            for k, d_pre in enumerate((both(saved[3], dgate), both(saved[4], dup))):
-                part = mm_tn(all_rows, d_pre).astype(BF16)
-                first[k] = part[:half]
-                second[k] = part[half:]
+            d_pre = jnp.concatenate([both(saved[3], dgate), both(saved[4], dup)], axis=1)
+            part = mm_tn(all_rows, d_pre).astype(BF16)
+            for k in (0, 1):
+                at = slice(k * dgate.shape[2], (k + 1) * dgate.shape[2])
+                first[k] = part[:half, at]
+                second[k] = part[half:, at]
             part = mm_tn(both(saved[2], hid), all_cots).astype(BF16)
             first[2] = part[:, :half]
             second[2] = part[:, half:]
@@ -342,7 +344,6 @@
     for_far = add(keep[0], got[0])
     for_skip = add(keep[1], got[1]).astype(BF16)
     from_x, from_y = send_dp(d0, x_pair), send_dp(d1, y_pair)
-    for_near, x0, y1 = lax.optimization_barrier((for_near, x0, y1))
     last_x, last_y = send_dp(x0, x_pair), send_dp(y1, y_pair)
     from_skip = send(for_skip, skip_back)
     from_skip, from_x, from_y = lax.optimization_barrier((from_skip, from_x, from_y))
@@ -351,6 +352,7 @@
     from_far = send(for_far.astype(BF16), far)
     y0, x1 = add(y0, from_x).astype(BF16), add(x1, from_y).astype(BF16)
     y0, x1 = send_dp(y0, y_pair), send_dp(x1, x_pair)
+    from_far, from_near = lax.optimization_barrier((from_far, from_near))
     result = for_own + from_near + from_far + jnp.where(edge, from_skip.astype(F32), 0.0)
     head_output, grad_tokens = result[0].astype(BF16), result[1].astype(BF16)
     grads = run_finish(k0, last_x, y0, k1, last_y, x1)

time: 65.6 us -> 65.6 us (level)
  no operation moved by 1% of the time
where the time goes in v6:
time: 65.6 us; the launch traced here: 65.4 us
  waiting for transfers between devices  29.3 us (45%)
  starting transfers between devices  21.1 us (32%)
  Pallas kernels  7.98 us (12%)
  local copies, waits for them, and re-layouts  5.65 us (9%)
  between operations  0.73 us (1%)
    ppermute x12, waiting for transfers between devices, on_line(): send = lambda value, pairs: lax.ppermute(value, 'expert', pairs)  21.2 us
    ppermute x12, starting transfers between devices, on_line(): send = lambda value, pairs: lax.ppermute(value, 'expert', pairs)  14.6 us
    ppermute x6, waiting for transfers between devices, on_line(): send_dp = lambda value, pairs: lax.ppermute(value, 'dp', pairs)  8.04 us
    pallas_call x2, Pallas kernels, run_arm(): pl.pallas_call(functools.partial(arm_kernel, blocks, len(outs)), in_specs...  6.87 us
    ppermute x6, starting transfers between devices, on_line(): send_dp = lambda value, pairs: lax.ppermute(value, 'dp', pairs)  6.54 us
    unnamed x16, local copies, waits for them, and re-layouts  4.93 us
  transfers between devices with their start and end apart: 18, of which 9 were waited for; matrix products, arithmetic and copies ran while one was open for 2% of the time, Pallas kernels for 4%

profile of v6, /device:TPU:0, one launch (start us, length us, event | category | flops | bytes accessed | tf_op | source)
XLA Modules:
  0.0 65.4 jit_solution(16059319596950362667)
XLA Ops:
  0.6 0.7 %copy-done.2 = s32[128,2]{0,1:T(2,128)S(1)} copy-done((s32[128,2]{0,1:T(2,128)S(1)}, s32[128,2]{0,1:T(2,128)}, u32[]{:S(2)}) %copy-start.2) | copy-done | bytes 1048
  1.3 0.9 %copy-done = bf16[128,512]{1,0:T(8,128)(2,1)S(1)} copy-done((bf16[128,512]{1,0:T(8,128)(2,1)S(1)}, bf16[128,512]{1,0:T(8,128)(2,1)}, u32[]{:S(2)}) %copy-start) | copy-done | bytes 131096
  2.2 0.9 %copy-done.1 = bf16[128,512]{1,0:T(8,128)(2,1)S(1)} copy-done((bf16[128,512]{1,0:T(8,128)(2,1)S(1)}, bf16[128,512]{1,0:T(8,128)(2,1)}, u32[]{:S(2)}) %copy-start.1) | copy-done | bytes 131096
  3.1 3.1 %collective-permute-start.2 = (bf16[272,512]{1,0:T(8,128)(2,1)S(1)}, bf16[272,512]{1,0:T(8,128)(2,1)S(1)}, u32[]{:S(2)}, u32[]{:S(2)}) collective-permute-start(bf16[272,512]{1,0:T(8,128)(2,1)S(1)} %pack.1.refs_0_), channel_id=1, source_target_pairs={{0,2},{1,3},{2,0},{3,1},{4,6},{5,7},{6,4},{7,5},{8,10},{9,11},{10,... | collective-permute-start | bytes 835592 | tf_op jit(solution)/shard_map/ppermute | solution.py:321
  6.2 2.5 %collective-permute-start = (bf16[272,512]{1,0:T(8,128)(2,1)S(1)}, bf16[272,512]{1,0:T(8,128)(2,1)S(1)}, u32[]{:S(2)}, u32[]{:S(2)}) collective-permute-start(bf16[272,512]{1,0:T(8,128)(2,1)S(1)} %pack.1.refs_0_), channel_id=1, source_target_pairs={{0,6},{1,7},{6,0},{7,1},{2,4},{3,5},{4,2},{5,3},{8,14},{9,15},{14,... | collective-permute-start | bytes 835592 | tf_op jit(solution)/shard_map/ppermute | solution.py:321
  8.7 0.0 collective-permute-start.3
  8.7 4.6 %collective-permute-done.2.refs_1_ = bf16[272,512]{1,0:T(8,128)(2,1)S(1)} collective-permute-done((bf16[272,512]{1,0:T(8,128)(2,1)S(1)}, bf16[272,512]{1,0:T(8,128)(2,1)S(1)}, u32[]{:S(2)}, u32[]{:S(2)}) %collective-permute-start.2) | collective-permute-done | bytes 278560 | tf_op jit(solution)/shard_map/ppermute | solution.py:321
  13.3 0.0 collective-permute-start.4
  13.3 7.9 %collective-permute-done.refs_0_ = bf16[272,512]{1,0:T(8,128)(2,1)S(1)} collective-permute-done((bf16[272,512]{1,0:T(8,128)(2,1)S(1)}, bf16[272,512]{1,0:T(8,128)(2,1)S(1)}, u32[]{:S(2)}, u32[]{:S(2)}) %collective-permute-start) | collective-permute-done | bytes 278560 | tf_op jit(solution)/shard_map/ppermute | solution.py:321
  21.2 1.8 %collective-permute-start.1 = (bf16[272,512]{1,0:T(8,128)(2,1)S(1)}, bf16[272,512]{1,0:T(8,128)(2,1)S(1)}, u32[]{:S(2)}, u32[]{:S(2)}) collective-permute-start(bf16[272,512]{1,0:T(8,128)(2,1)S(1)} %broadcast_select_fusion), channel_id=1, source_target_pairs={{0,4},{1,5},{4,6},{5,7},{6,2},{7,3},{2,0},{3,1},{8,12},{9,13},{12,... | collective-permute-start | bytes 835592 | tf_op jit(solution)/shard_map/ppermute | solution.py:321
  23.0 0.0 collective-permute-start.6
  23.0 0.0 collective-permute-done.3.refs_2_
  23.0 0.0 collective-permute-done.4.refs_3_
  23.0 0.0 copy-start.4
  23.0 1.2 %copy-done.4 = bf16[1,512,1024]{2,1,0:T(8,128)(2,1)S(1)} copy-done((bf16[1,512,1024]{2,1,0:T(8,128)(2,1)S(1)}, bf16[1,512,1024]{2,1,0:T(8,128)(2,1)}, u32[]{:S(2)}) %copy-start.4) | copy-done | bytes 1048600
  24.3 1.2 %copy-done.6 = bf16[1,1024,512]{2,1,0:T(8,128)(2,1)S(1)} copy-done((bf16[1,1024,512]{2,1,0:T(8,128)(2,1)S(1)}, bf16[1,1024,512]{2,1,0:T(8,128)(2,1)}, u32[]{:S(2)}) %copy-start.6) | copy-done | bytes 1048600
  25.5 2.6 %arm_early.1 = (bf16[2,2,128,512]{3,2,1,0:T(8,128)(2,1)S(1)}, bf16[2,2,128,512]{3,2,1,0:T(8,128)(2,1)S(1)}, bf16[256,512]{1,0:T(8,128)(2,1)S(1)}, bf16[256,512]{...) custom-call(bf16[272,512]{1,0:T(8,128)(2,1)S(1)} %pack.1.refs_0_, ...), custom_call_target="tpu_custom_call" | custom-call | flops 1610612736 | bytes 12582912 | tf_op jit(solution)/shard_map/arm_early/pallas_call | solution.py:271
  28.1 0.6 collective-permute-done.1.refs_1_
  28.7 0.0 collective-permute-start.7
  28.7 0.0 collective-permute-done.6.refs_2_
  28.7 1.6 %collective-permute-done.7.refs_3_ = bf16[272,512]{1,0:T(8,128)(2,1)S(1)} collective-permute-done((bf16[272,512]{1,0:T(8,128)(2,1)S(1)}, bf16[272,512]{1,0:T(8,128)(2,1)S(1)}, u32[]{:S(2)}, u32[]{:S(2)}) %collective-permute-start.7) | collective-permute-done | bytes 278560 | tf_op jit(solution)/shard_map/ppermute | solution.py:321
  30.3 4.2 %arm_late.1 = (bf16[2,2,128,512]{3,2,1,0:T(8,128)(2,1)S(1)}, bf16[2,2,128,512]{3,2,1,0:T(8,128)(2,1)S(1)}, bf16[3,256,256]{2,1,0:T(8,128)(2,1)S(1)}, bf16[3,256,...) custom-call(bf16[272,512]{1,0:T(8,128)(2,1)S(1)} %collective-permute, ...), custom_call_target="tpu_custom_call" | custom-call | flops 3221225472 | bytes 12582912 | tf_op jit(solution)/shard_map/arm_late/pallas_call | solution.py:271
  34.5 0.2 collective-permute-start.8
  34.7 0.4 collective-permute-start.5
  35.1 1.5 %collective-permute-start.10 = (bf16[3,256,256]{2,1,0:T(8,128)(2,1)S(1)}, bf16[3,256,256]{2,1,0:T(8,128)(2,1)S(1)}, u32[]{:S(2)}, u32[]{:S(2)}) collective-permute-start(bf16[3,256,256]{2,1,0:T(8,128)(2,1)S(1)} %get-tuple-element.43), channel_id=1, source_target_pairs={{0,8},{8,0},{16,24},{24,16},{1,9},{9,1},{17,25},{25,17},{2,10},{10... | collective-permute-start | bytes 1179656 | tf_op jit(solution)/shard_map/ppermute | solution.py:322
  36.6 1.5 %collective-permute-start.11 = (bf16[3,256,256]{2,1,0:T(8,128)(2,1)S(1)}, bf16[3,256,256]{2,1,0:T(8,128)(2,1)S(1)}, u32[]{:S(2)}, u32[]{:S(2)}) collective-permute-start(bf16[3,256,256]{2,1,0:T(8,128)(2,1)S(1)} %get-tuple-element.44), channel_id=1, source_target_pairs={{0,16},{8,24},{16,0},{24,8},{1,17},{9,25},{17,1},{25,9},{2,18},{10... | collective-permute-start | bytes 1179656 | tf_op jit(solution)/shard_map/ppermute | solution.py:322
  38.1 0.1 fusion.5
  38.2 2.0 %collective-permute-start.9 = (bf16[2,128,512]{2,1,0:T(8,128)(2,1)S(1)}, bf16[2,128,512]{2,1,0:T(8,128)(2,1)S(1)}, u32[]{:S(2)}, u32[]{:S(2)}) collective-permute-start(bf16[2,128,512]{2,1,0:T(8,128)(2,1)S(1)} %fusion.5), channel_id=1, source_target_pairs={{4,0},{5,1},{6,4},{7,5},{2,6},{3,7},{0,2},{1,3},{12,8},{13,9},{14,... | collective-permute-start | bytes 786440 | tf_op jit(solution)/shard_map/ppermute | solution.py:321
  40.1 0.6 collective-permute-start.14
  40.7 0.8 %collective-permute-start.16 = (bf16[3,256,256]{2,1,0:T(8,128)(2,1)S(1)}, bf16[3,256,256]{2,1,0:T(8,128)(2,1)S(1)}, u32[]{:S(2)}, u32[]{:S(2)}) collective-permute-start(bf16[3,256,256]{2,1,0:T(8,128)(2,1)S(1)} %get-tuple-element.53), channel_id=1, source_target_pairs={{0,16},{8,24},{16,0},{24,8},{1,17},{9,25},{17,1},{25,9},{2,18},{10... | collective-permute-start | bytes 1179656 | tf_op jit(solution)/shard_map/ppermute | solution.py:322
  41.5 0.1 fusion.6
  41.6 5.5 %collective-permute-done.10 = bf16[3,256,256]{2,1,0:T(8,128)(2,1)S(1)} collective-permute-done((bf16[3,256,256]{2,1,0:T(8,128)(2,1)S(1)}, bf16[3,256,256]{2,1,0:T(8,128)(2,1)S(1)}, u32[]{:S(2)}, u32[]{:S(2)}) %collective-permute-start.10) | collective-permute-done | bytes 393248 | tf_op jit(solution)/shard_map/ppermute | solution.py:322
  47.1 1.9 %collective-permute-start.13 = (bf16[2,128,512]{2,1,0:T(8,128)(2,1)S(1)}, bf16[2,128,512]{2,1,0:T(8,128)(2,1)S(1)}, u32[]{:S(2)}, u32[]{:S(2)}) collective-permute-start(bf16[2,128,512]{2,1,0:T(8,128)(2,1)S(1)} %fusion.6), channel_id=1, source_target_pairs={{0,2},{1,3},{2,0},{3,1},{4,6},{5,7},{6,4},{7,5},{8,10},{9,11},{10,... | collective-permute-start | bytes 786440 | tf_op jit(solution)/shard_map/ppermute | solution.py:321
  49.0 0.0 collective-permute-done.11
  49.0 0.0 collective-permute-done.9
  49.0 0.1 fusion.1
  49.1 2.8 %collective-permute-start.12 = (bf16[2,128,512]{2,1,0:T(8,128)(2,1)S(1)}, bf16[2,128,512]{2,1,0:T(8,128)(2,1)S(1)}, u32[]{:S(2)}, u32[]{:S(2)}) collective-permute-start(bf16[2,128,512]{2,1,0:T(8,128)(2,1)S(1)} %fusion.1), channel_id=1, source_target_pairs={{0,6},{1,7},{6,0},{7,1},{2,4},{3,5},{4,2},{5,3},{8,14},{9,15},{14,... | collective-permute-start | bytes 786440 | tf_op jit(solution)/shard_map/ppermute | solution.py:321
  51.9 0.1 add_convert_fusion
  52.0 0.6 collective-permute-start.17
  52.6 0.1 add_convert_fusion.1
  52.7 3.1 %collective-permute-done.13 = bf16[2,128,512]{2,1,0:T(8,128)(2,1)S(1)} collective-permute-done((bf16[2,128,512]{2,1,0:T(8,128)(2,1)S(1)}, bf16[2,128,512]{2,1,0:T(8,128)(2,1)S(1)}, u32[]{:S(2)}, u32[]{:S(2)}) %collective-permute-start.13) | collective-permute-done | bytes 262176 | tf_op jit(solution)/shard_map/ppermute | solution.py:321
  55.7 1.5 %collective-permute-start.15 = (bf16[3,256,256]{2,1,0:T(8,128)(2,1)S(1)}, bf16[3,256,256]{2,1,0:T(8,128)(2,1)S(1)}, u32[]{:S(2)}, u32[]{:S(2)}) collective-permute-start(bf16[3,256,256]{2,1,0:T(8,128)(2,1)S(1)} %add_convert_fusion.1), channel_id=1, source_target_pairs={{0,16},{8,24},{16,0},{24,8},{1,17},{9,25},{17,1},{25,9},{2,18},{10... | collective-permute-start | bytes 1179656 | tf_op jit(solution)/shard_map/ppermute | solution.py:322
  57.3 3.6 %collective-permute-done.12 = bf16[2,128,512]{2,1,0:T(8,128)(2,1)S(1)} collective-permute-done((bf16[2,128,512]{2,1,0:T(8,128)(2,1)S(1)}, bf16[2,128,512]{2,1,0:T(8,128)(2,1)S(1)}, u32[]{:S(2)}, u32[]{:S(2)}) %collective-permute-start.12) | collective-permute-done | bytes 262176 | tf_op jit(solution)/shard_map/ppermute | solution.py:321
  60.8 0.2 fusion.3
  61.0 0.7 %slice_bitcast_fusion = (bf16[128,512]{1,0:T(8,128)(2,1)}, bf16[128,512]{1,0:T(8,128)(2,1)}) fusion(bf16[2,128,512]{2,1,0:T(8,128)(2,1)S(1)} %fusion.3), kind=kLoop, calls=%fused_computation.15 | loop fusion | bytes 524288 | tf_op jit(solution)/shard_map/convert_element_type | solution.py:357
  61.7 1.4 %collective-permute-done.17.refs_5_ = bf16[3,256,256]{2,1,0:T(8,128)(2,1)S(1)} collective-permute-done((bf16[3,256,256]{2,1,0:T(8,128)(2,1)S(1)}, bf16[3,256,256]{2,1,0:T(8,128)(2,1)S(1)}, u32[]{:S(2)}, u32[]{:S(2)}) %collective-permute-start.17) | collective-permute-done | bytes 393248 | tf_op jit(solution)/shard_map/ppermute | solution.py:322
  63.1 1.2 %collective-permute-done.15.refs_2_ = bf16[3,256,256]{2,1,0:T(8,128)(2,1)S(1)} collective-permute-done((bf16[3,256,256]{2,1,0:T(8,128)(2,1)S(1)}, bf16[3,256,256]{2,1,0:T(8,128)(2,1)S(1)}, u32[]{:S(2)}, u32[]{:S(2)}) %collective-permute-start.15) | collective-permute-done | bytes 393248 | tf_op jit(solution)/shard_map/ppermute | solution.py:322
  64.3 1.1 %finish.1 = (bf16[512,256]{1,0:T(8,128)(2,1)}, bf16[512,256]{1,0:T(8,128)(2,1)}, bf16[256,512]{1,0:T(8,128)(2,1)}) custom-call(bf16[3,256,256]{2,1,0:T(8,128)(2,1)S(1)} %get-tuple-element.48.refs_0_, bf16[3,256,256]{2,1,0:T(8,128)(2,1)S(1)} %collective-permute-done.14.refs_1_, bf16[3,256,256]{2,1,0:T(8,128)(2,1)S(1)} %collective-permute-done.15.refs_2_, ...), custom_call_target="tpu_custom_call" | custom-call | tf_op jit(solution)/shard_map/finish/pallas_call | solution.py:291
  (16 shorter events, 0.1 us)
Async XLA Ops:
  0.6 0.7 %copy-start.2 = (s32[128,2]{0,1:T(2,128)S(1)}, s32[128,2]{0,1:T(2,128)}, u32[]{:S(2)}) copy-start(s32[128,2]{0,1:T(2,128)} %param.7) | copy-start | bytes 3076
  1.3 0.9 %copy-start = (bf16[128,512]{1,0:T(8,128)(2,1)S(1)}, bf16[128,512]{1,0:T(8,128)(2,1)}, u32[]{:S(2)}) copy-start(bf16[128,512]{1,0:T(8,128)(2,1)} %tokens_ref.1) | copy-start | bytes 393220
  2.2 0.9 %copy-start.1 = (bf16[128,512]{1,0:T(8,128)(2,1)S(1)}, bf16[128,512]{1,0:T(8,128)(2,1)}, u32[]{:S(2)}) copy-start(bf16[128,512]{1,0:T(8,128)(2,1)} %cot_ref.1) | copy-start | bytes 393220
  3.1 19.9 %copy-start.3 = (bf16[1,512,1024]{2,1,0:T(8,128)(2,1)S(1)}, bf16[1,512,1024]{2,1,0:T(8,128)(2,1)}, u32[]{:S(2)}) copy-start(bf16[1,512,1024]{2,1,0:T(8,128)(2,1)} %param.9) | copy-start | bytes 3145732
  3.1 10.2 %collective-permute-start.2 = (bf16[272,512]{1,0:T(8,128)(2,1)S(1)}, bf16[272,512]{1,0:T(8,128)(2,1)S(1)}, u32[]{:S(2)}, u32[]{:S(2)}) collective-permute-start(bf16[272,512]{1,0:T(8,128)(2,1)S(1)} %pack.1.refs_0_), channel_id=1, source_target_pairs={{0,2},{1,3},{2,0},{3,1},{4,6},{5,7},{6,4},{7,5},{8,10},{9,11},{10,... | collective-permute-start | bytes 835592 | tf_op jit(solution)/shard_map/ppermute | solution.py:321
  6.2 14.9 %collective-permute-start = (bf16[272,512]{1,0:T(8,128)(2,1)S(1)}, bf16[272,512]{1,0:T(8,128)(2,1)S(1)}, u32[]{:S(2)}, u32[]{:S(2)}) collective-permute-start(bf16[272,512]{1,0:T(8,128)(2,1)S(1)} %pack.1.refs_0_), channel_id=1, source_target_pairs={{0,6},{1,7},{6,0},{7,1},{2,4},{3,5},{4,2},{5,3},{8,14},{9,15},{14,... | collective-permute-start | bytes 835592 | tf_op jit(solution)/shard_map/ppermute | solution.py:321
  8.7 14.3 %collective-permute-start.3 = (bf16[272,512]{1,0:T(8,128)(2,1)S(1)}, bf16[272,512]{1,0:T(8,128)(2,1)S(1)}, u32[]{:S(2)}, u32[]{:S(2)}) collective-permute-start(bf16[272,512]{1,0:T(8,128)(2,1)S(1)} %pack.1.refs_0_), channel_id=1, source_target_pairs={{0,1},{1,0},{2,3},{3,2},{4,5},{5,4},{6,7},{7,6},{8,9},{9,8},{10,11... | collective-permute-start | bytes 835592 | tf_op jit(solution)/shard_map/ppermute | solution.py:321
  13.3 9.7 %collective-permute-start.4 = (bf16[272,512]{1,0:T(8,128)(2,1)S(1)}, bf16[272,512]{1,0:T(8,128)(2,1)S(1)}, u32[]{:S(2)}, u32[]{:S(2)}) collective-permute-start(bf16[272,512]{1,0:T(8,128)(2,1)S(1)} %collective-permute-done.2.refs_1_), channel_id=1, source_target_pairs={{0,1},{1,0},{2,3},{3,2},{4,5},{5,4},{6,7},{7,6},{8,9},{9,8},{10,11... | collective-permute-start | bytes 835592 | tf_op jit(solution)/shard_map/ppermute | solution.py:321
  21.2 7.5 %collective-permute-start.1 = (bf16[272,512]{1,0:T(8,128)(2,1)S(1)}, bf16[272,512]{1,0:T(8,128)(2,1)S(1)}, u32[]{:S(2)}, u32[]{:S(2)}) collective-permute-start(bf16[272,512]{1,0:T(8,128)(2,1)S(1)} %broadcast_select_fusion), channel_id=1, source_target_pairs={{0,4},{1,5},{4,6},{5,7},{6,2},{7,3},{2,0},{3,1},{8,12},{9,13},{12,... | collective-permute-start | bytes 835592 | tf_op jit(solution)/shard_map/ppermute | solution.py:321
  23.0 5.7 %collective-permute-start.6 = (bf16[272,512]{1,0:T(8,128)(2,1)S(1)}, bf16[272,512]{1,0:T(8,128)(2,1)S(1)}, u32[]{:S(2)}, u32[]{:S(2)}) collective-permute-start(bf16[272,512]{1,0:T(8,128)(2,1)S(1)} %collective-permute-done.refs_0_), channel_id=1, source_target_pairs={{0,1},{1,0},{2,3},{3,2},{4,5},{5,4},{6,7},{7,6},{8,9},{9,8},{10,11... | collective-permute-start | bytes 835592 | tf_op jit(solution)/shard_map/ppermute | solution.py:321
  23.0 1.2 %copy-start.4 = (bf16[1,512,1024]{2,1,0:T(8,128)(2,1)S(1)}, bf16[1,512,1024]{2,1,0:T(8,128)(2,1)}, u32[]{:S(2)}) copy-start(bf16[1,512,1024]{2,1,0:T(8,128)(2,1)} %param.10) | copy-start | bytes 3145732
  24.3 1.2 %copy-start.6 = (bf16[1,1024,512]{2,1,0:T(8,128)(2,1)S(1)}, bf16[1,1024,512]{2,1,0:T(8,128)(2,1)}, u32[]{:S(2)}) copy-start(bf16[1,1024,512]{2,1,0:T(8,128)(2,1)} %param.11) | copy-start | bytes 3145732
  25.5 4.8 %copy-start.5 = (bf16[1,512,1024]{2,1,0:T(8,128)(2,1)S(1)}, bf16[1,512,1024]{2,1,0:T(8,128)(2,1)}, u32[]{:S(2)}) copy-start(bf16[1,512,1024]{2,1,0:T(8,128)(2,1)} %param.10) | copy-start | bytes 3145732
  25.5 4.8 %copy-start.7 = (bf16[1,1024,512]{2,1,0:T(8,128)(2,1)S(1)}, bf16[1,1024,512]{2,1,0:T(8,128)(2,1)}, u32[]{:S(2)}) copy-start(bf16[1,1024,512]{2,1,0:T(8,128)(2,1)} %param.11) | copy-start | bytes 3145732
  28.7 1.6 %collective-permute-start.7 = (bf16[272,512]{1,0:T(8,128)(2,1)S(1)}, bf16[272,512]{1,0:T(8,128)(2,1)S(1)}, u32[]{:S(2)}, u32[]{:S(2)}) collective-permute-start(bf16[272,512]{1,0:T(8,128)(2,1)S(1)} %collective-permute-done.1.refs_1_), channel_id=1, source_target_pairs={{0,1},{1,0},{2,3},{3,2},{4,5},{5,4},{6,7},{7,6},{8,9},{9,8},{10,11... | collective-permute-start | bytes 835592 | tf_op jit(solution)/shard_map/ppermute | solution.py:321
  34.5 3.6 %collective-permute-start.8 = (bf16[2,2,128,512]{3,2,1,0:T(8,128)(2,1)S(1)}, bf16[2,2,128,512]{3,2,1,0:T(8,128)(2,1)S(1)}, u32[]{:S(2)}, u32[]{:S(2)}) collective-permute-start(bf16[2,2,128,512]{3,2,1,0:T(8,128)(2,1)S(1)} %get-tuple-element.42), channel_id=1, source_target_pairs={{0,1},{1,0},{2,3},{3,2},{4,5},{5,4},{6,7},{7,6},{8,9},{9,8},{10,11... | collective-permute-start | bytes 1572872 | tf_op jit(solution)/shard_map/ppermute | solution.py:321
  34.7 6.0 %collective-permute-start.5 = (bf16[2,2,128,512]{3,2,1,0:T(8,128)(2,1)S(1)}, bf16[2,2,128,512]{3,2,1,0:T(8,128)(2,1)S(1)}, u32[]{:S(2)}, u32[]{:S(2)}) collective-permute-start(bf16[2,2,128,512]{3,2,1,0:T(8,128)(2,1)S(1)} %get-tuple-element.34), channel_id=1, source_target_pairs={{0,1},{1,0},{2,3},{3,2},{4,5},{5,4},{6,7},{7,6},{8,9},{9,8},{10,11... | collective-permute-start | bytes 1572872 | tf_op jit(solution)/shard_map/ppermute | solution.py:321
  35.1 12.0 %collective-permute-start.10 = (bf16[3,256,256]{2,1,0:T(8,128)(2,1)S(1)}, bf16[3,256,256]{2,1,0:T(8,128)(2,1)S(1)}, u32[]{:S(2)}, u32[]{:S(2)}) collective-permute-start(bf16[3,256,256]{2,1,0:T(8,128)(2,1)S(1)} %get-tuple-element.43), channel_id=1, source_target_pairs={{0,8},{8,0},{16,24},{24,16},{1,9},{9,1},{17,25},{25,17},{2,10},{10... | collective-permute-start | bytes 1179656 | tf_op jit(solution)/shard_map/ppermute | solution.py:322
  36.6 12.4 %collective-permute-start.11 = (bf16[3,256,256]{2,1,0:T(8,128)(2,1)S(1)}, bf16[3,256,256]{2,1,0:T(8,128)(2,1)S(1)}, u32[]{:S(2)}, u32[]{:S(2)}) collective-permute-start(bf16[3,256,256]{2,1,0:T(8,128)(2,1)S(1)} %get-tuple-element.44), channel_id=1, source_target_pairs={{0,16},{8,24},{16,0},{24,8},{1,17},{9,25},{17,1},{25,9},{2,18},{10... | collective-permute-start | bytes 1179656 | tf_op jit(solution)/shard_map/ppermute | solution.py:322
  38.2 10.8 %collective-permute-start.9 = (bf16[2,128,512]{2,1,0:T(8,128)(2,1)S(1)}, bf16[2,128,512]{2,1,0:T(8,128)(2,1)S(1)}, u32[]{:S(2)}, u32[]{:S(2)}) collective-permute-start(bf16[2,128,512]{2,1,0:T(8,128)(2,1)S(1)} %fusion.5), channel_id=1, source_target_pairs={{4,0},{5,1},{6,4},{7,5},{2,6},{3,7},{0,2},{1,3},{12,8},{13,9},{14,... | collective-permute-start | bytes 786440 | tf_op jit(solution)/shard_map/ppermute | solution.py:321
  40.1 21.6 %collective-permute-start.14 = (bf16[3,256,256]{2,1,0:T(8,128)(2,1)S(1)}, bf16[3,256,256]{2,1,0:T(8,128)(2,1)S(1)}, u32[]{:S(2)}, u32[]{:S(2)}) collective-permute-start(bf16[3,256,256]{2,1,0:T(8,128)(2,1)S(1)} %get-tuple-element.49), channel_id=1, source_target_pairs={{0,8},{8,0},{16,24},{24,16},{1,9},{9,1},{17,25},{25,17},{2,10},{10... | collective-permute-start | bytes 1179656 | tf_op jit(solution)/shard_map/ppermute | solution.py:322
  40.7 21.0 %collective-permute-start.16 = (bf16[3,256,256]{2,1,0:T(8,128)(2,1)S(1)}, bf16[3,256,256]{2,1,0:T(8,128)(2,1)S(1)}, u32[]{:S(2)}, u32[]{:S(2)}) collective-permute-start(bf16[3,256,256]{2,1,0:T(8,128)(2,1)S(1)} %get-tuple-element.53), channel_id=1, source_target_pairs={{0,16},{8,24},{16,0},{24,8},{1,17},{9,25},{17,1},{25,9},{2,18},{10... | collective-permute-start | bytes 1179656 | tf_op jit(solution)/shard_map/ppermute | solution.py:322
  47.1 8.7 %collective-permute-start.13 = (bf16[2,128,512]{2,1,0:T(8,128)(2,1)S(1)}, bf16[2,128,512]{2,1,0:T(8,128)(2,1)S(1)}, u32[]{:S(2)}, u32[]{:S(2)}) collective-permute-start(bf16[2,128,512]{2,1,0:T(8,128)(2,1)S(1)} %fusion.6), channel_id=1, source_target_pairs={{0,2},{1,3},{2,0},{3,1},{4,6},{5,7},{6,4},{7,5},{8,10},{9,11},{10,... | collective-permute-start | bytes 786440 | tf_op jit(solution)/shard_map/ppermute | solution.py:321
  49.1 11.7 %collective-permute-start.12 = (bf16[2,128,512]{2,1,0:T(8,128)(2,1)S(1)}, bf16[2,128,512]{2,1,0:T(8,128)(2,1)S(1)}, u32[]{:S(2)}, u32[]{:S(2)}) collective-permute-start(bf16[2,128,512]{2,1,0:T(8,128)(2,1)S(1)} %fusion.1), channel_id=1, source_target_pairs={{0,6},{1,7},{6,0},{7,1},{2,4},{3,5},{4,2},{5,3},{8,14},{9,15},{14,... | collective-permute-start | bytes 786440 | tf_op jit(solution)/shard_map/ppermute | solution.py:321
  52.0 11.1 %collective-permute-start.17 = (bf16[3,256,256]{2,1,0:T(8,128)(2,1)S(1)}, bf16[3,256,256]{2,1,0:T(8,128)(2,1)S(1)}, u32[]{:S(2)}, u32[]{:S(2)}) collective-permute-start(bf16[3,256,256]{2,1,0:T(8,128)(2,1)S(1)} %add_convert_fusion), channel_id=1, source_target_pairs={{0,8},{8,0},{16,24},{24,16},{1,9},{9,1},{17,25},{25,17},{2,10},{10... | collective-permute-start | bytes 1179656 | tf_op jit(solution)/shard_map/ppermute | solution.py:322
  55.7 8.6 %collective-permute-start.15 = (bf16[3,256,256]{2,1,0:T(8,128)(2,1)S(1)}, bf16[3,256,256]{2,1,0:T(8,128)(2,1)S(1)}, u32[]{:S(2)}, u32[]{:S(2)}) collective-permute-start(bf16[3,256,256]{2,1,0:T(8,128)(2,1)S(1)} %add_convert_fusion.1), channel_id=1, source_target_pairs={{0,16},{8,24},{16,0},{24,8},{1,17},{9,25},{17,1},{25,9},{2,18},{10... | collective-permute-start | bytes 1179656 | tf_op jit(solution)/shard_map/ppermute | solution.py:322

commit v7 on v6

--- a/solution.py
+++ b/solution.py
@@ -13,7 +13,7 @@
 F32 = jnp.float32
 BF16 = jnp.bfloat16
 CODE_ROWS = 16
-VMEM_BYTES = 16 * 1024 * 1024
+VMEM_BYTES = 24 * 1024 * 1024
 
 def rounded(value):
     return lax.optimization_barrier(value.astype(jnp.bfloat16)).astype(jnp.float32)

time: 65.6 us -> 65.6 us (level)
  no operation moved by 1% of the time
where the time goes in v7:
time: 65.6 us; the launch traced here: 65.4 us
  waiting for transfers between devices  29.3 us (45%)
  starting transfers between devices  21.1 us (32%)
  Pallas kernels  7.98 us (12%)
  local copies, waits for them, and re-layouts  5.65 us (9%)
  between operations  0.73 us (1%)
    ppermute x12, waiting for transfers between devices, on_line(): send = lambda value, pairs: lax.ppermute(value, 'expert', pairs)  21.2 us
    ppermute x12, starting transfers between devices, on_line(): send = lambda value, pairs: lax.ppermute(value, 'expert', pairs)  14.6 us
    ppermute x6, waiting for transfers between devices, on_line(): send_dp = lambda value, pairs: lax.ppermute(value, 'dp', pairs)  8.04 us
    pallas_call x2, Pallas kernels, run_arm(): pl.pallas_call(functools.partial(arm_kernel, blocks, len(outs)), in_specs...  6.87 us
    ppermute x6, starting transfers between devices, on_line(): send_dp = lambda value, pairs: lax.ppermute(value, 'dp', pairs)  6.54 us
    unnamed x16, local copies, waits for them, and re-layouts  4.93 us
  transfers between devices with their start and end apart: 18, of which 9 were waited for; matrix products, arithmetic and copies ran while one was open for 2% of the time, Pallas kernels for 4%

profile of v7, /device:TPU:0, one launch (start us, length us, event | category | flops | bytes accessed | tf_op | source)
XLA Modules:
  0.0 65.4 jit_solution(7655224580121615081)
XLA Ops:
  0.6 0.7 %copy-done.2 = s32[128,2]{0,1:T(2,128)S(1)} copy-done((s32[128,2]{0,1:T(2,128)S(1)}, s32[128,2]{0,1:T(2,128)}, u32[]{:S(2)}) %copy-start.2) | copy-done | bytes 1048
  1.3 0.9 %copy-done = bf16[128,512]{1,0:T(8,128)(2,1)S(1)} copy-done((bf16[128,512]{1,0:T(8,128)(2,1)S(1)}, bf16[128,512]{1,0:T(8,128)(2,1)}, u32[]{:S(2)}) %copy-start) | copy-done | bytes 131096
  2.2 0.9 %copy-done.1 = bf16[128,512]{1,0:T(8,128)(2,1)S(1)} copy-done((bf16[128,512]{1,0:T(8,128)(2,1)S(1)}, bf16[128,512]{1,0:T(8,128)(2,1)}, u32[]{:S(2)}) %copy-start.1) | copy-done | bytes 131096
  3.1 3.1 %collective-permute-start.2 = (bf16[272,512]{1,0:T(8,128)(2,1)S(1)}, bf16[272,512]{1,0:T(8,128)(2,1)S(1)}, u32[]{:S(2)}, u32[]{:S(2)}) collective-permute-start(bf16[272,512]{1,0:T(8,128)(2,1)S(1)} %pack.1.refs_0_), channel_id=1, source_target_pairs={{0,2},{1,3},{2,0},{3,1},{4,6},{5,7},{6,4},{7,5},{8,10},{9,11},{10,... | collective-permute-start | bytes 835592 | tf_op jit(solution)/shard_map/ppermute | solution.py:321
  6.2 2.5 %collective-permute-start = (bf16[272,512]{1,0:T(8,128)(2,1)S(1)}, bf16[272,512]{1,0:T(8,128)(2,1)S(1)}, u32[]{:S(2)}, u32[]{:S(2)}) collective-permute-start(bf16[272,512]{1,0:T(8,128)(2,1)S(1)} %pack.1.refs_0_), channel_id=1, source_target_pairs={{0,6},{1,7},{6,0},{7,1},{2,4},{3,5},{4,2},{5,3},{8,14},{9,15},{14,... | collective-permute-start | bytes 835592 | tf_op jit(solution)/shard_map/ppermute | solution.py:321
  8.7 0.0 collective-permute-start.3
  8.7 4.6 %collective-permute-done.2.refs_1_ = bf16[272,512]{1,0:T(8,128)(2,1)S(1)} collective-permute-done((bf16[272,512]{1,0:T(8,128)(2,1)S(1)}, bf16[272,512]{1,0:T(8,128)(2,1)S(1)}, u32[]{:S(2)}, u32[]{:S(2)}) %collective-permute-start.2) | collective-permute-done | bytes 278560 | tf_op jit(solution)/shard_map/ppermute | solution.py:321
  13.3 0.0 collective-permute-start.4
  13.3 7.9 %collective-permute-done.refs_0_ = bf16[272,512]{1,0:T(8,128)(2,1)S(1)} collective-permute-done((bf16[272,512]{1,0:T(8,128)(2,1)S(1)}, bf16[272,512]{1,0:T(8,128)(2,1)S(1)}, u32[]{:S(2)}, u32[]{:S(2)}) %collective-permute-start) | collective-permute-done | bytes 278560 | tf_op jit(solution)/shard_map/ppermute | solution.py:321
  21.2 1.8 %collective-permute-start.1 = (bf16[272,512]{1,0:T(8,128)(2,1)S(1)}, bf16[272,512]{1,0:T(8,128)(2,1)S(1)}, u32[]{:S(2)}, u32[]{:S(2)}) collective-permute-start(bf16[272,512]{1,0:T(8,128)(2,1)S(1)} %broadcast_select_fusion), channel_id=1, source_target_pairs={{0,4},{1,5},{4,6},{5,7},{6,2},{7,3},{2,0},{3,1},{8,12},{9,13},{12,... | collective-permute-start | bytes 835592 | tf_op jit(solution)/shard_map/ppermute | solution.py:321
  23.0 0.0 collective-permute-start.6
  23.0 0.0 collective-permute-done.3.refs_2_
  23.0 0.0 collective-permute-done.4.refs_3_
  23.0 0.0 copy-start.4
  23.0 1.2 %copy-done.4 = bf16[1,512,1024]{2,1,0:T(8,128)(2,1)S(1)} copy-done((bf16[1,512,1024]{2,1,0:T(8,128)(2,1)S(1)}, bf16[1,512,1024]{2,1,0:T(8,128)(2,1)}, u32[]{:S(2)}) %copy-start.4) | copy-done | bytes 1048600
  24.3 1.2 %copy-done.6 = bf16[1,1024,512]{2,1,0:T(8,128)(2,1)S(1)} copy-done((bf16[1,1024,512]{2,1,0:T(8,128)(2,1)S(1)}, bf16[1,1024,512]{2,1,0:T(8,128)(2,1)}, u32[]{:S(2)}) %copy-start.6) | copy-done | bytes 1048600
  25.5 2.6 %arm_early.1 = (bf16[2,2,128,512]{3,2,1,0:T(8,128)(2,1)S(1)}, bf16[2,2,128,512]{3,2,1,0:T(8,128)(2,1)S(1)}, bf16[256,512]{1,0:T(8,128)(2,1)S(1)}, bf16[256,512]{...) custom-call(bf16[272,512]{1,0:T(8,128)(2,1)S(1)} %pack.1.refs_0_, ...), custom_call_target="tpu_custom_call" | custom-call | flops 1610612736 | bytes 12582912 | tf_op jit(solution)/shard_map/arm_early/pallas_call | solution.py:271
  28.1 0.6 collective-permute-done.1.refs_1_
  28.7 0.0 collective-permute-start.7
  28.7 1.6 %collective-permute-done.7.refs_3_ = bf16[272,512]{1,0:T(8,128)(2,1)S(1)} collective-permute-done((bf16[272,512]{1,0:T(8,128)(2,1)S(1)}, bf16[272,512]{1,0:T(8,128)(2,1)S(1)}, u32[]{:S(2)}, u32[]{:S(2)}) %collective-permute-start.7) | collective-permute-done | bytes 278560 | tf_op jit(solution)/shard_map/ppermute | solution.py:321
  30.3 4.2 %arm_late.1 = (bf16[2,2,128,512]{3,2,1,0:T(8,128)(2,1)S(1)}, bf16[2,2,128,512]{3,2,1,0:T(8,128)(2,1)S(1)}, bf16[3,256,256]{2,1,0:T(8,128)(2,1)S(1)}, bf16[3,256,...) custom-call(bf16[272,512]{1,0:T(8,128)(2,1)S(1)} %collective-permute, ...), custom_call_target="tpu_custom_call" | custom-call | flops 3221225472 | bytes 12582912 | tf_op jit(solution)/shard_map/arm_late/pallas_call | solution.py:271
  34.5 0.2 collective-permute-start.8
  34.7 0.4 collective-permute-start.5
  35.1 1.5 %collective-permute-start.10 = (bf16[3,256,256]{2,1,0:T(8,128)(2,1)S(1)}, bf16[3,256,256]{2,1,0:T(8,128)(2,1)S(1)}, u32[]{:S(2)}, u32[]{:S(2)}) collective-permute-start(bf16[3,256,256]{2,1,0:T(8,128)(2,1)S(1)} %get-tuple-element.43), channel_id=1, source_target_pairs={{0,8},{8,0},{16,24},{24,16},{1,9},{9,1},{17,25},{25,17},{2,10},{10... | collective-permute-start | bytes 1179656 | tf_op jit(solution)/shard_map/ppermute | solution.py:322
  36.6 1.5 %collective-permute-start.11 = (bf16[3,256,256]{2,1,0:T(8,128)(2,1)S(1)}, bf16[3,256,256]{2,1,0:T(8,128)(2,1)S(1)}, u32[]{:S(2)}, u32[]{:S(2)}) collective-permute-start(bf16[3,256,256]{2,1,0:T(8,128)(2,1)S(1)} %get-tuple-element.44), channel_id=1, source_target_pairs={{0,16},{8,24},{16,0},{24,8},{1,17},{9,25},{17,1},{25,9},{2,18},{10... | collective-permute-start | bytes 1179656 | tf_op jit(solution)/shard_map/ppermute | solution.py:322
  38.1 0.1 fusion.5
  38.2 2.0 %collective-permute-start.9 = (bf16[2,128,512]{2,1,0:T(8,128)(2,1)S(1)}, bf16[2,128,512]{2,1,0:T(8,128)(2,1)S(1)}, u32[]{:S(2)}, u32[]{:S(2)}) collective-permute-start(bf16[2,128,512]{2,1,0:T(8,128)(2,1)S(1)} %fusion.5), channel_id=1, source_target_pairs={{4,0},{5,1},{6,4},{7,5},{2,6},{3,7},{0,2},{1,3},{12,8},{13,9},{14,... | collective-permute-start | bytes 786440 | tf_op jit(solution)/shard_map/ppermute | solution.py:321
  40.1 0.6 collective-permute-start.14
  40.7 0.0 collective-permute-done.5
  40.7 0.8 %collective-permute-start.16 = (bf16[3,256,256]{2,1,0:T(8,128)(2,1)S(1)}, bf16[3,256,256]{2,1,0:T(8,128)(2,1)S(1)}, u32[]{:S(2)}, u32[]{:S(2)}) collective-permute-start(bf16[3,256,256]{2,1,0:T(8,128)(2,1)S(1)} %get-tuple-element.53), channel_id=1, source_target_pairs={{0,16},{8,24},{16,0},{24,8},{1,17},{9,25},{17,1},{25,9},{2,18},{10... | collective-permute-start | bytes 1179656 | tf_op jit(solution)/shard_map/ppermute | solution.py:322
  41.5 0.1 fusion.6
  41.6 5.5 %collective-permute-done.10 = bf16[3,256,256]{2,1,0:T(8,128)(2,1)S(1)} collective-permute-done((bf16[3,256,256]{2,1,0:T(8,128)(2,1)S(1)}, bf16[3,256,256]{2,1,0:T(8,128)(2,1)S(1)}, u32[]{:S(2)}, u32[]{:S(2)}) %collective-permute-start.10) | collective-permute-done | bytes 393248 | tf_op jit(solution)/shard_map/ppermute | solution.py:322
  47.1 1.9 %collective-permute-start.13 = (bf16[2,128,512]{2,1,0:T(8,128)(2,1)S(1)}, bf16[2,128,512]{2,1,0:T(8,128)(2,1)S(1)}, u32[]{:S(2)}, u32[]{:S(2)}) collective-permute-start(bf16[2,128,512]{2,1,0:T(8,128)(2,1)S(1)} %fusion.6), channel_id=1, source_target_pairs={{0,2},{1,3},{2,0},{3,1},{4,6},{5,7},{6,4},{7,5},{8,10},{9,11},{10,... | collective-permute-start | bytes 786440 | tf_op jit(solution)/shard_map/ppermute | solution.py:321
  49.0 0.0 collective-permute-done.11
  49.0 0.0 collective-permute-done.9
  49.0 0.1 fusion.1
  49.1 2.8 %collective-permute-start.12 = (bf16[2,128,512]{2,1,0:T(8,128)(2,1)S(1)}, bf16[2,128,512]{2,1,0:T(8,128)(2,1)S(1)}, u32[]{:S(2)}, u32[]{:S(2)}) collective-permute-start(bf16[2,128,512]{2,1,0:T(8,128)(2,1)S(1)} %fusion.1), channel_id=1, source_target_pairs={{0,6},{1,7},{6,0},{7,1},{2,4},{3,5},{4,2},{5,3},{8,14},{9,15},{14,... | collective-permute-start | bytes 786440 | tf_op jit(solution)/shard_map/ppermute | solution.py:321
  51.9 0.1 add_convert_fusion
  52.0 0.6 collective-permute-start.17
  52.6 0.1 add_convert_fusion.1
  52.7 3.1 %collective-permute-done.13 = bf16[2,128,512]{2,1,0:T(8,128)(2,1)S(1)} collective-permute-done((bf16[2,128,512]{2,1,0:T(8,128)(2,1)S(1)}, bf16[2,128,512]{2,1,0:T(8,128)(2,1)S(1)}, u32[]{:S(2)}, u32[]{:S(2)}) %collective-permute-start.13) | collective-permute-done | bytes 262176 | tf_op jit(solution)/shard_map/ppermute | solution.py:321
  55.7 1.5 %collective-permute-start.15 = (bf16[3,256,256]{2,1,0:T(8,128)(2,1)S(1)}, bf16[3,256,256]{2,1,0:T(8,128)(2,1)S(1)}, u32[]{:S(2)}, u32[]{:S(2)}) collective-permute-start(bf16[3,256,256]{2,1,0:T(8,128)(2,1)S(1)} %add_convert_fusion.1), channel_id=1, source_target_pairs={{0,16},{8,24},{16,0},{24,8},{1,17},{9,25},{17,1},{25,9},{2,18},{10... | collective-permute-start | bytes 1179656 | tf_op jit(solution)/shard_map/ppermute | solution.py:322
  57.3 3.6 %collective-permute-done.12 = bf16[2,128,512]{2,1,0:T(8,128)(2,1)S(1)} collective-permute-done((bf16[2,128,512]{2,1,0:T(8,128)(2,1)S(1)}, bf16[2,128,512]{2,1,0:T(8,128)(2,1)S(1)}, u32[]{:S(2)}, u32[]{:S(2)}) %collective-permute-start.12) | collective-permute-done | bytes 262176 | tf_op jit(solution)/shard_map/ppermute | solution.py:321
  60.8 0.2 fusion.3
  61.0 0.7 %slice_bitcast_fusion = (bf16[128,512]{1,0:T(8,128)(2,1)}, bf16[128,512]{1,0:T(8,128)(2,1)}) fusion(bf16[2,128,512]{2,1,0:T(8,128)(2,1)S(1)} %fusion.3), kind=kLoop, calls=%fused_computation.15 | loop fusion | bytes 524288 | tf_op jit(solution)/shard_map/convert_element_type | solution.py:357
  61.7 1.4 %collective-permute-done.17.refs_5_ = bf16[3,256,256]{2,1,0:T(8,128)(2,1)S(1)} collective-permute-done((bf16[3,256,256]{2,1,0:T(8,128)(2,1)S(1)}, bf16[3,256,256]{2,1,0:T(8,128)(2,1)S(1)}, u32[]{:S(2)}, u32[]{:S(2)}) %collective-permute-start.17) | collective-permute-done | bytes 393248 | tf_op jit(solution)/shard_map/ppermute | solution.py:322
  63.1 1.2 %collective-permute-done.15.refs_2_ = bf16[3,256,256]{2,1,0:T(8,128)(2,1)S(1)} collective-permute-done((bf16[3,256,256]{2,1,0:T(8,128)(2,1)S(1)}, bf16[3,256,256]{2,1,0:T(8,128)(2,1)S(1)}, u32[]{:S(2)}, u32[]{:S(2)}) %collective-permute-start.15) | collective-permute-done | bytes 393248 | tf_op jit(solution)/shard_map/ppermute | solution.py:322
  64.3 1.1 %finish.1 = (bf16[512,256]{1,0:T(8,128)(2,1)}, bf16[512,256]{1,0:T(8,128)(2,1)}, bf16[256,512]{1,0:T(8,128)(2,1)}) custom-call(bf16[3,256,256]{2,1,0:T(8,128)(2,1)S(1)} %get-tuple-element.48.refs_0_, bf16[3,256,256]{2,1,0:T(8,128)(2,1)S(1)} %collective-permute-done.14.refs_1_, bf16[3,256,256]{2,1,0:T(8,128)(2,1)S(1)} %collective-permute-done.15.refs_2_, ...), custom_call_target="tpu_custom_call" | custom-call | tf_op jit(solution)/shard_map/finish/pallas_call | solution.py:291
  (16 shorter events, 0.1 us)
Async XLA Ops:
  0.6 0.7 %copy-start.2 = (s32[128,2]{0,1:T(2,128)S(1)}, s32[128,2]{0,1:T(2,128)}, u32[]{:S(2)}) copy-start(s32[128,2]{0,1:T(2,128)} %param.7) | copy-start | bytes 3076
  1.3 0.9 %copy-start = (bf16[128,512]{1,0:T(8,128)(2,1)S(1)}, bf16[128,512]{1,0:T(8,128)(2,1)}, u32[]{:S(2)}) copy-start(bf16[128,512]{1,0:T(8,128)(2,1)} %tokens_ref.1) | copy-start | bytes 393220
  2.2 0.9 %copy-start.1 = (bf16[128,512]{1,0:T(8,128)(2,1)S(1)}, bf16[128,512]{1,0:T(8,128)(2,1)}, u32[]{:S(2)}) copy-start(bf16[128,512]{1,0:T(8,128)(2,1)} %cot_ref.1) | copy-start | bytes 393220
  3.1 19.9 %copy-start.3 = (bf16[1,512,1024]{2,1,0:T(8,128)(2,1)S(1)}, bf16[1,512,1024]{2,1,0:T(8,128)(2,1)}, u32[]{:S(2)}) copy-start(bf16[1,512,1024]{2,1,0:T(8,128)(2,1)} %param.9) | copy-start | bytes 3145732
  3.1 10.2 %collective-permute-start.2 = (bf16[272,512]{1,0:T(8,128)(2,1)S(1)}, bf16[272,512]{1,0:T(8,128)(2,1)S(1)}, u32[]{:S(2)}, u32[]{:S(2)}) collective-permute-start(bf16[272,512]{1,0:T(8,128)(2,1)S(1)} %pack.1.refs_0_), channel_id=1, source_target_pairs={{0,2},{1,3},{2,0},{3,1},{4,6},{5,7},{6,4},{7,5},{8,10},{9,11},{10,... | collective-permute-start | bytes 835592 | tf_op jit(solution)/shard_map/ppermute | solution.py:321
  6.2 14.9 %collective-permute-start = (bf16[272,512]{1,0:T(8,128)(2,1)S(1)}, bf16[272,512]{1,0:T(8,128)(2,1)S(1)}, u32[]{:S(2)}, u32[]{:S(2)}) collective-permute-start(bf16[272,512]{1,0:T(8,128)(2,1)S(1)} %pack.1.refs_0_), channel_id=1, source_target_pairs={{0,6},{1,7},{6,0},{7,1},{2,4},{3,5},{4,2},{5,3},{8,14},{9,15},{14,... | collective-permute-start | bytes 835592 | tf_op jit(solution)/shard_map/ppermute | solution.py:321
  8.7 14.3 %collective-permute-start.3 = (bf16[272,512]{1,0:T(8,128)(2,1)S(1)}, bf16[272,512]{1,0:T(8,128)(2,1)S(1)}, u32[]{:S(2)}, u32[]{:S(2)}) collective-permute-start(bf16[272,512]{1,0:T(8,128)(2,1)S(1)} %pack.1.refs_0_), channel_id=1, source_target_pairs={{0,1},{1,0},{2,3},{3,2},{4,5},{5,4},{6,7},{7,6},{8,9},{9,8},{10,11... | collective-permute-start | bytes 835592 | tf_op jit(solution)/shard_map/ppermute | solution.py:321
  13.3 9.7 %collective-permute-start.4 = (bf16[272,512]{1,0:T(8,128)(2,1)S(1)}, bf16[272,512]{1,0:T(8,128)(2,1)S(1)}, u32[]{:S(2)}, u32[]{:S(2)}) collective-permute-start(bf16[272,512]{1,0:T(8,128)(2,1)S(1)} %collective-permute-done.2.refs_1_), channel_id=1, source_target_pairs={{0,1},{1,0},{2,3},{3,2},{4,5},{5,4},{6,7},{7,6},{8,9},{9,8},{10,11... | collective-permute-start | bytes 835592 | tf_op jit(solution)/shard_map/ppermute | solution.py:321
  21.2 7.5 %collective-permute-start.1 = (bf16[272,512]{1,0:T(8,128)(2,1)S(1)}, bf16[272,512]{1,0:T(8,128)(2,1)S(1)}, u32[]{:S(2)}, u32[]{:S(2)}) collective-permute-start(bf16[272,512]{1,0:T(8,128)(2,1)S(1)} %broadcast_select_fusion), channel_id=1, source_target_pairs={{0,4},{1,5},{4,6},{5,7},{6,2},{7,3},{2,0},{3,1},{8,12},{9,13},{12,... | collective-permute-start | bytes 835592 | tf_op jit(solution)/shard_map/ppermute | solution.py:321
  23.0 5.7 %collective-permute-start.6 = (bf16[272,512]{1,0:T(8,128)(2,1)S(1)}, bf16[272,512]{1,0:T(8,128)(2,1)S(1)}, u32[]{:S(2)}, u32[]{:S(2)}) collective-permute-start(bf16[272,512]{1,0:T(8,128)(2,1)S(1)} %collective-permute-done.refs_0_), channel_id=1, source_target_pairs={{0,1},{1,0},{2,3},{3,2},{4,5},{5,4},{6,7},{7,6},{8,9},{9,8},{10,11... | collective-permute-start | bytes 835592 | tf_op jit(solution)/shard_map/ppermute | solution.py:321
  23.0 1.2 %copy-start.4 = (bf16[1,512,1024]{2,1,0:T(8,128)(2,1)S(1)}, bf16[1,512,1024]{2,1,0:T(8,128)(2,1)}, u32[]{:S(2)}) copy-start(bf16[1,512,1024]{2,1,0:T(8,128)(2,1)} %param.10) | copy-start | bytes 3145732
  24.3 1.2 %copy-start.6 = (bf16[1,1024,512]{2,1,0:T(8,128)(2,1)S(1)}, bf16[1,1024,512]{2,1,0:T(8,128)(2,1)}, u32[]{:S(2)}) copy-start(bf16[1,1024,512]{2,1,0:T(8,128)(2,1)} %param.11) | copy-start | bytes 3145732
  25.5 4.8 %copy-start.5 = (bf16[1,512,1024]{2,1,0:T(8,128)(2,1)S(1)}, bf16[1,512,1024]{2,1,0:T(8,128)(2,1)}, u32[]{:S(2)}) copy-start(bf16[1,512,1024]{2,1,0:T(8,128)(2,1)} %param.10) | copy-start | bytes 3145732
  25.5 4.8 %copy-start.7 = (bf16[1,1024,512]{2,1,0:T(8,128)(2,1)S(1)}, bf16[1,1024,512]{2,1,0:T(8,128)(2,1)}, u32[]{:S(2)}) copy-start(bf16[1,1024,512]{2,1,0:T(8,128)(2,1)} %param.11) | copy-start | bytes 3145732
  28.7 1.6 %collective-permute-start.7 = (bf16[272,512]{1,0:T(8,128)(2,1)S(1)}, bf16[272,512]{1,0:T(8,128)(2,1)S(1)}, u32[]{:S(2)}, u32[]{:S(2)}) collective-permute-start(bf16[272,512]{1,0:T(8,128)(2,1)S(1)} %collective-permute-done.1.refs_1_), channel_id=1, source_target_pairs={{0,1},{1,0},{2,3},{3,2},{4,5},{5,4},{6,7},{7,6},{8,9},{9,8},{10,11... | collective-permute-start | bytes 835592 | tf_op jit(solution)/shard_map/ppermute | solution.py:321
  34.5 3.6 %collective-permute-start.8 = (bf16[2,2,128,512]{3,2,1,0:T(8,128)(2,1)S(1)}, bf16[2,2,128,512]{3,2,1,0:T(8,128)(2,1)S(1)}, u32[]{:S(2)}, u32[]{:S(2)}) collective-permute-start(bf16[2,2,128,512]{3,2,1,0:T(8,128)(2,1)S(1)} %get-tuple-element.42), channel_id=1, source_target_pairs={{0,1},{1,0},{2,3},{3,2},{4,5},{5,4},{6,7},{7,6},{8,9},{9,8},{10,11... | collective-permute-start | bytes 1572872 | tf_op jit(solution)/shard_map/ppermute | solution.py:321
  34.7 6.0 %collective-permute-start.5 = (bf16[2,2,128,512]{3,2,1,0:T(8,128)(2,1)S(1)}, bf16[2,2,128,512]{3,2,1,0:T(8,128)(2,1)S(1)}, u32[]{:S(2)}, u32[]{:S(2)}) collective-permute-start(bf16[2,2,128,512]{3,2,1,0:T(8,128)(2,1)S(1)} %get-tuple-element.34), channel_id=1, source_target_pairs={{0,1},{1,0},{2,3},{3,2},{4,5},{5,4},{6,7},{7,6},{8,9},{9,8},{10,11... | collective-permute-start | bytes 1572872 | tf_op jit(solution)/shard_map/ppermute | solution.py:321
  35.1 12.0 %collective-permute-start.10 = (bf16[3,256,256]{2,1,0:T(8,128)(2,1)S(1)}, bf16[3,256,256]{2,1,0:T(8,128)(2,1)S(1)}, u32[]{:S(2)}, u32[]{:S(2)}) collective-permute-start(bf16[3,256,256]{2,1,0:T(8,128)(2,1)S(1)} %get-tuple-element.43), channel_id=1, source_target_pairs={{0,8},{8,0},{16,24},{24,16},{1,9},{9,1},{17,25},{25,17},{2,10},{10... | collective-permute-start | bytes 1179656 | tf_op jit(solution)/shard_map/ppermute | solution.py:322
  36.6 12.4 %collective-permute-start.11 = (bf16[3,256,256]{2,1,0:T(8,128)(2,1)S(1)}, bf16[3,256,256]{2,1,0:T(8,128)(2,1)S(1)}, u32[]{:S(2)}, u32[]{:S(2)}) collective-permute-start(bf16[3,256,256]{2,1,0:T(8,128)(2,1)S(1)} %get-tuple-element.44), channel_id=1, source_target_pairs={{0,16},{8,24},{16,0},{24,8},{1,17},{9,25},{17,1},{25,9},{2,18},{10... | collective-permute-start | bytes 1179656 | tf_op jit(solution)/shard_map/ppermute | solution.py:322
  38.2 10.8 %collective-permute-start.9 = (bf16[2,128,512]{2,1,0:T(8,128)(2,1)S(1)}, bf16[2,128,512]{2,1,0:T(8,128)(2,1)S(1)}, u32[]{:S(2)}, u32[]{:S(2)}) collective-permute-start(bf16[2,128,512]{2,1,0:T(8,128)(2,1)S(1)} %fusion.5), channel_id=1, source_target_pairs={{4,0},{5,1},{6,4},{7,5},{2,6},{3,7},{0,2},{1,3},{12,8},{13,9},{14,... | collective-permute-start | bytes 786440 | tf_op jit(solution)/shard_map/ppermute | solution.py:321
  40.1 21.6 %collective-permute-start.14 = (bf16[3,256,256]{2,1,0:T(8,128)(2,1)S(1)}, bf16[3,256,256]{2,1,0:T(8,128)(2,1)S(1)}, u32[]{:S(2)}, u32[]{:S(2)}) collective-permute-start(bf16[3,256,256]{2,1,0:T(8,128)(2,1)S(1)} %get-tuple-element.49), channel_id=1, source_target_pairs={{0,8},{8,0},{16,24},{24,16},{1,9},{9,1},{17,25},{25,17},{2,10},{10... | collective-permute-start | bytes 1179656 | tf_op jit(solution)/shard_map/ppermute | solution.py:322
  40.7 21.0 %collective-permute-start.16 = (bf16[3,256,256]{2,1,0:T(8,128)(2,1)S(1)}, bf16[3,256,256]{2,1,0:T(8,128)(2,1)S(1)}, u32[]{:S(2)}, u32[]{:S(2)}) collective-permute-start(bf16[3,256,256]{2,1,0:T(8,128)(2,1)S(1)} %get-tuple-element.53), channel_id=1, source_target_pairs={{0,16},{8,24},{16,0},{24,8},{1,17},{9,25},{17,1},{25,9},{2,18},{10... | collective-permute-start | bytes 1179656 | tf_op jit(solution)/shard_map/ppermute | solution.py:322
  47.1 8.7 %collective-permute-start.13 = (bf16[2,128,512]{2,1,0:T(8,128)(2,1)S(1)}, bf16[2,128,512]{2,1,0:T(8,128)(2,1)S(1)}, u32[]{:S(2)}, u32[]{:S(2)}) collective-permute-start(bf16[2,128,512]{2,1,0:T(8,128)(2,1)S(1)} %fusion.6), channel_id=1, source_target_pairs={{0,2},{1,3},{2,0},{3,1},{4,6},{5,7},{6,4},{7,5},{8,10},{9,11},{10,... | collective-permute-start | bytes 786440 | tf_op jit(solution)/shard_map/ppermute | solution.py:321
  49.1 11.7 %collective-permute-start.12 = (bf16[2,128,512]{2,1,0:T(8,128)(2,1)S(1)}, bf16[2,128,512]{2,1,0:T(8,128)(2,1)S(1)}, u32[]{:S(2)}, u32[]{:S(2)}) collective-permute-start(bf16[2,128,512]{2,1,0:T(8,128)(2,1)S(1)} %fusion.1), channel_id=1, source_target_pairs={{0,6},{1,7},{6,0},{7,1},{2,4},{3,5},{4,2},{5,3},{8,14},{9,15},{14,... | collective-permute-start | bytes 786440 | tf_op jit(solution)/shard_map/ppermute | solution.py:321
  52.0 11.1 %collective-permute-start.17 = (bf16[3,256,256]{2,1,0:T(8,128)(2,1)S(1)}, bf16[3,256,256]{2,1,0:T(8,128)(2,1)S(1)}, u32[]{:S(2)}, u32[]{:S(2)}) collective-permute-start(bf16[3,256,256]{2,1,0:T(8,128)(2,1)S(1)} %add_convert_fusion), channel_id=1, source_target_pairs={{0,8},{8,0},{16,24},{24,16},{1,9},{9,1},{17,25},{25,17},{2,10},{10... | collective-permute-start | bytes 1179656 | tf_op jit(solution)/shard_map/ppermute | solution.py:322
  55.7 8.6 %collective-permute-start.15 = (bf16[3,256,256]{2,1,0:T(8,128)(2,1)S(1)}, bf16[3,256,256]{2,1,0:T(8,128)(2,1)S(1)}, u32[]{:S(2)}, u32[]{:S(2)}) collective-permute-start(bf16[3,256,256]{2,1,0:T(8,128)(2,1)S(1)} %add_convert_fusion.1), channel_id=1, source_target_pairs={{0,16},{8,24},{16,0},{24,8},{1,17},{9,25},{17,1},{25,9},{2,18},{10... | collective-permute-start | bytes 1179656 | tf_op jit(solution)/shard_map/ppermute | solution.py:322
